TPU v7x, 32 devices: a whole 2x2x4 slice. The times are simulated.
32 devices in a mesh: batch: 8 (over z, core), seq: 4 (over y, x).
Axes of the slice: x: 2, y: 2, z: 4, core: 2. Of those that a mesh axis runs over, the one named last changes fastest.
Arguments:
- layer_input: bfloat16 [8, 2048, 2048], P('batch', 'seq'), may hold values from -6 to 6
- cotangent: bfloat16 [8, 2048, 2048], P('batch', 'seq'), may hold values from -6 to 6
- w_qkv: bfloat16 [2048, 6144], P(('batch', 'seq')), may hold values from -0.125 to 0.125
- bias_qkv: bfloat16 [3, 2048], P(None, ('batch', 'seq')), may hold values from -2 to 2
- w_out: bfloat16 [2048, 2048], P(('batch', 'seq')), may hold values from -0.125 to 0.125
- w_up: bfloat16 [2048, 8192], P(('batch', 'seq')), may hold values from -0.125 to 0.125
- w_down: bfloat16 [8192, 2048], P(('batch', 'seq')), may hold values from -0.0625 to 0.0625
- gains_d: bfloat16 [3, 2048], P(None, ('batch', 'seq')), may hold values from 0.25 to 1.75
- biases_d: bfloat16 [5, 2048], P(None, ('batch', 'seq')), may hold values from -2 to 2
- gain_ff: bfloat16 [8192], P(('batch', 'seq')), may hold values from 0.25 to 1.75
- biases_ff: bfloat16 [2, 8192], P(None, ('batch', 'seq')), may hold values from -2 to 2
- data_type: int32 [8], P('batch'), may hold values from 0 to 2
- doc_bounds: int32 [8, 3], P('batch'), may hold values from 1 to 2048, as said below
- span_starts: int32 [8, 4], P('batch'), may hold values from 0 to 1984, as said below
Outputs:
- layer_output: bfloat16 [8, 2048, 2048], P('batch', 'seq')
- grad_input: float32 [8, 2048, 2048], P('batch', 'seq')
- grad_w_qkv: float32 [2048, 6144], P(('batch', 'seq'))
- grad_bias_qkv: float32 [3, 2048], P(None, ('batch', 'seq'))
- grad_w_out: float32 [2048, 2048], P(('batch', 'seq'))
- grad_w_up: float32 [2048, 8192], P(('batch', 'seq'))
- grad_w_down: float32 [8192, 2048], P(('batch', 'seq'))
- grad_gains_d: float32 [3, 2048], P(None, ('batch', 'seq'))
- grad_biases_d: float32 [5, 2048], P(None, ('batch', 'seq'))
- grad_gain_ff: float32 [8192], P(('batch', 'seq'))
- grad_biases_ff: float32 [2, 8192], P(None, ('batch', 'seq'))
Inputs may be any that keep to these rules, and one draw needn't show every extreme that they name: `doc_bounds`: in each pair of sequences 2b and 2b + 1 one has all its entries equal to 2048; the other's entries lie in 1 to 2047 in no particular order. `span_starts`: span j starts between j * 512 and (j + 1) * 512 - 64, so spans never intersect; in every draw some sequence's first span starts at 0 and some sequence's last span starts at 1984.
All inputs are finite; a program needn't handle non-finite values.
Results may differ from a plain program's by a relative error of at most 0.017.
Values may be sent and summed in bfloat16 or wider, within the bound.
No kernel may reach another device: no remote copies, remote signals or barrier semaphores. Data moves between devices by JAX's collectives and lax.ppermute only.
A program may use at most 512 MiB of HBM per device.

v0:
```python
import jax
import jax.numpy as jnp
from jax import lax
from jax.sharding import PartitionSpec as P

D = 2048
HEADS = 32
HEAD_DIM = 64
SEQ_LEN = 2048
SPAN = 64


NEG_FILL = -1e30
NORM_EPS = 1e-05


def contract_rows(left, right):
    return lax.dot_general(
        left, right, (((0,), (0,)), ((), ())), preferred_element_type=jnp.float32
    )


def times_transpose(left, right):
    return lax.dot_general(
        left, right, (((1,), (1,)), ((), ())), preferred_element_type=jnp.float32
    )


def gelu_tanh(values):
    return jax.nn.gelu(values, approximate=True)


def norm_rows(values, gain, shift):
    center = jnp.mean(values, axis=-1, keepdims=True)
    spread = values - center
    inverse = lax.rsqrt(jnp.mean(spread * spread, axis=-1, keepdims=True) + NORM_EPS)
    normed = spread * inverse
    return (normed * gain + shift, normed, inverse)


def norm_back(normed, inverse, gain, upper):
    scaled = upper * gain
    first_mean = jnp.mean(scaled, axis=-1, keepdims=True)
    second_mean = jnp.mean(scaled * normed, axis=-1, keepdims=True)
    lower = inverse * (scaled - first_mean - normed * second_mean)
    return (lower, jnp.sum(upper * normed, axis=0), jnp.sum(upper, axis=0))


def partner(values):
    is_even = jnp.arange(values.shape[-1]) % 2 == 0
    return jnp.where(is_even, -jnp.roll(values, -1, axis=-1), jnp.roll(values, 1, axis=-1))


def rot_tables(places):
    column = jnp.arange(D) % HEAD_DIM
    pair_idx = (column // 2).astype(jnp.float32)
    frequency = jnp.power(10000.0, -2.0 * pair_idx / HEAD_DIM)
    place_float = places.astype(jnp.float32)
    angles = place_float[:, None] * frequency[None, :]
    zeta_base = (2.0 * pair_idx + 0.4 * HEAD_DIM) / (1.4 * HEAD_DIM)
    exponent = (place_float - SEQ_LEN // 2) / 512.0
    scales = jnp.power(zeta_base[None, :], exponent[:, None])
    return (jnp.cos(angles), jnp.sin(angles), scales)


def turn(values, cosine, sine_vals, factor):
    return (values * cosine + partner(values) * sine_vals) * factor


def turn_back(grads, cosine, sine_vals, factor):
    scaled = grads * factor
    return scaled * cosine - partner(scaled) * sine_vals


def place_info(places, seq_kind, bounds_rows, spans_rows):
    doc_ids = jnp.sum((bounds_rows[:, None, :] <= places[None, :, None]).astype(jnp.int32), axis=2)
    in_span = (
        (spans_rows[:, None, :] <= places[None, :, None])
        & (places[None, :, None] < spans_rows[:, None, :] + SPAN)
        & (seq_kind[:, None, None] > 0)
    )
    return (doc_ids, in_span.astype(jnp.float32))


def allowed_pairs(query_info, query_places, key_info, key_places):
    same_doc = query_info[0][:, :, None] == key_info[0][:, None, :]
    same_span = jnp.einsum("gqj,gkj->gqk", query_info[1], key_info[1]) > 0.5
    causal = key_places[None, None, :] <= query_places[None, :, None]
    return same_doc & (causal | same_span)


def local(
    layer_input,
    cotangent,
    w_qkv,
    bias_qkv,
    w_out,
    w_up,
    w_down,
    gains_d,
    biases_d,
    gain_ff,
    biases_ff,
    data_type,
    doc_bounds,
    span_starts,
):
    seqs_here, local_len = (layer_input.shape[0], layer_input.shape[1])
    row_total = seqs_here * local_len
    head_scale = HEAD_DIM ** (-0.5)
    seq_index = lax.axis_index("seq")
    places = seq_index * local_len + jnp.arange(local_len, dtype=jnp.int32)
    cosine, sine_vals, scales = rot_tables(places)
    query_info = place_info(places, data_type, doc_bounds, span_starts)

    def key_mask(key_rows):
        key_places = jnp.arange(key_rows, dtype=jnp.int32)
        key_info = place_info(key_places, data_type, doc_bounds, span_starts)
        return allowed_pairs(query_info, places, key_info, key_places)

    full_qkv, full_out, qkv_bias, gains_all, shifts_all = (
        lax.all_gather(w_qkv, ("batch", "seq"), axis=0, tiled=True),
        lax.all_gather(w_out, ("batch", "seq"), axis=0, tiled=True),
        lax.all_gather(bias_qkv, ("batch", "seq"), axis=1, tiled=True),
        lax.all_gather(gains_d, ("batch", "seq"), axis=1, tiled=True),
        lax.all_gather(biases_d, ("batch", "seq"), axis=1, tiled=True),
    )
    gain_rows = gains_all.astype(jnp.float32)
    shift_rows = shifts_all.astype(jnp.float32)
    qkv_shift = qkv_bias.astype(jnp.float32).reshape(3 * D)
    input_float = layer_input.astype(jnp.float32).reshape(row_total, D)
    normed_in, norm1_n, norm1_i = norm_rows(input_float, gain_rows[0], shift_rows[0])
    input_low = normed_in.astype(jnp.bfloat16)
    qkv = jnp.dot(input_low, full_qkv, preferred_element_type=jnp.float32) + qkv_shift
    shaped = qkv.reshape(seqs_here, local_len, 3 * D)
    query_rot = turn(shaped[:, :, :D], cosine, sine_vals, scales).astype(jnp.bfloat16)
    key_rot = turn(shaped[:, :, D : 2 * D], cosine, sine_vals, 1.0 / scales).astype(jnp.bfloat16)
    value_low = shaped[:, :, 2 * D :].astype(jnp.bfloat16)
    query_heads = query_rot.reshape(seqs_here, local_len, HEADS, HEAD_DIM)
    key_part = lax.all_gather(key_rot, "seq", axis=1, tiled=True)
    val_part = lax.all_gather(value_low, "seq", axis=1, tiled=True)
    key_rows = key_part.shape[1]
    allowed = key_mask(key_rows)
    running_max = jnp.full((seqs_here, HEADS, local_len), NEG_FILL, jnp.float32)
    accum = jnp.zeros((seqs_here, local_len, HEADS, HEAD_DIM), jnp.float32)
    key_heads = key_part.reshape(seqs_here, key_rows, HEADS, HEAD_DIM)
    val_heads = val_part.reshape(seqs_here, key_rows, HEADS, HEAD_DIM)
    scores = (
        jnp.einsum("gqhd,gkhd->ghqk", query_heads, key_heads, preferred_element_type=jnp.float32)
        * head_scale
    )
    masked = jnp.where(allowed[:, None], scores, NEG_FILL)
    new_max = jnp.maximum(running_max, jnp.max(masked, axis=-1))
    weights = jnp.where(allowed[:, None], jnp.exp(masked - new_max[..., None]), 0.0)
    fade = jnp.exp(running_max - new_max)
    totals = jnp.sum(weights, axis=-1)
    accum = accum * jnp.swapaxes(fade, 1, 2)[..., None] + jnp.einsum(
        "ghqk,gkhd->gqhd",
        weights.astype(jnp.bfloat16),
        val_heads,
        preferred_element_type=jnp.float32,
    )
    running_max, totals, accum = (new_max, totals, accum)
    attn_heads = accum / jnp.swapaxes(totals, 1, 2)[..., None]
    log_total = running_max + jnp.log(totals)
    attn = attn_heads.reshape(row_total, D)
    normed_branch, norm2_n, norm2_i = norm_rows(attn, gain_rows[1], shift_rows[1])
    branch_low = normed_branch.astype(jnp.bfloat16)
    resid = input_float + (
        jnp.dot(branch_low, full_out, preferred_element_type=jnp.float32) + shift_rows[3]
    )
    full_up, full_down, gain_vec, ffn_shifts = (
        lax.all_gather(w_up, ("batch", "seq"), axis=0, tiled=True),
        lax.all_gather(w_down, ("batch", "seq"), axis=0, tiled=True),
        lax.all_gather(gain_ff, ("batch", "seq"), axis=0, tiled=True),
        lax.all_gather(biases_ff, ("batch", "seq"), axis=1, tiled=True),
    )
    gain_ffn = gain_vec.astype(jnp.float32)
    shift_ffn = ffn_shifts.astype(jnp.float32)
    normed_mid, norm3_n, norm3_i = norm_rows(resid, gain_rows[2], shift_rows[2])
    mid_low = normed_mid.astype(jnp.bfloat16)
    up_proj = jnp.dot(mid_low, full_up, preferred_element_type=jnp.float32) + shift_ffn[1]
    normed_ffn, norm4_n, norm4_i = norm_rows(gelu_tanh(up_proj), gain_ffn, shift_ffn[0])
    ffn_low = normed_ffn.astype(jnp.bfloat16)
    result = resid + (
        jnp.dot(ffn_low, full_down, preferred_element_type=jnp.float32) + shift_rows[4]
    )
    back_up, back_down = (
        lax.all_gather(w_up, ("batch", "seq"), axis=0, tiled=True),
        lax.all_gather(w_down, ("batch", "seq"), axis=0, tiled=True),
    )
    grad_given = cotangent.reshape(row_total, D)
    grad_float = grad_given.astype(jnp.float32)
    g_down = contract_rows(ffn_low, grad_given)
    down_shift_grad = jnp.sum(grad_float, axis=0)
    grad_ffn = times_transpose(grad_given, back_down)
    grad_gel, gain_ff_grad, ffn_shift_grad = norm_back(norm4_n, norm4_i, gain_ffn, grad_ffn)
    grad_up = jax.vjp(gelu_tanh, up_proj)[1](grad_gel)[0].astype(jnp.bfloat16)
    g_up = contract_rows(mid_low, grad_up)
    up_shift_grad = jnp.sum(grad_up.astype(jnp.float32), axis=0)
    grad_mid = times_transpose(grad_up, back_up)
    grad_norm3, gain3_grad, shift3_grad = norm_back(norm3_n, norm3_i, gain_rows[2], grad_mid)
    grad_resid = grad_float + grad_norm3
    ffn_sums = (
        lax.psum_scatter(g_up, ("batch", "seq"), scatter_dimension=0, tiled=True),
        lax.psum_scatter(g_down, ("batch", "seq"), scatter_dimension=0, tiled=True),
        lax.psum_scatter(gain_ff_grad, ("batch", "seq"), scatter_dimension=0, tiled=True),
        lax.psum_scatter(
            jnp.stack([ffn_shift_grad, up_shift_grad]),
            ("batch", "seq"),
            scatter_dimension=1,
            tiled=True,
        ),
    )
    back_qkv, back_out = (
        lax.all_gather(w_qkv, ("batch", "seq"), axis=0, tiled=True),
        lax.all_gather(w_out, ("batch", "seq"), axis=0, tiled=True),
    )
    resid_low = grad_resid.astype(jnp.bfloat16)
    g_out = contract_rows(branch_low, resid_low)
    out_shift_grad = jnp.sum(resid_low.astype(jnp.float32), axis=0)
    grad_branch = times_transpose(resid_low, back_out)
    grad_attn, gain2_grad, shift2_grad = norm_back(norm2_n, norm2_i, gain_rows[1], grad_branch)
    attn_grad_low = grad_attn.astype(jnp.bfloat16).reshape(seqs_here, local_len, HEADS, HEAD_DIM)
    row_dots = jnp.einsum("gqhd,gqhd->ghq", attn_grad_low.astype(jnp.float32), attn_heads)
    key_part = lax.all_gather(key_rot, "seq", axis=1, tiled=True)
    val_part = lax.all_gather(value_low, "seq", axis=1, tiled=True)
    key_rows = key_part.shape[1]
    key_rows = key_part.shape[1]
    allowed = key_mask(key_rows)
    key_heads = key_part.reshape(seqs_here, key_rows, HEADS, HEAD_DIM)
    val_heads = val_part.reshape(seqs_here, key_rows, HEADS, HEAD_DIM)
    scores = (
        jnp.einsum("gqhd,gkhd->ghqk", query_heads, key_heads, preferred_element_type=jnp.float32)
        * head_scale
    )
    weights = jnp.where(allowed[:, None], jnp.exp(scores - log_total[..., None]), 0.0)
    grad_weights = jnp.einsum(
        "gqhd,gkhd->ghqk", attn_grad_low, val_heads, preferred_element_type=jnp.float32
    )
    grad_scores = (weights * (grad_weights - row_dots[..., None])).astype(jnp.bfloat16)
    query_add = head_scale * jnp.einsum(
        "ghqk,gkhd->gqhd", grad_scores, key_heads, preferred_element_type=jnp.float32
    )
    key_new = (
        head_scale
        * jnp.einsum(
            "ghqk,gqhd->gkhd", grad_scores, query_heads, preferred_element_type=jnp.float32
        )
    ).reshape(seqs_here, key_rows, D)
    val_new = jnp.einsum(
        "ghqk,gqhd->gkhd",
        weights.astype(jnp.bfloat16),
        attn_grad_low,
        preferred_element_type=jnp.float32,
    ).reshape(seqs_here, key_rows, D)
    query_add, key_new, val_new = (query_add, key_new, val_new)
    key_accum = key_new
    val_accum = val_new
    grad_query, key_accum, val_accum = (query_add, key_accum, val_accum)
    key_sum, val_sum = (
        lax.psum_scatter(
            key_accum.astype(jnp.bfloat16), "seq", scatter_dimension=1, tiled=True
        ).astype(jnp.float32),
        lax.psum_scatter(
            val_accum.astype(jnp.bfloat16), "seq", scatter_dimension=1, tiled=True
        ).astype(jnp.float32),
    )
    grad_qrot = turn_back(grad_query.reshape(seqs_here, local_len, D), cosine, sine_vals, scales)
    grad_krot = turn_back(key_sum, cosine, sine_vals, 1.0 / scales)
    grad_qkv = (
        jnp.concatenate([grad_qrot, grad_krot, val_sum], axis=-1)
        .reshape(row_total, 3 * D)
        .astype(jnp.bfloat16)
    )
    g_qkv = contract_rows(input_low, grad_qkv)
    qkv_shift_grad = jnp.sum(grad_qkv.astype(jnp.float32), axis=0).reshape(3, D)
    grad_in = times_transpose(grad_qkv, back_qkv)
    grad_norm1, gain1_grad, shift1_grad = norm_back(norm1_n, norm1_i, gain_rows[0], grad_in)
    grad_total = grad_resid + grad_norm1
    gains_grad = jnp.stack([gain1_grad, gain2_grad, gain3_grad])
    shifts_grad = jnp.stack(
        [shift1_grad, shift2_grad, shift3_grad, out_shift_grad, down_shift_grad]
    )
    attn_sums = (
        lax.psum_scatter(g_qkv, ("batch", "seq"), scatter_dimension=0, tiled=True),
        lax.psum_scatter(g_out, ("batch", "seq"), scatter_dimension=0, tiled=True),
        lax.psum_scatter(qkv_shift_grad, ("batch", "seq"), scatter_dimension=1, tiled=True),
        lax.psum_scatter(gains_grad, ("batch", "seq"), scatter_dimension=1, tiled=True),
        lax.psum_scatter(shifts_grad, ("batch", "seq"), scatter_dimension=1, tiled=True),
    )
    return (
        result.reshape(seqs_here, local_len, D).astype(jnp.bfloat16),
        grad_total.reshape(seqs_here, local_len, D),
        attn_sums[0],
        attn_sums[2],
        attn_sums[1],
        ffn_sums[0],
        ffn_sums[1],
        attn_sums[3],
        attn_sums[4],
        ffn_sums[2],
        ffn_sums[3],
    )


def solution(mesh):
    return jax.shard_map(
        local,
        mesh=mesh,
        in_specs=(
            P("batch", "seq", None),
            P("batch", "seq", None),
            P(("batch", "seq"), None),
            P(None, ("batch", "seq")),
            P(("batch", "seq"), None),
            P(("batch", "seq"), None),
            P(("batch", "seq"), None),
            P(None, ("batch", "seq")),
            P(None, ("batch", "seq")),
            P(("batch", "seq")),
            P(None, ("batch", "seq")),
            P("batch"),
            P("batch", None),
            P("batch", None),
        ),
        out_specs=(
            P("batch", "seq", None),
            P("batch", "seq", None),
            P(("batch", "seq"), None),
            P(None, ("batch", "seq")),
            P(("batch", "seq"), None),
            P(("batch", "seq"), None),
            P(("batch", "seq"), None),
            P(None, ("batch", "seq")),
            P(None, ("batch", "seq")),
            P(("batch", "seq")),
            P(None, ("batch", "seq")),
        ),
        check_vma=False,
    )
```

profile of v0, /device:TPU:1, one launch (start us, length us, event | category | flops | bytes accessed | tf_op | source)
XLA Modules:
  0.0 5488.7 jit_solution(15556540422887311303)
XLA Ops:
  8.0 66.1 %all-gather.1 = bf16[32,64,5]{1,2,0:T(8,128)(2,1)S(1)} all-gather(bf16[1,64,5]{1,2,0:T(8,128)(2,1)} %bitcast.265), channel_id=1, replica_groups=mesh['batch'=8,'seq'=4] {'batch','seq'}, dimensions={0}, use_global_device_ids=true | all-gather | bytes 21120 | tf_op jit(solution)/shard_map/all_gather | solution.py:126
  74.2 65.2 %all-gather.2 = bf16[32,64,3]{1,2,0:T(4,128)(2,1)S(1)} all-gather(bf16[1,64,3]{1,2,0:T(4,128)(2,1)} %bitcast.268), channel_id=1, replica_groups=mesh['batch'=8,'seq'=4] {'batch','seq'}, dimensions={0}, use_global_device_ids=true | all-gather | bytes 12672 | tf_op jit(solution)/shard_map/all_gather | solution.py:124
  139.5 66.2 %all-gather = bf16[32,64,3]{1,2,0:T(4,128)(2,1)S(1)} all-gather(bf16[1,64,3]{1,2,0:T(4,128)(2,1)} %bitcast.269), channel_id=1, replica_groups=mesh['batch'=8,'seq'=4] {'batch','seq'}, dimensions={0}, use_global_device_ids=true | all-gather | bytes 12672 | tf_op jit(solution)/shard_map/all_gather | solution.py:125
  244.5 31.0 fusion.57
  281.9 63.3 %all-gather.3 = bf16[32,1,256]{2,1,0:T(2,128)(2,1)S(1)} all-gather(bf16[1,1,256]{2,1,0:T(2,128)(2,1)S(1)} %reshape.1363), channel_id=1, replica_groups=mesh['batch'=8,'seq'=4] {'batch','seq'}, dimensions={0}, use_global_device_ids=true | all-gather | bytes 16896 | tf_op jit(solution)/shard_map/all_gather | solution.py:175
  345.8 66.0 %all_gather.47 = bf16[2,8192]{1,0:T(2,128)(2,1)S(1)} all-gather(bf16[2,256]{1,0:T(2,128)(2,1)S(1)} %copy-done.82), channel_id=1, replica_groups=mesh['batch'=8,'seq'=4] {'batch','seq'}, dimensions={1}, use_global_device_ids=true | all-gather | bytes 33792 | tf_op jit(solution)/shard_map/all_gather | solution.py:176
  466.5 49.1 select_reduce_fusion
  515.6 43.0 fusion.1
  559.3 52.4 fusion.141
  631.3 99.8 %all-gather.19.cloned.1.call-done = bf16[2048,8192]{1,0:T(8,128)(2,1)} async-done(((bf16[64,8192]{1,0:T(8,128)(2,1)}), bf16[2048,8192]{1,0:T(8,128)(2,1)}) %all-gather.19.cloned.1.call-update) | async-done | bytes 33554448 | tf_op jit(solution)/shard_map/all_gather | solution.py:173
  772.3 154.5 %all-gather.21.cloned.1.call-done = bf16[8192,2048]{1,0:T(8,128)(2,1)} async-done(((bf16[256,2048]{1,0:T(8,128)(2,1)}), bf16[8192,2048]{1,0:T(8,128)(2,1)}) %all-gather.21.cloned.1.call-update) | async-done | bytes 33554448 | tf_op jit(solution)/shard_map/all_gather | solution.py:174
  1032.1 80.8 %multiply_convert_fusion = bf16[32,512,2048]{2,1,0:T(8,128)(2,1)} fusion(f32[32,512,2048]{2,1,0:T(8,128)} %get-tuple-element.71, f32[32,512]{1,0:T(8,128)S(1)} %fusion.72, f32[32,512]{1,0:T(8,128)S(1)} %copy-done.47, pred[512,2048]{1,0:T(8,128)(4,1)S(1)} %copy-done.7, bf16[512,32,64]{0,2,1:T(8,128)(2,1)} %bitcast.207, bf16[2048,32,64]{0,2,1:T(8,128)(2,1)} %bitcast.210), kind=kOutput, calls=%fused_computation | convolution fusion | flops 4496293888 | bytes 212992000 | tf_op jit(solution)/shard_map/gqhd,gkhd->ghqk/dot_general | solution.py:238
  1154.1 51.6 fusion.30
  1218.1 32.2 broadcast_multiply_fusion
  1427.1 32.2 fusion.130
  1461.0 33.7 fusion.82
  1495.5 39.3 all-reduce
  1535.5 37.1 fusion.75
  1602.3 131.9 %reduce-scatter.33.cloned.1.call-done = f32[64,3]{1,0:T(8,128)} async-done(((f32[2048,3]{1,0:T(8,128)}), f32[64,3]{1,0:T(8,128)}) %reduce-scatter.33.cloned.1.call-update) | async-done | bytes 784
  1735.6 131.7 %reduce-scatter.35.cloned.1.call-done = f32[64,5]{1,0:T(8,128)} async-done(((f32[2048,5]{1,0:T(8,128)}), f32[64,5]{1,0:T(8,128)}) %reduce-scatter.35.cloned.1.call-update) | async-done | bytes 1296
  1868.7 359.8 %reduce-scatter.25.cloned.1.call-done = f32[64,2048]{1,0:T(8,128)} async-done(((f32[2048,2048]{1,0:T(8,128)}), f32[64,2048]{1,0:T(8,128)}) %reduce-scatter.25.cloned.1.call-update) | async-done | bytes 524304 | tf_op jit(solution)/shard_map/reduce_scatter | solution.py:287
  2228.5 441.2 %reduce-scatter.23.cloned.1.call-done = f32[64,6144]{1,0:T(8,128)} async-done(((f32[2048,6144]{1,0:T(8,128)}), f32[64,6144]{1,0:T(8,128)}) %reduce-scatter.23.cloned.1.call-update) | async-done | bytes 1572880 | tf_op jit(solution)/shard_map/reduce_scatter | solution.py:286
  2669.7 1404.9 %reduce-scatter.27.cloned.1.call-done = f32[64,8192]{1,0:T(8,128)} async-done(((f32[2048,8192]{1,0:T(8,128)}), f32[64,8192]{1,0:T(8,128)}) %reduce-scatter.27.cloned.1.call-update) | async-done | bytes 2097168 | tf_op jit(solution)/shard_map/reduce_scatter | solution.py:205
  4074.5 1407.4 %reduce-scatter.29.cloned.1.call-done = f32[256,2048]{1,0:T(8,128)} async-done(((f32[8192,2048]{1,0:T(8,128)}), f32[256,2048]{1,0:T(8,128)}) %reduce-scatter.29.cloned.1.call-update) | async-done | bytes 2097168 | tf_op jit(solution)/shard_map/reduce_scatter | solution.py:206
  (309 shorter events, 532.5 us)
Async XLA Ops:
  7.2 200.7 %copy-start.2 = (bf16[1,512,2048]{2,1,0:T(8,128)(2,1)S(1)}, bf16[1,512,2048]{2,1,0:T(8,128)(2,1)}, u32[]{:S(2)}) copy-start(bf16[1,512,2048]{2,1,0:T(8,128)(2,1)} %param.14) | copy-start | bytes 6291460
  7.2 202.7 %all-gather.11.cloned.1.call-start = ((), (), s32[]{:S(2)}) async-start(), calls=%async_computation.10 | async-start | bytes 25952256 | tf_op jit(solution)/shard_map/all_gather | solution.py:122
  7.9 410.0 %all-gather.13.cloned.1.call-start = ((), (), s32[]{:S(2)}) async-start(), calls=%async_computation.11 | async-start | bytes 10485760 | tf_op jit(solution)/shard_map/all_gather | solution.py:140
  275.6 178.7 %all-gather.15.cloned.1.call-start = ((), (), s32[]{:S(2)}) async-start(), calls=%async_computation.12 | async-start | bytes 10485760 | tf_op jit(solution)/shard_map/all_gather | solution.py:141
  279.5 340.6 %all-gather.17.cloned.1.call-start = ((), (), s32[]{:S(2)}) async-start(), calls=%async_computation.13 | async-start | bytes 8650752 | tf_op jit(solution)/shard_map/all_gather | solution.py:123
  280.0 451.0 %all-gather.19.cloned.1.call-start = ((), (), s32[]{:S(2)}) async-start(), calls=%async_computation.14 | async-start | bytes 34603008 | tf_op jit(solution)/shard_map/all_gather | solution.py:173
  280.6 646.2 %all-gather.21.cloned.1.call-start = ((), (), s32[]{:S(2)}) async-start(), calls=%async_computation.15 | async-start | bytes 34603008 | tf_op jit(solution)/shard_map/all_gather | solution.py:174
  281.2 977.8 %reduce-scatter.19.cloned.1.call-start = ((), (), s32[]{:S(2)}) async-start(), calls=%async_computation.16 | async-start | bytes 10485760 | tf_op jit(solution)/shard_map/reduce_scatter | solution.py:262
  617.2 405.7 %copy-start.63 = (f32[512]{0:T(512)}, f32[512]{0:T(512)S(1)}, u32[]{:S(2)}) copy-start(f32[512]{0:T(512)S(1)} %broadcast_multiply_fusion.11) | copy-start | bytes 6148
  620.0 402.8 %copy-start.69 = (f32[512]{0:T(512)}, f32[512]{0:T(512)S(1)}, u32[]{:S(2)}) copy-start(f32[512]{0:T(512)S(1)} %add_rsqrt_fusion.2) | copy-start | bytes 6148
  628.8 378.7 %copy-start.24 = (f32[512]{0:T(512)}, f32[512]{0:T(512)S(1)}, u32[]{:S(2)}) copy-start(f32[512]{0:T(512)S(1)} %broadcast_multiply_fusion.10) | copy-start | bytes 6148
  631.3 376.3 %copy-start.32 = (f32[512]{0:T(512)}, f32[512]{0:T(512)S(1)}, u32[]{:S(2)}) copy-start(f32[512]{0:T(512)S(1)} %add_rsqrt_fusion.1) | copy-start | bytes 6148
  761.8 195.1 %copy-start.65 = (f32[512]{0:T(512)}, f32[512]{0:T(512)S(1)}, u32[]{:S(2)}) copy-start(f32[512]{0:T(512)S(1)} %broadcast_multiply_fusion.3) | copy-start | bytes 6148
  761.8 165.0 %copy-start.17 = (bf16[1,512,2048]{2,1,0:T(8,128)(2,1)S(1)}, bf16[1,512,2048]{2,1,0:T(8,128)(2,1)}, u32[]{:S(2)}) copy-start(bf16[1,512,2048]{2,1,0:T(8,128)(2,1)} %param.15) | copy-start | bytes 6291460
  772.3 184.6 %copy-start.67 = (f32[512]{0:T(512)}, f32[512]{0:T(512)S(1)}, u32[]{:S(2)}) copy-start(f32[512]{0:T(512)S(1)} %add_rsqrt_fusion) | copy-start | bytes 6148
  1152.5 174.1 %reduce-scatter.21.cloned.1.call-start = ((), (), s32[]{:S(2)}) async-start(), calls=%async_computation.17 | async-start | bytes 10485760 | tf_op jit(solution)/shard_map/reduce_scatter | solution.py:265
  1218.1 354.5 %reduce-scatter.37.cloned.1.call-start = ((), (), s32[]{:S(2)}) async-start(), calls=%async_computation.25 | async-start | bytes 4325376
  1258.7 342.2 %reduce-scatter.31.cloned.1.call-start = ((), (), s32[]{:S(2)}) async-start(), calls=%async_computation.22 | async-start | bytes 1081344
  1332.2 402.0 %reduce-scatter.33.cloned.1.call-start = ((), (), s32[]{:S(2)}) async-start(), calls=%async_computation.23 | async-start | bytes 1081344
  1356.3 511.0 %reduce-scatter.35.cloned.1.call-start = ((), (), s32[]{:S(2)}) async-start(), calls=%async_computation.24 | async-start | bytes 1081344
  1357.8 870.7 %reduce-scatter.25.cloned.1.call-start = ((), (), s32[]{:S(2)}) async-start(), calls=%async_computation.19 | async-start | bytes 17301504 | tf_op jit(solution)/shard_map/reduce_scatter | solution.py:287
  1371.9 1297.8 %reduce-scatter.23.cloned.1.call-start = ((), (), s32[]{:S(2)}) async-start(), calls=%async_computation.18 | async-start | bytes 51904512 | tf_op jit(solution)/shard_map/reduce_scatter | solution.py:286
  1426.5 2648.1 %reduce-scatter.27.cloned.1.call-start = ((), (), s32[]{:S(2)}) async-start(), calls=%async_computation.20 | async-start | bytes 69206016 | tf_op jit(solution)/shard_map/reduce_scatter | solution.py:205
  1459.4 4022.5 %reduce-scatter.29.cloned.1.call-start = ((), (), s32[]{:S(2)}) async-start(), calls=%async_computation.21 | async-start | bytes 69206016 | tf_op jit(solution)/shard_map/reduce_scatter | solution.py:206
  (80 other events, 1980.1 us)
Sparse Core Ops, SparseCore 0:
  10.9 158.1 all-gather.10
  275.6 88.2 all-gather.12
  366.4 87.7 all-gather.14
  456.9 77.9 all-gather.16
  537.7 193.3 all-gather.18
  733.8 192.9 all-gather.20
  1152.7 84.1 reduce-scatter.18
  1240.2 86.4 reduce-scatter.20
  1328.9 137.1 reduce-scatter.36
  1468.2 132.6 reduce-scatter.30
  1603.3 130.9 reduce-scatter.32
  1736.3 130.9 reduce-scatter.34
  1870.3 358.2 reduce-scatter.24
  2236.5 433.1 reduce-scatter.22
  2672.6 1401.9 reduce-scatter.26
  4077.4 1404.4 reduce-scatter.28
where the time goes:
time: 5500 us; the launch traced here: 5490 us
  waiting for transfers between devices  4180 us (76%)
  matrix products  587 us (11%)
  blocking collectives  366 us (7%)
  other arithmetic  206 us (4%)
  local copies, waits for them, and re-layouts  129 us (2%)
    reduce_scatter x1, waiting for transfers between devices, local(): lax.psum_scatter(g_down, ('batch', 'seq'), scatter_dimension=0, tiled=True)  1410 us
    reduce_scatter x1, waiting for transfers between devices, local(): lax.psum_scatter(g_up, ('batch', 'seq'), scatter_dimension=0, tiled=True)  1400 us
    reduce_scatter x1, waiting for transfers between devices, local(): lax.psum_scatter(g_qkv, ('batch', 'seq'), scatter_dimension=0, tiled=True)  441 us
    reduce_scatter x1, waiting for transfers between devices, local(): lax.psum_scatter(g_out, ('batch', 'seq'), scatter_dimension=0, tiled=True)  360 us
    unnamed x20, waiting for transfers between devices  287 us
    all_gather x1, waiting for transfers between devices, local(): lax.all_gather(w_down, ('batch', 'seq'), axis=0, tiled=True)  154 us
  transfers between devices with their start and end apart: 16, of which 11 were waited for; matrix products, arithmetic and copies ran while one was open for 11% of the time, Pallas kernels for 0%

commit v1 on v0

v1 whole, which is shorter than its diff:
```python
import jax
import jax.numpy as jnp
from jax import lax
from jax.experimental import pallas as pl
from jax.experimental.pallas import tpu as pltpu
from jax.sharding import PartitionSpec as P

D = 2048
HEADS = 32
HEAD_DIM = 64
SEQ_LEN = 2048
SPAN = 64
BLK = 256
NEG_FILL = -1e30
NORM_EPS = 1e-05
EVERY = ("batch", "seq")


def nt(a, b):
    return lax.dot_general(a, b, (((1,), (1,)), ((), ())), preferred_element_type=jnp.float32)


def tn(a, b):
    return lax.dot_general(a, b, (((0,), (0,)), ((), ())), preferred_element_type=jnp.float32)


def nn(a, b):
    return jnp.dot(a, b, preferred_element_type=jnp.float32)


def launch(body, grid, ins, outs, scratch=(), prefetch=(), after=(), name=None, flops=0, moved=0):
    n_pre, n_in, n_after = len(prefetch), len(ins), len(after)

    def kernel(*refs):
        body(*refs[: n_pre + n_in], *refs[n_pre + n_in + n_after :])

    return pl.pallas_call(
        kernel,
        out_shape=tuple(jax.ShapeDtypeStruct(s, d) for s, d, _ in outs),
        grid_spec=pltpu.PrefetchScalarGridSpec(
            num_scalar_prefetch=n_pre,
            grid=grid,
            in_specs=[b for _, b in ins] + [pl.BlockSpec(memory_space=pl.ANY)] * n_after,
            out_specs=[b for _, _, b in outs],
            scratch_shapes=list(scratch),
        ),
        compiler_params=pltpu.CompilerParams(vmem_limit_bytes=58 << 20),
        cost_estimate=pl.CostEstimate(flops=flops, bytes_accessed=moved, transcendentals=0),
        name=name,
    )(*prefetch, *(a for a, _ in ins), *after)


def tile(rows, cols):
    return pl.BlockSpec((rows, cols), lambda i, *_: (i, 0))


def fixed(array):
    zeros = (0,) * array.ndim
    return (array, pl.BlockSpec(array.shape, lambda *_: zeros, pipeline_mode=pl.Buffered(1)))


def columns(lines):
    count, width = len(lines), lines[0].shape[1]
    pad = [jnp.zeros((8 - count, width), jnp.float32)] if count < 8 else []
    flat = jnp.concatenate(list(lines) + pad, axis=0).T
    return [flat[:, i : i + 1] for i in range(count)]


def joined(centers, squares, width):
    count = len(centers)
    center = sum(centers) * (1.0 / count)
    total = sum(squares) + width * sum((c - center) ** 2 for c in centers)
    return center, lax.rsqrt(total * (1.0 / (width * count)) + NORM_EPS)


def rotate(value, tables, sign):
    straight, from_right, from_left = tables
    turned = pltpu.roll(value, 127, 1) * from_right + pltpu.roll(value, 1, 1) * from_left
    return value * straight + turned if sign > 0 else value * straight - turned


def qkv_project(low, weight, bias, tables):
    rows, width = low.shape
    cols = weight.shape[1] // 3

    def body(low_ref, w_ref, b_ref, *rest):
        table_refs, outs = rest[:6], rest[6:]
        for part in range(3):
            span = slice(part * cols, (part + 1) * cols)
            value = nn(low_ref[...], w_ref[:, span]) + b_ref[:, span]
            if part == 2:
                outs[2][...] = value.astype(jnp.bfloat16)
                continue
            own = [t[...] for t in table_refs[3 * part : 3 * part + 3]]
            for at in range(0, cols, 128):
                outs[part][:, at : at + 128] = rotate(value[:, at : at + 128], own, 1).astype(jnp.bfloat16)

    return launch(
        body,
        (rows // BLK,),
        [(low, tile(BLK, width)), fixed(weight), fixed(bias)] + [(t, tile(BLK, 128)) for t in tables],
        [((rows, cols), jnp.bfloat16, tile(BLK, cols))] * 3,
        name="qkv_project",
        flops=2 * rows * width * 3 * cols,
        moved=rows * width * 4,
    )


def attention_fwd(q, k, v, lo, hi, slots, first, last):
    rows, width = q.shape
    blocks = rows // BLK
    heads = width // HEAD_DIM
    extra = 16

    def body(slots, first, last, q_ref, k_ref, v_ref, lo_ref, hi_ref, o_ref, lse_ref, stat_ref, vt, acc, qt, kept):
        step = pl.program_id(0)

        @pl.when(step == 0)
        def _():
            for i in range(blocks):
                at = slice(i * BLK, (i + 1) * BLK)
                flat = v_ref[at, :].T
                for h in range(heads):
                    vt[h, :HEAD_DIM, at] = flat[h * HEAD_DIM : (h + 1) * HEAD_DIM]
                    vt[h, HEAD_DIM:, at] = jnp.ones((extra, BLK), jnp.bfloat16)

        flat = (q_ref[...] * jnp.bfloat16(HEAD_DIM**-0.5)).T
        zero = jnp.zeros((HEAD_DIM, BLK), jnp.bfloat16)
        for h in range(heads):
            mine = flat[h * HEAD_DIM : (h + 1) * HEAD_DIM, :]
            qt[h] = jnp.concatenate([mine, zero] if h % 2 == 0 else [zero, mine], axis=0)
        low, high = lo_ref[...], hi_ref[...]
        key_row = lax.broadcasted_iota(jnp.int32, (BLK, BLK), 0)

        def scores(kb, peaks):
            at = pl.ds(pl.multiple_of(slots[kb] * BLK, BLK), BLK)
            spot = key_row + kb * BLK
            seen = (spot >= low) & (spot <= high)
            out = []
            for h in range(heads):
                two = slice(h // 2 * 128, h // 2 * 128 + 128)
                s = jnp.where(seen, nn(k_ref[at, two], qt[h]), NEG_FILL)
                kept[kb, h] = s
                out.append(jnp.maximum(peaks[h], jnp.max(s, axis=0, keepdims=True)))
            return tuple(out)

        start = tuple(jnp.full((1, BLK), NEG_FILL, jnp.float32) for _ in range(heads))
        peaks = lax.fori_loop(first[step], last[step], scores, start)
        acc[...] = jnp.zeros_like(acc)

        def weigh(kb, _):
            at = pl.ds(pl.multiple_of(slots[kb] * BLK, BLK), BLK)
            for h in range(heads):
                p = jnp.exp(kept[kb, h] - peaks[h]).astype(jnp.bfloat16)
                acc[h] += nn(vt[h, :, at], p)
            return 0

        lax.fori_loop(first[step], last[step], weigh, 0)
        parts = []
        for h in range(heads):
            total = acc[h, HEAD_DIM : HEAD_DIM + 1, :]
            lse_ref[h : h + 1, :] = peaks[h] + jnp.log(total)
            parts.append(acc[h, :HEAD_DIM] / total)
        flat = jnp.concatenate(parts, axis=0)
        center = jnp.mean(flat, axis=0, keepdims=True)
        stat_ref[0:1, :] = center
        stat_ref[1:2, :] = jnp.sum((flat - center) ** 2, axis=0, keepdims=True)
        stat_ref[2:8, :] = jnp.zeros((6, BLK), jnp.float32)
        o_ref[...] = flat.T

    by_slot = pl.BlockSpec((BLK, width), lambda i, s, *_: (s[i], 0))
    line = pl.BlockSpec((1, BLK), lambda i, *_: (0, i))
    return launch(
        body,
        (blocks,),
        [(q, by_slot), fixed(k), fixed(v), (lo, line), (hi, line)],
        [
            ((rows, width), jnp.float32, by_slot),
            ((heads, rows), jnp.float32, pl.BlockSpec((heads, BLK), lambda i, s, *_: (0, s[i]))),
            ((8, rows), jnp.float32, pl.BlockSpec((8, BLK), lambda i, s, *_: (0, s[i]))),
        ],
        scratch=[
            pltpu.VMEM((heads, HEAD_DIM + extra, rows), jnp.bfloat16),
            pltpu.VMEM((heads, HEAD_DIM + extra, BLK), jnp.float32),
            pltpu.VMEM((heads, 128, BLK), jnp.bfloat16),
            pltpu.VMEM((blocks, heads, BLK, BLK), jnp.float32),
        ],
        prefetch=(slots, first, last),
        name="attention_forward",
        flops=4 * rows * rows * width,
        moved=rows * width * 12,
    )


def out_project(attn, stats, gain, shift, weight):
    rows, width = attn.shape
    wide = weight.shape[1]

    def body(a_ref, g_ref, s_ref, w_ref, *rest):
        stat_refs, (low_ref, part_ref) = rest[: len(stats)], rest[len(stats) :]
        center, inverse = columns(joined([r[0:1] for r in stat_refs], [r[1:2] for r in stat_refs], width))
        low = ((a_ref[...] - center) * inverse * g_ref[...] + s_ref[...]).astype(jnp.bfloat16)
        low_ref[...] = low
        part_ref[...] = nn(low, w_ref[...]).astype(jnp.bfloat16)

    return launch(
        body,
        (rows // BLK,),
        [(attn, tile(BLK, width)), fixed(gain), fixed(shift), fixed(weight)] + list(stats),
        [((rows, width), jnp.bfloat16, tile(BLK, width)), ((rows, wide), jnp.bfloat16, tile(BLK, wide))],
        name="out_project",
        flops=2 * rows * width * wide,
        moved=rows * (width * 6 + wide * 2),
    )


def own_rows(body, wholes, rows_in, terms, outs, sums=0, after=(), name=None):
    two, half, wide = rows_in[0].shape
    piece = min(128, half)
    count = len(terms[0])

    def kernel(*refs):
        whole_refs, refs = refs[: len(wholes)], refs[len(wholes) :]
        row_refs, refs = refs[: len(rows_in)], refs[len(rows_in) :]
        term_refs, out_refs = refs[: 2 * count], refs[2 * count :]
        vectors = [r[...] for r in whole_refs]
        added = [0.0] * sums
        for side in range(2):
            total = term_refs[side * count][...].astype(jnp.float32)
            for r in term_refs[side * count + 1 : (side + 1) * count]:
                total = total + r[...].astype(jnp.float32)
            values = body(vectors, [r[side] for r in row_refs], total)
            for ref, value in zip(out_refs, values[: len(outs)]):
                ref[side] = value.astype(ref.dtype)
            added = [a + jnp.sum(v, axis=0, keepdims=True) for a, v in zip(added, values[len(outs) :])]
        if sums:
            sum_ref = out_refs[len(outs)]

            @pl.when(pl.program_id(0) == 0)
            def _():
                sum_ref[...] = jnp.zeros_like(sum_ref)

            for i, a in enumerate(added):
                sum_ref[i : i + 1, :] += a

    own = pl.BlockSpec((2, piece, wide), lambda i: (0, i, 0))
    pieces = []
    for side in range(2):
        for array, start in terms[side]:
            pieces.append((array, pl.BlockSpec((piece, wide), lambda i, at=start // piece: (at + i, 0))))
    results = [((2, half, wide), d, own) for d in outs]
    if sums:
        results.append(((8, wide), jnp.float32, pl.BlockSpec((8, wide), lambda i: (0, 0))))
    return launch(
        kernel,
        (half // piece,),
        [fixed(w) for w in wholes] + [(r, own) for r in rows_in] + pieces,
        results,
        after=after,
        name=name,
        flops=40 * half * wide,
        moved=half * wide * 16,
    )


def norm_parts(values):
    center = jnp.mean(values, axis=-1, keepdims=True)
    spread = values - center
    inverse = lax.rsqrt(jnp.mean(spread * spread, axis=-1, keepdims=True) + NORM_EPS)
    return spread * inverse, inverse


def norm_lower(normed, inverse, gain, upper):
    scaled = upper * gain
    first_mean = jnp.mean(scaled, axis=-1, keepdims=True)
    second_mean = jnp.mean(scaled * normed, axis=-1, keepdims=True)
    return inverse * (scaled - first_mean - normed * second_mean)


GELU_A = 0.044715
GELU_C = 0.7978845608028654


def ffn_up(mid, cot, w_up, w_down, bias, gain, after=()):
    rows, wide = mid.shape
    units = w_up.shape[1]
    chunk = min(512, units)

    def body(m_ref, c_ref, u_w, d_w, b_ref, g_ref, up_ref, grad_ref, stat_ref, gel_ref):
        total = scaled_total = 0.0
        for at in range(0, units, chunk):
            span = slice(at, at + chunk)
            up = nn(m_ref[...], u_w[:, span]) + b_ref[:, span]
            grad = nt(c_ref[...], d_w[span, :])
            up_ref[:, span] = up
            grad_ref[:, span] = grad
            gel = 0.5 * up * (1.0 + jnp.tanh(GELU_C * (up + GELU_A * up * up * up)))
            gel_ref[:, span] = gel
            total = total + jnp.sum(gel, axis=1, keepdims=True)
            scaled_total = scaled_total + jnp.sum(grad * g_ref[:, span], axis=1, keepdims=True)
        center = total * (1.0 / units)
        square = product = 0.0
        for at in range(0, units, chunk):
            span = slice(at, at + chunk)
            spread = gel_ref[:, span] - center
            square = square + jnp.sum(spread * spread, axis=1, keepdims=True)
            product = product + jnp.sum(grad_ref[:, span] * g_ref[:, span] * spread, axis=1, keepdims=True)
        lane = lax.broadcasted_iota(jnp.int32, (BLK, 128), 1)
        flat = jnp.zeros((BLK, 128), jnp.float32)
        for i, value in enumerate((center, square, scaled_total, product)):
            flat = jnp.where(lane == i, value, flat)
        stat_ref[...] = flat.T[0:8, :]

    return launch(
        body,
        (rows // BLK,),
        [(mid, tile(BLK, wide)), (cot, tile(BLK, wide)), fixed(w_up), fixed(w_down), fixed(bias), fixed(gain)],
        [
            ((rows, units), jnp.float32, tile(BLK, units)),
            ((rows, units), jnp.float32, tile(BLK, units)),
            ((8, rows), jnp.float32, pl.BlockSpec((8, BLK), lambda i, *_: (0, i))),
        ],
        scratch=[pltpu.VMEM((BLK, units), jnp.float32)],
        after=after,
        name="ffn_up",
        flops=4 * rows * wide * units,
        moved=rows * (wide * 4 + units * 8),
    )


def ffn_mid(up, grad, stats, gain, shift, w_up):
    rows, units = up.shape
    wide = w_up.shape[0]
    chunk = min(512, units)
    ranks = len(stats)

    def body(u_ref, f_ref, g_ref, s_ref, w_ref, *rest):
        stat_refs, (low_ref, gup_ref, part_ref, sum_ref) = rest[:ranks], rest[ranks:]
        centers = [r[0:1] for r in stat_refs]
        center, inverse = joined(centers, [r[1:2] for r in stat_refs], units)
        share = 1.0 / (units * ranks)
        first = sum(r[2:3] for r in stat_refs) * share
        second = inverse * share * sum(r[3:4] + (c - center) * r[2:3] for r, c in zip(stat_refs, centers))
        center, inverse, first, second = columns([center, inverse, first, second])

        @pl.when(pl.program_id(0) == 0)
        def _():
            sum_ref[...] = jnp.zeros_like(sum_ref)

        for at in range(0, units, chunk):
            span = slice(at, at + chunk)
            u, f = u_ref[:, span], f_ref[:, span]
            squared = u * u
            t = jnp.tanh(GELU_C * u * (1.0 + GELU_A * squared))
            one = 0.5 * (1.0 + t)
            slope = one + 0.5 * u * (1.0 - t * t) * (GELU_C * (1.0 + 3.0 * GELU_A * squared))
            normed = (u * one - center) * inverse
            low_ref[:, span] = (normed * g_ref[:, span] + s_ref[:, span]).astype(jnp.bfloat16)
            lower = inverse * (f * g_ref[:, span] - first - normed * second)
            gup = (lower * slope).astype(jnp.bfloat16)
            gup_ref[:, span] = gup
            sum_ref[0:1, span] += jnp.sum(f * normed, axis=0, keepdims=True)
            sum_ref[1:2, span] += jnp.sum(f, axis=0, keepdims=True)
            sum_ref[2:3, span] += jnp.sum(gup.astype(jnp.float32), axis=0, keepdims=True)
        part_ref[...] = nt(gup_ref[...], w_ref[...]).astype(jnp.bfloat16)

    return launch(
        body,
        (rows // BLK,),
        [(up, tile(BLK, units)), (grad, tile(BLK, units)), fixed(gain), fixed(shift), fixed(w_up)] + list(stats),
        [
            ((rows, units), jnp.bfloat16, tile(BLK, units)),
            ((rows, units), jnp.bfloat16, tile(BLK, units)),
            ((rows, wide), jnp.bfloat16, tile(BLK, wide)),
            ((8, units), jnp.float32, pl.BlockSpec((8, units), lambda i, *_: (0, 0))),
        ],
        name="ffn_mid",
        flops=2 * rows * wide * units,
        moved=rows * (wide * 2 + units * 12),
    )


def branch_back(resid, w_out, attn, stats, gain, after=()):
    rows, wide = resid.shape
    width = attn.shape[1]
    ranks = len(stats)

    def body(r_ref, w_ref, a_ref, g_ref, *rest):
        stat_refs, (grad_ref, stat_ref, sum_ref) = rest[:ranks], rest[ranks:]
        center, inverse = columns(joined([r[0:1] for r in stat_refs], [r[1:2] for r in stat_refs], width))

        @pl.when(pl.program_id(0) == 0)
        def _():
            sum_ref[...] = jnp.zeros_like(sum_ref)

        grad = nt(r_ref[...], w_ref[...])
        grad_ref[...] = grad
        normed = (a_ref[...] - center) * inverse
        scaled = grad * g_ref[...]
        sum_ref[0:1, :] += jnp.sum(grad * normed, axis=0, keepdims=True)
        sum_ref[1:2, :] += jnp.sum(grad, axis=0, keepdims=True)
        lane = lax.broadcasted_iota(jnp.int32, (BLK, 128), 1)
        flat = jnp.where(lane == 0, jnp.sum(scaled, axis=1, keepdims=True), 0.0)
        flat = jnp.where(lane == 1, jnp.sum(scaled * normed, axis=1, keepdims=True), flat)
        stat_ref[...] = flat.T[0:8, :]

    return launch(
        body,
        (rows // BLK,),
        [(resid, tile(BLK, wide)), fixed(w_out), (attn, tile(BLK, width)), fixed(gain)] + list(stats),
        [
            ((rows, width), jnp.float32, tile(BLK, width)),
            ((8, rows), jnp.float32, pl.BlockSpec((8, BLK), lambda i, *_: (0, i))),
            ((8, width), jnp.float32, pl.BlockSpec((8, width), lambda i, *_: (0, 0))),
        ],
        after=after,
        name="branch_back",
        flops=2 * rows * wide * width,
        moved=rows * (wide * 2 + width * 8),
    )


def attn_grad(grad, attn, stats, sums, gain, after=()):
    rows, width = attn.shape
    ranks = len(stats)
    heads = width // HEAD_DIM

    def body(f_ref, a_ref, g_ref, *rest):
        stat_refs, sum_refs = rest[:ranks], rest[ranks : 2 * ranks]
        out_ref, dot_ref = rest[2 * ranks :]
        center, inverse = joined([r[0:1] for r in stat_refs], [r[1:2] for r in stat_refs], width)
        share = 1.0 / (width * ranks)
        first = sum(r[0:1] for r in sum_refs) * share
        second = sum(r[1:2] for r in sum_refs) * share
        center, inverse, first, second = columns([center, inverse, first, second])
        attn_here = a_ref[...]
        normed = (attn_here - center) * inverse
        out = (inverse * (f_ref[...] * g_ref[...] - first - normed * second)).astype(jnp.bfloat16)
        out_ref[...] = out
        product = (out.astype(jnp.float32) * attn_here).T
        for h in range(heads):
            dot_ref[h : h + 1, :] = jnp.sum(product[h * HEAD_DIM : (h + 1) * HEAD_DIM], axis=0, keepdims=True)

    return launch(
        body,
        (rows // BLK,),
        [(grad, tile(BLK, width)), (attn, tile(BLK, width)), fixed(gain)] + list(stats) + list(sums),
        [
            ((rows, width), jnp.bfloat16, tile(BLK, width)),
            ((heads, rows), jnp.float32, pl.BlockSpec((heads, BLK), lambda i, *_: (0, i))),
        ],
        after=after,
        name="attn_grad",
        flops=20 * rows * width,
        moved=rows * width * 10,
    )


def attention_bwd(q, k, v, g, lse, dot, lo, hi, tables, slots, first, last, after=()):
    rows, width = q.shape
    blocks = rows // BLK
    heads = width // HEAD_DIM
    scale = HEAD_DIM**-0.5

    def body(slots, first, last, q_ref, k_ref, v_ref, g_ref, lse_ref, dot_ref, lo_ref, hi_ref, *rest):
        table_refs, (out_ref, dqt, qt, gt, accs) = rest[:6], rest[6:]
        key_row = lax.broadcasted_iota(jnp.int32, (BLK, BLK), 0)
        lane = lax.broadcasted_iota(jnp.int32, (BLK, 128), 1)
        zero = jnp.zeros((), jnp.bfloat16)
        dqt[...] = jnp.zeros_like(dqt)
        for i in range(blocks):
            at = slice(i * BLK, (i + 1) * BLK)
            qt[:, at] = q_ref[at, :].T
            gt[:, at] = g_ref[at, :].T

        def outer(kb, _):
            rows_k = pl.ds(pl.multiple_of(slots[kb] * BLK, BLK), BLK)
            k, v = k_ref[rows_k, :] * jnp.bfloat16(scale), v_ref[rows_k, :]
            kts = k.T
            spot = key_row + kb * BLK

            def halves(x, h):
                x = x[:, h // 2 * 128 : h // 2 * 128 + 128]
                return jnp.where((lane < HEAD_DIM) == (h % 2 == 0), x, zero)

            ks = [halves(k, h) for h in range(heads)]
            vs = [halves(v, h) for h in range(heads)]
            accs[...] = jnp.zeros_like(accs)

            def inner(qb, _):
                at = pl.ds(pl.multiple_of(slots[qb] * BLK, BLK), BLK)
                here = pl.ds(pl.multiple_of(qb * BLK, BLK), BLK)
                seen = (spot >= lo_ref[0:1, here]) & (spot <= hi_ref[0:1, here])
                for h in range(heads):
                    two = slice(h // 2 * 128, h // 2 * 128 + 128)
                    span = slice(h * HEAD_DIM, (h + 1) * HEAD_DIM)
                    s = nn(ks[h], qt[two, at])
                    p = jnp.where(seen, jnp.exp(s - lse_ref[h : h + 1, at]), 0.0)
                    dp = nn(vs[h], gt[two, at])
                    ds = (p * (dp - dot_ref[h : h + 1, at])).astype(jnp.bfloat16)
                    accs[1, h] += nn(p.astype(jnp.bfloat16), g_ref[at, two])
                    accs[0, h] += nn(ds, q_ref[at, two])
                    dqt[span, at] += nn(kts[span, :], ds)
                return 0

            lax.fori_loop(first[kb], last[kb], inner, 0)
            own = [t[rows_k, :] for t in table_refs[3:]]
            for h in range(0, heads, 2):
                at = h * HEAD_DIM
                grad_k = jnp.where(lane < HEAD_DIM, accs[0, h], accs[0, h + 1]) * scale
                grad_v = jnp.where(lane < HEAD_DIM, accs[1, h], accs[1, h + 1])
                out_ref[rows_k, width + at : width + at + 128] = rotate(grad_k, own, -1).astype(jnp.bfloat16)
                out_ref[rows_k, 2 * width + at : 2 * width + at + 128] = grad_v.astype(jnp.bfloat16)
            return 0

        lax.fori_loop(0, blocks, outer, 0)
        for i in range(blocks):
            at = slice(i * BLK, (i + 1) * BLK)
            grad_q = dqt[:, at].T
            own = [t[at, :] for t in table_refs[:3]]
            for col in range(0, width, 128):
                out_ref[at, col : col + 128] = rotate(grad_q[:, col : col + 128], own, -1).astype(jnp.bfloat16)

    return launch(
        body,
        (1,),
        [fixed(a) for a in (q, k, v, g, lse, dot, lo, hi, *tables)],
        [((rows, 3 * width), jnp.bfloat16, pl.BlockSpec((rows, 3 * width), lambda *_: (0, 0), pipeline_mode=pl.Buffered(1)))],
        scratch=[
            pltpu.VMEM((width, rows), jnp.float32),
            pltpu.VMEM((width, rows), jnp.bfloat16),
            pltpu.VMEM((width, rows), jnp.bfloat16),
            pltpu.VMEM((2, heads, BLK, 128), jnp.float32),
        ],
        prefetch=(slots, first, last),
        after=after,
        name="attention_backward",
        flops=10 * rows * rows * width,
        moved=rows * width * 14,
    )[0]


def input_back(grad, weight, x, after=()):
    rows, cols = grad.shape
    wide = weight.shape[0]

    def body(g_ref, w_ref, x_ref, part_ref, bias_ref, sum_ref):
        @pl.when(pl.program_id(0) == 0)
        def _():
            sum_ref[...] = jnp.zeros_like(sum_ref)
            bias_ref[...] = jnp.zeros_like(bias_ref)

        part = nt(g_ref[...], w_ref[...])
        part_ref[...] = part.astype(jnp.bfloat16)
        bias_ref[0:1, :] += jnp.sum(g_ref[...].astype(jnp.float32), axis=0, keepdims=True)
        normed, _ = norm_parts(x_ref[...].astype(jnp.float32))
        sum_ref[0:1, :] += jnp.sum(part * normed, axis=0, keepdims=True)
        sum_ref[1:2, :] += jnp.sum(part, axis=0, keepdims=True)

    return launch(
        body,
        (rows // BLK,),
        [(grad, tile(BLK, cols)), fixed(weight), (x, tile(BLK, wide))],
        [
            ((rows, wide), jnp.bfloat16, tile(BLK, wide)),
            ((8, cols), jnp.float32, pl.BlockSpec((8, cols), lambda i, *_: (0, 0))),
            ((8, wide), jnp.float32, pl.BlockSpec((8, wide), lambda i, *_: (0, 0))),
        ],
        after=after,
        name="input_back",
        flops=2 * rows * cols * wide,
        moved=rows * (wide * 4 + cols * 2),
    )


def key_limits(bounds, spans, kind, total):
    places = jnp.arange(total, dtype=jnp.int32)
    below = bounds[:, None] <= places[None, :]
    doc_first = jnp.max(jnp.where(below, bounds[:, None], 0), axis=0)
    doc_last = jnp.min(jnp.where(below, total, bounds[:, None]), axis=0) - 1
    doc_last = jnp.minimum(doc_last, total - 1)
    inside = (spans[:, None] <= places[None, :]) & (places[None, :] < spans[:, None] + SPAN) & (kind > 0)
    span_last = jnp.max(jnp.where(inside, spans[:, None] + SPAN - 1, 0), axis=0)
    span_first = jnp.min(jnp.where(inside, spans[:, None], total), axis=0)
    hi = jnp.minimum(jnp.maximum(places, span_last), doc_last)
    q_first = jnp.maximum(jnp.minimum(places, span_first), doc_first)
    return doc_first, hi, q_first, doc_last


def block_limits(lo, hi, qf, ql):
    low = lo.reshape(-1, BLK)[:, 0] // BLK
    high = hi.reshape(-1, BLK)[:, -1] // BLK + 1
    qlow = qf.reshape(-1, BLK)[:, 0] // BLK
    qhigh = ql.reshape(-1, BLK)[:, -1] // BLK + 1
    return low, high, qlow, qhigh


class Exchange:
    def __init__(self, ranks, batches, rows, me):
        self.ranks, self.batches, self.rows, self.me = ranks, batches, rows, me
        self.square = ranks == 4 and rows == 2 * BLK
        self.half = rows // 2
        self.order = ((0, 1, 2, 3), (0, 2, 1, 3))
        total = ranks * rows
        block = jnp.arange(total // BLK, dtype=jnp.int32)
        if self.square:
            owner, part = block // 2, block % 2
            near = owner ^ me
            swapped = (near >> 1) | ((near & 1) << 1)
            self.slots = (part * 4 + jnp.where(part == 0, near, swapped)).astype(jnp.int32)
            owners = jnp.stack([me ^ r for half in self.order for r in half])
            firsts = owners * rows + jnp.repeat(jnp.arange(2), 4) * self.half
            self.places = (firsts[:, None] + jnp.arange(self.half)[None, :]).reshape(total).astype(jnp.int32)
        else:
            self.slots = block
            self.places = jnp.arange(total, dtype=jnp.int32)

    def swap(self, value, bit):
        return lax.ppermute(value, "seq", [(r, r ^ bit) for r in range(self.ranks)])

    def gather(self, upper, lower):
        if not self.square:
            return lax.all_gather(jnp.concatenate([upper, lower], axis=0), "seq", axis=0, tiled=True)
        upper = jnp.concatenate([upper, self.swap(upper, 1)], axis=0)
        lower = jnp.concatenate([lower, self.swap(lower, 2)], axis=0)
        return jnp.concatenate([upper, self.swap(upper, 2), lower, self.swap(lower, 1)], axis=0)

    def scatter(self, low):
        n = self.half
        if not self.square:
            own = lax.psum_scatter(low, "seq", scatter_dimension=0, tiled=True)
            return [[(own, 0)], [(own, n)]]
        out = []
        for at, bits in ((0, (2, 1)), (4 * n, (1, 2))):
            near = self.swap(low[at + 2 * n : at + 4 * n], bits[0])
            far = low[at + n : at + 2 * n].astype(jnp.float32) + near[n:].astype(jnp.float32)
            far = self.swap(far.astype(jnp.bfloat16), bits[1])
            out.append([(low, at), (near, 0), (far, 0)])
        return out

    def spread(self, value):
        lines = value.shape[0]
        if not self.square:
            every = lax.all_gather(value, "seq", axis=0)
            return [(every[r], pl.BlockSpec((lines, BLK), lambda i, *_: (0, i))) for r in range(self.ranks)]
        out = [(value, pl.BlockSpec((lines, BLK), lambda i, *_: (0, i)))]
        for bit, other in ((1, 2), (2, 1), (3, 3)):
            spec = pl.BlockSpec(
                (lines, BLK), lambda i, *_, a=bit, b=other: (0, (i // 4) * 4 + ((i % 4) ^ (a + (i // 4) * (b - a))))
            )
            out.append((self.swap(value, bit), spec))
        return out


def flipped(value, batch, me, bits):
    device = batch * 4 + me
    shape = value.shape
    for bit in range(bits):
        two = value.reshape((-1, 2, 1 << bit) + shape[1:])
        value = jnp.where((device >> bit) & 1, two[:, ::-1], two).reshape(shape)
    return value


def share_small(value, batches, ranks):
    if (batches, ranks) != (8, 4):
        return lax.all_gather(value, EVERY, axis=0)
    batch, me = lax.axis_index("batch"), lax.axis_index("seq")
    parts = value[None]
    for axis, count, steps in (("seq", ranks, (1, 2, 3)), ("batch", batches, (1,)), ("batch", batches, (2, 4, 6))):
        parts = jnp.concatenate(
            [parts] + [lax.ppermute(parts, axis, [(r, r ^ s) for r in range(count)]) for s in steps], axis=0
        )
    return flipped(parts, batch, me, 5)


def sum_small(value, batches, ranks):
    if (batches, ranks) != (8, 4):
        return lax.psum_scatter(value, EVERY, scatter_dimension=0, tiled=True)[0]
    batch, me = lax.axis_index("batch"), lax.axis_index("seq")
    value = flipped(value, batch, me, 5)
    for axis, count, steps, left in (("batch", batches, (2, 4, 6), 8), ("batch", batches, (1,), 4), ("seq", ranks, (1, 2, 3), 1)):
        total = value[:left]
        for i, s in enumerate(steps):
            at = (i + 1) * left
            total = total + lax.ppermute(value[at : at + left], axis, [(r, r ^ s) for r in range(count)])
        value = total
    return value[0]


def rot_tables(places):
    column = jnp.arange(128) % HEAD_DIM
    pair_idx = (column // 2).astype(jnp.float32)
    frequency = jnp.power(10000.0, -2.0 * pair_idx / HEAD_DIM)
    place_float = places.astype(jnp.float32)
    angles = place_float[:, None] * frequency[None, :]
    zeta_base = (2.0 * pair_idx + 0.4 * HEAD_DIM) / (1.4 * HEAD_DIM)
    exponent = (place_float - SEQ_LEN // 2) / 512.0
    scales = jnp.power(zeta_base[None, :], exponent[:, None])
    cosine, sine = jnp.cos(angles), jnp.sin(angles)
    even = (column % 2 == 0)[None, :]
    right, left = jnp.where(even, -sine, 0.0), jnp.where(even, 0.0, sine)
    return tuple(t * s for s in (scales, 1.0 / scales) for t in (cosine, right, left))


def local(
    layer_input,
    cotangent,
    w_qkv,
    bias_qkv,
    w_out,
    w_up,
    w_down,
    gains_d,
    biases_d,
    gain_ff,
    biases_ff,
    data_type,
    doc_bounds,
    span_starts,
    *,
    batches,
    ranks,
):
    me = lax.axis_index("seq")
    rows = layer_input.shape[1]
    half = rows // 2
    move = Exchange(ranks, batches, rows, me)
    tokens = rows * ranks
    cols = D // ranks
    strip, d_rows = w_down.shape[0], w_up.shape[0]
    units = strip * batches
    f32, bf16 = jnp.float32, jnp.bfloat16
    x_own, cot_own = layer_input.reshape(2, half, D), cotangent.reshape(2, half, D)

    part_qkv = lax.all_to_all(w_qkv.reshape(d_rows, 3, ranks, cols), "seq", 2, 0).reshape(d_rows * ranks, 3 * cols)
    full_qkv = lax.all_gather(part_qkv, "batch", axis=0, tiled=True)
    x_full = move.gather(x_own[0], x_own[1])
    small = jnp.concatenate(
        [bias_qkv.reshape(-1), gains_d.reshape(-1), biases_d.reshape(-1), gain_ff, biases_ff.reshape(-1)]
    )
    small = share_small(small, batches, ranks)
    cut = 11 * d_rows
    rows_d = small[:, :cut].reshape(-1, 11, d_rows).swapaxes(0, 1).reshape(11, D).astype(f32)
    rows_f = small[:, cut:].reshape(batches, ranks, 3, strip)
    rows_f = lax.dynamic_index_in_dim(rows_f, me, 1, False).swapaxes(0, 1).reshape(3, units).astype(f32)
    qkv_shift = lax.dynamic_slice_in_dim(rows_d[:3], me * cols, cols, 1).reshape(1, 3 * cols)
    branch = lax.dynamic_slice_in_dim(rows_d[3:], me * cols, cols, 1)
    gain_in, gain_mid = rows_d[3:4], rows_d[5:6]
    shift_in, shift_mid, shift_out, shift_down = rows_d[6:7], rows_d[8:9], rows_d[9:10], rows_d[10:11]
    gain_branch, shift_branch = branch[1:2], branch[4:5]
    gain_ffn, shift_ffn, shift_up = rows_f[0:1], rows_f[1:2], rows_f[2:3]

    order = [(i, (i % batches) * ranks + i // batches) for i in range(batches * ranks)]
    part_out = lax.ppermute(w_out, EVERY, order)
    full_out = lax.all_gather(part_out, "batch", axis=0, tiled=True)
    part_up = lax.all_to_all(w_up.reshape(d_rows, batches, ranks, strip), "seq", 2, 0).reshape(d_rows * ranks, units)
    full_down = lax.all_gather(w_down, "batch", axis=0, tiled=True)
    full_up = lax.all_gather(part_up, "batch", axis=0, tiled=True)
    cot_full = move.gather(cot_own[0], cot_own[1])

    normed_all, _ = norm_parts(x_full.astype(f32))
    input_low = (normed_all * gain_in + shift_in).astype(bf16)
    tables = rot_tables(move.places)
    query_rot, key_rot, value_low = qkv_project(input_low, full_qkv, qkv_shift, tables)
    lo, hi, q_lo, q_hi = key_limits(doc_bounds[0], span_starts[0], data_type[0], tokens)
    k_first, k_last, q_first, q_last = block_limits(lo, hi, q_lo, q_hi)
    lo, hi = lo[None], hi[None]
    attn, lse, stat = attention_fwd(query_rot, key_rot, value_low, lo, hi, move.slots, k_first, k_last)
    stats2 = move.spread(stat)
    branch_low, part = out_project(attn, stats2, gain_branch, shift_branch, full_out)

    def enter(vectors, values, arrived):
        resid = values[0].astype(f32) + (arrived + vectors[0])
        normed, _ = norm_parts(resid)
        return resid, normed * vectors[1] + vectors[2]

    resid, mid_own = own_rows(
        enter, [shift_out, gain_mid, shift_mid], [x_own], move.scatter(part), [f32, bf16], name="enter_ffn"
    )
    mid_low = move.gather(mid_own[0], mid_own[1])
    up_proj, grad_ffn, stat = ffn_up(mid_low, cot_full, full_up, full_down, shift_up, gain_ffn)
    stats4 = move.spread(stat)
    ffn_low, grad_up, part, sums_ff = ffn_mid(up_proj, grad_ffn, stats4, gain_ffn, shift_ffn, full_up)
    arriving = move.scatter(part)
    g_up = tn(mid_low, grad_up).astype(bf16)
    g_down = tn(ffn_low, cot_full).astype(bf16)
    sum_up = lax.psum_scatter(g_up, "batch", scatter_dimension=0, tiled=True)
    sum_down = lax.psum_scatter(g_down, "batch", scatter_dimension=0, tiled=True)

    def leave(vectors, values, arrived):
        normed, inverse = norm_parts(values[0])
        cot = values[1].astype(f32)
        grad = cot + norm_lower(normed, inverse, vectors[0], arrived)
        low = grad.astype(bf16)
        return grad, low, arrived * normed, arrived, low.astype(f32), cot

    grad_resid, resid_own, sums_mid = own_rows(
        leave, [gain_mid], [resid, cot_own], arriving, [f32, bf16], sums=4, after=(g_up, g_down), name="leave_ffn"
    )
    resid_low = move.gather(resid_own[0], resid_own[1])
    down = nn(ffn_low, full_down).astype(bf16)

    grad_branch, stat, sums_branch = branch_back(resid_low, full_out, attn, stats2, gain_branch, after=(down,))
    down, _ = lax.optimization_barrier((down, stat))
    arriving = move.scatter(down)
    stats3 = move.spread(stat)
    g_out = tn(branch_low, resid_low).astype(bf16)
    attn_low, dots = attn_grad(grad_branch, attn, stats2, stats3, gain_branch, after=(g_out,))
    sum_out = lax.psum_scatter(g_out, "batch", scatter_dimension=0, tiled=True)
    grad_qkv = attention_bwd(
        query_rot, key_rot, value_low, attn_low, lse, dots, lo, hi, tables, move.slots, q_first, q_last
    )

    def finish(vectors, values, arrived):
        return (values[0] + (arrived + vectors[0]),)

    result = own_rows(finish, [shift_down], [resid], arriving, [bf16], after=(grad_qkv,), name="finish")[0]
    g_qkv = tn(input_low, grad_qkv).astype(bf16)
    sum_qkv = lax.psum_scatter(g_qkv, "batch", scatter_dimension=0, tiled=True)
    part, sums_qkv, sums_in = input_back(grad_qkv, full_qkv, x_full, after=(g_qkv,))
    arriving = move.scatter(part)

    def end(vectors, values, arrived):
        normed, inverse = norm_parts(values[0].astype(f32))
        return (values[1] + norm_lower(normed, inverse, vectors[0], arrived),)

    def placed(value):
        return lax.dynamic_update_slice(jnp.zeros((value.shape[0], D), f32), value, (0, me * cols))

    branch_rows = placed(sums_branch[:2])
    vector_d = jnp.concatenate(
        [
            placed(sums_qkv[0].reshape(3, cols)),
            sums_in[:1],
            branch_rows[:1],
            sums_mid[:1],
            sums_in[1:2],
            branch_rows[1:],
            sums_mid[1:4],
        ]
    )
    vector_f = sums_ff[:3].reshape(3, batches, 1, strip)
    vector_f = lax.dynamic_update_slice(jnp.zeros((3, batches, ranks, strip), f32), vector_f, (0, 0, me, 0))
    vector = jnp.concatenate(
        [
            vector_d.reshape(11, batches * ranks, d_rows).swapaxes(0, 1).reshape(batches * ranks, -1),
            vector_f.reshape(3, batches * ranks, strip).swapaxes(0, 1).reshape(batches * ranks, -1),
        ],
        axis=1,
    )
    vector = sum_small(vector, batches, ranks)
    grad_total = own_rows(end, [gain_in], [x_own, grad_resid], arriving, [f32], name="end")[0]

    def to_rows(value, groups, wide):
        value = lax.all_to_all(value.reshape(ranks, d_rows, groups, wide), "seq", 0, 2)
        return value.reshape(d_rows, groups * ranks * wide).astype(f32)

    out_qkv = to_rows(sum_qkv, 3, cols)
    out_up = to_rows(sum_up, batches, strip)
    out_out = lax.ppermute(sum_out, EVERY, [(b, a) for a, b in order]).astype(f32)
    out_down = sum_down.astype(f32)
    own_d = vector[:cut].reshape(11, d_rows)
    own_f = vector[cut:].reshape(3, strip)
    return (
        result.reshape(1, rows, D),
        grad_total.reshape(1, rows, D),
        out_qkv,
        own_d[:3],
        out_out,
        out_up,
        out_down,
        own_d[3:6],
        own_d[6:],
        own_f[0],
        own_f[1:],
    )


def solution(mesh):
    sizes = dict(mesh.shape)

    def run(*args):
        return local(*args, batches=sizes["batch"], ranks=sizes["seq"])

    return jax.shard_map(
        run,
        mesh=mesh,
        in_specs=(
            P("batch", "seq", None),
            P("batch", "seq", None),
            P(("batch", "seq"), None),
            P(None, ("batch", "seq")),
            P(("batch", "seq"), None),
            P(("batch", "seq"), None),
            P(("batch", "seq"), None),
            P(None, ("batch", "seq")),
            P(None, ("batch", "seq")),
            P(("batch", "seq")),
            P(None, ("batch", "seq")),
            P("batch"),
            P("batch", None),
            P("batch", None),
        ),
        out_specs=(
            P("batch", "seq", None),
            P("batch", "seq", None),
            P(("batch", "seq"), None),
            P(None, ("batch", "seq")),
            P(("batch", "seq"), None),
            P(("batch", "seq"), None),
            P(("batch", "seq"), None),
            P(None, ("batch", "seq")),
            P(None, ("batch", "seq")),
            P(("batch", "seq")),
            P(None, ("batch", "seq")),
        ),
        check_vma=False,
    )
```

time: 5500 us -> 1090 us (0.20)
  waiting for transfers between devices: 4180 us -> 295 us
  matrix products: 587 us -> 100 us
  blocking collectives: 366 us -> 14.3 us
  Pallas kernels: 0 us -> 300 us
  starting transfers between devices: 1.96 us -> 194 us
  other arithmetic: 206 us -> 59.6 us
    reduce_scatter x6 -> x4, waiting for transfers between devices: 3620 us -> 18.6 us  [the longest x1 18.6 us: local(): lax.psum_scatter(g_down, 'batch', scatter_dimension=0, tiled=True)]
    dot_general x19 -> x5, matrix products: 587 us -> 100 us  [the longest x4 76.1 us: tn(): lax.dot_general(a, b, (((0,), (0,)), ((), ())), preferred_element_type=jn...]
    all_gather x5 -> x0, blocking collectives: 327 us -> none  [the longest x1 66.2 us: local(): lax.all_gather(gains_d, ('batch', 'seq'), axis=1, tiled=True)]
    pallas_call x0 -> x13, Pallas kernels: none -> 300 us  [launch(): pl.pallas_call(kernel, out_shape=tuple((jax.ShapeDtypeStruct(s, d) for s,...]
    unnamed x20 -> x8, waiting for transfers between devices: 287 us -> 1.26 us
    all_gather x6 -> x4, waiting for transfers between devices: 278 us -> 0.01 us  [the longest x1 0.01 us: local(): full_qkv = lax.all_gather(part_qkv, 'batch', axis=0, tiled=True)]
    ppermute x0 -> x57, waiting for transfers between devices: none -> 275 us  [the longest x41 214 us: swap(): return lax.ppermute(value, 'seq', [(r, r ^ bit) for r in range(self.ranks)])]
    ppermute x0 -> x57, starting transfers between devices: none -> 181 us  [the longest x7 112 us: sum_small(): lax.ppermute(value[at:at + left], axis, [(r, r ^ s) for r in range(count)])]
  transfers between devices with their start and end apart: 16 -> 68, of which waited for: 11 -> 31; matrix products, arithmetic and copies ran while one was open for 11% -> 21% of each run, Pallas kernels for 0% -> 18%
where the time goes in v1:
time: 1090 us
  Pallas kernels  300 us (28%)
  waiting for transfers between devices  295 us (27%)
  starting transfers between devices  194 us (18%)
  local copies, waits for them, and re-layouts  112 us (10%)
  matrix products  100 us (9%)
  other arithmetic  59.6 us (5%)
  between operations  16.3 us (1%)
  blocking collectives  14.3 us (1%)
    pallas_call x13, Pallas kernels, launch(): pl.pallas_call(kernel, out_shape=tuple((jax.ShapeDtypeStruct(s, d) for s,...  300 us
    ppermute x41, waiting for transfers between devices, swap(): return lax.ppermute(value, 'seq', [(r, r ^ bit) for r in range(self.ranks)])  214 us
    ppermute x7, starting transfers between devices, sum_small(): lax.ppermute(value[at:at + left], axis, [(r, r ^ s) for r in range(count)])  112 us
    dot_general x4, matrix products, tn(): lax.dot_general(a, b, (((0,), (0,)), ((), ())), preferred_element_type=jn...  76.1 us
    ppermute x7, waiting for transfers between devices, sum_small(): lax.ppermute(value[at:at + left], axis, [(r, r ^ s) for r in range(count)])  54.1 us
    unnamed x111, local copies, waits for them, and re-layouts  45.6 us
    ppermute x41, starting transfers between devices, swap(): return lax.ppermute(value, 'seq', [(r, r ^ bit) for r in range(self.ranks)])  35.8 us
    dot_general x1, matrix products, nn(): return jnp.dot(a, b, preferred_element_type=jnp.float32)  23.9 us
  transfers between devices with their start and end apart: 68, of which 31 were waited for; matrix products, arithmetic and copies ran while one was open for 21% of the time, Pallas kernels for 18%

profile of v1, /device:TPU:1, one launch (start us, length us, event | category | flops | bytes accessed | tf_op | source)
XLA Modules:
  0.0 1091.0 jit_solution(137867324622142030)
XLA Ops:
  9.8 14.3 %all_to_all.48 = bf16[1,64,3,4,512]{4,1,2,0,3:T(8,128)(2,1)S(1)} all-to-all(bf16[1,64,3,4,512]{4,1,2,0,3:T(8,128)(2,1)S(1)} %copy.66), channel_id=1, replica_groups=mesh['batch'=8,'seq'=4] {'seq'}, dimensions={3} | all-to-all | bytes 1572864 | tf_op jit(solution)/shard_map/all_to_all | solution.py:735
  106.9 30.4 %collective-permute-done.8 = bf16[512,2048]{1,0:T(8,128)(2,1)} collective-permute-done((bf16[512,2048]{1,0:T(8,128)(2,1)}, bf16[512,2048]{1,0:T(8,128)(2,1)}, u32[]{:S(2)}, u32[]{:S(2)}) %collective-permute-start.8) | collective-permute-done | bytes 2097184 | tf_op jit(solution)/shard_map/ppermute | solution.py:619
  160.8 19.0 %qkv_project.1 = (bf16[2048,512]{1,0:T(8,128)(2,1)}, bf16[2048,512]{1,0:T(8,128)(2,1)}, bf16[2048,512]{1,0:T(8,128)(2,1)}) custom-call(bf16[2048,2048]{1,0:T(8,128)(2,1)} %fusion.5.refs_0_, bf16[2048,1536]{1,0:T(8,128)(2,1)} %all-gather.5.cloned.1.call-done.refs_1_, f32[1,1536]{1,0:T(1,128)} %bitcast.162, f32[2048,128]{1,0:T(8,128)} %get-tuple-element.131.refs_3_.refs_11_, ...), custom_call_target="tpu_custom_call" | custom-call | flops 12884901888 | bytes 16777216 | tf_op jit(solution)/shard_map/qkv_project/pallas_call | solution.py:37
  179.8 27.3 %attention_forward.1 = (f32[2048,512]{1,0:T(8,128)}, f32[8,2048]{1,0:T(8,128)}, f32[8,2048]{1,0:T(8,128)}) custom-call(s32[8]{0:T(128)} %fusion.21.refs_0_, s32[8]{0:T(128)} %get-tuple-element.140.refs_1_, s32[8]{0:T(128)} %get-tuple-element.141.refs_2_, bf16[2048,512]{1,0:T(8,128)(2,1)} %get-tuple-element.40.refs_3_, ...), custom_call_target="tpu_custom_call" | custom-call | flops 8589934592 | bytes 12582912 | tf_op jit(solution)/shard_map/attention_forward/pallas_call | solution.py:37
  214.5 12.9 %out_project.1 = (bf16[2048,512]{1,0:T(8,128)(2,1)}, bf16[2048,2048]{1,0:T(8,128)(2,1)}) custom-call(f32[2048,512]{1,0:T(8,128)} %get-tuple-element.43.refs_0_.refs_2_.refs_1_, f32[1,512]{1,0:T(1,128)} %get-tuple-element.116.refs_1_.refs_3_.refs_2_, f32[1,512]{1,0:T(1,128)} %get-tuple-element.115.refs_2_, ...), custom_call_target="tpu_custom_call" | custom-call | flops 4294967296 | bytes 14680064 | tf_op jit(solution)/shard_map/out_project/pallas_call | solution.py:37
  233.4 27.1 %collective-permute-done.15.refs_5_ = bf16[512,2048]{1,0:T(8,128)(2,1)S(1)} collective-permute-done((bf16[512,2048]{1,0:T(8,128)(2,1)S(1)}, bf16[512,2048]{1,0:T(8,128)(2,1)S(1)}, u32[]{:S(2)}, u32[]{:S(2)}) %collective-permute-start.15) | collective-permute-done | bytes 2097184 | tf_op jit(solution)/shard_map/ppermute | solution.py:619
  287.3 17.8 %collective-permute-done.16.refs_6_ = bf16[256,2048]{1,0:T(8,128)(2,1)} collective-permute-done((bf16[256,2048]{1,0:T(8,128)(2,1)}, bf16[256,2048]{1,0:T(8,128)(2,1)}, u32[]{:S(2)}, u32[]{:S(2)}) %collective-permute-start.16) | collective-permute-done | bytes 1048608 | tf_op jit(solution)/shard_map/ppermute | solution.py:619
  345.6 18.2 %collective-permute-done.21 = bf16[256,2048]{1,0:T(8,128)(2,1)S(1)} collective-permute-done((bf16[256,2048]{1,0:T(8,128)(2,1)S(1)}, bf16[256,2048]{1,0:T(8,128)(2,1)S(1)}, u32[]{:S(2)}, u32[]{:S(2)}) %collective-permute-start.21) | collective-permute-done | bytes 1048608 | tf_op jit(solution)/shard_map/ppermute | solution.py:619
  376.6 32.0 %collective-permute-done.20 = bf16[512,2048]{1,0:T(8,128)(2,1)S(1)} collective-permute-done((bf16[512,2048]{1,0:T(8,128)(2,1)S(1)}, bf16[512,2048]{1,0:T(8,128)(2,1)S(1)}, u32[]{:S(2)}, u32[]{:S(2)}) %collective-permute-start.20) | collective-permute-done | bytes 2097184 | tf_op jit(solution)/shard_map/ppermute | solution.py:619
  414.6 61.0 %ffn_up.1 = (f32[2048,2048]{1,0:T(8,128)}, f32[2048,2048]{1,0:T(8,128)}, f32[8,2048]{1,0:T(8,128)}) custom-call(bf16[2048,2048]{1,0:T(8,128)(2,1)} %constant_dynamic-update-slice_fusion.6.refs_0_, bf16[2048,2048]{1,0:T(8,128)(2,1)} %constant_dynamic-update-slice_fusion.12.refs_1_, bf16[2048,2048]{1,0:T(8,128)(2,1)} %all-gather.9.cloned.1.call-done.refs_2_.refs_4_, ...), custom_call_target="tpu_custom_call" | custom-call | flops 34359738368 | bytes 50331648 | tf_op jit(solution)/shard_map/ffn_up/pallas_call | solution.py:37
  482.0 43.1 %ffn_mid.1 = (bf16[2048,2048]{1,0:T(8,128)(2,1)}, bf16[2048,2048]{1,0:T(8,128)(2,1)}, bf16[2048,2048]{1,0:T(8,128)(2,1)}, f32[8,2048]{1,0:T(8,128)}) custom-call(f32[2048,2048]{1,0:T(8,128)} %get-tuple-element.48.refs_0_, f32[2048,2048]{1,0:T(8,128)} %get-tuple-element.49.refs_1_, f32[1,2048]{1,0:T(1,128)} %bitcast.160, f32[1,2048]{1,0:T(1,128)} %bitcast.158, ...), custom_call_target="tpu_custom_call" | custom-call | flops 17179869184 | bytes 58720256 | tf_op jit(solution)/shard_map/ffn_mid/pallas_call | solution.py:37
  525.1 23.8 %convolution_convert_fusion.1.refs_9_ = bf16[2048,2048]{1,0:T(8,128)(2,1)} fusion(bf16[2048,2048]{1,0:T(8,128)(2,1)} %constant_dynamic-update-slice_fusion.6.refs_0_, bf16[2048,2048]{1,0:T(8,128)(2,1)} %get-tuple-element.53), kind=kOutput, calls=%fused_computation.9 | convolution fusion | flops 17184063488 | bytes 25165824 | tf_op jit(solution)/shard_map/dot_general | solution.py:24
  553.1 23.6 %collective-permute-done.30.refs_4_ = bf16[512,2048]{1,0:T(8,128)(2,1)S(1)} collective-permute-done((bf16[512,2048]{1,0:T(8,128)(2,1)S(1)}, bf16[512,2048]{1,0:T(8,128)(2,1)S(1)}, u32[]{:S(2)}, u32[]{:S(2)}) %collective-permute-start.30) | collective-permute-done | bytes 2097184 | tf_op jit(solution)/shard_map/ppermute | solution.py:619
  584.3 24.1 %convolution_convert_fusion.refs_10_ = bf16[2048,2048]{1,0:T(8,128)(2,1)} fusion(bf16[2048,2048]{1,0:T(8,128)(2,1)} %get-tuple-element.51, bf16[2048,2048]{1,0:T(8,128)(2,1)} %constant_dynamic-update-slice_fusion.12.refs_1_), kind=kOutput, calls=%fused_computation.8 | convolution fusion | flops 17184063488 | bytes 25165824 | tf_op jit(solution)/shard_map/dot_general | solution.py:24
  623.8 21.7 %collective-permute-done.34 = bf16[256,2048]{1,0:T(8,128)(2,1)S(1)} collective-permute-done((bf16[256,2048]{1,0:T(8,128)(2,1)S(1)}, bf16[256,2048]{1,0:T(8,128)(2,1)S(1)}, u32[]{:S(2)}, u32[]{:S(2)}) %collective-permute-start.34) | collective-permute-done | bytes 1048608 | tf_op jit(solution)/shard_map/ppermute | solution.py:619
  647.6 23.9 %convolution_convert_fusion.2.refs_8_.refs_2_.refs_5_ = bf16[2048,2048]{1,0:T(8,128)(2,1)} fusion(bf16[2048,2048]{1,0:T(8,128)(2,1)} %get-tuple-element.51, bf16[2048,2048]{1,0:T(8,128)(2,1)} %all-gather.11.cloned.1.call-done.refs_3_), kind=kOutput, calls=%fused_computation.10 | convolution fusion | flops 17184063488 | bytes 25165824 | tf_op jit(solution)/shard_map/dot_general | solution.py:28
  681.1 13.4 %branch_back.1 = (f32[2048,512]{1,0:T(8,128)}, f32[8,2048]{1,0:T(8,128)}, f32[8,512]{1,0:T(8,128)}) custom-call(bf16[2048,2048]{1,0:T(8,128)(2,1)} %constant_dynamic-update-slice_fusion.18.refs_0_, bf16[512,2048]{1,0:T(8,128)(2,1)} %all-gather.7.cloned.1.call-done.refs_3_.refs_1_, f32[2048,512]{1,0:T(8,128)} %get-tuple-element.43.refs_0_.refs_2_.refs_1_, ...), custom_call_target="tpu_custom_call" | custom-call | flops 4294967296 | bytes 16777216 | tf_op jit(solution)/shard_map/branch_back/pallas_call | solution.py:37
  716.3 61.0 %attention_backward.1.refs_8_.refs_0_ = bf16[2048,1536]{1,0:T(8,128)(2,1)} custom-call(s32[8]{0:T(128)} %fusion.21.refs_0_, s32[8]{0:T(128)} %get-tuple-element.138.refs_1_, s32[8]{0:T(128)} %get-tuple-element.139.refs_2_, bf16[2048,512]{1,0:T(8,128)(2,1)} %get-tuple-element.40.refs_3_, bf16[2048,512]{1,0:T(8,128)(2,1)} %get-tuple-element.41.refs_4_, ...), custom_call_target="tpu_custom_call" | custom-call | flops 21474836480 | bytes 14680064 | tf_op jit(solution)/shard_map/attention_backward/pallas_call | solution.py:37
  777.3 19.1 %convolution_convert_fusion.3.refs_3_ = bf16[2048,1536]{1,0:T(8,128)(2,1)} fusion(bf16[2048,2048]{1,0:T(8,128)(2,1)} %fusion.5.refs_0_, bf16[2048,1536]{1,0:T(8,128)(2,1)} %attention_backward.1.refs_8_.refs_0_), kind=kOutput, calls=%fused_computation.11 | convolution fusion | flops 12888047616 | bytes 20971520 | tf_op jit(solution)/shard_map/dot_general | solution.py:24
  803.6 22.6 %input_back.1 = (bf16[2048,2048]{1,0:T(8,128)(2,1)}, f32[8,1536]{1,0:T(8,128)}, f32[8,2048]{1,0:T(8,128)}) custom-call(bf16[2048,1536]{1,0:T(8,128)(2,1)} %attention_backward.1.refs_8_.refs_0_, bf16[2048,1536]{1,0:T(8,128)(2,1)} %all-gather.5.cloned.1.call-done.refs_1_, bf16[2048,2048]{1,0:T(8,128)(2,1)} %constant_dynamic-update-slice_fusion.refs_2_, ...), custom_call_target="tpu_custom_call" | custom-call | flops 12884901888 | bytes 23068672 | tf_op jit(solution)/shard_map/input_back/pallas_call | solution.py:37
  837.6 35.5 %collective-permute-start.51 = (f32[8,1472]{1,0:T(8,128)S(1)}, f32[8,1472]{1,0:T(8,128)S(1)}, u32[]{:S(2)}, u32[]{:S(2)}) collective-permute-start(f32[8,1472]{1,0:T(8,128)S(1)} %get-tuple-element.111), channel_id=1, source_target_pairs={{0,24},{4,28},{8,16},{12,20},{16,8},{20,12},{24,0},{28,4},{1,25},{... | collective-permute-start | bytes 141320 | tf_op jit(solution)/shard_map/ppermute | solution.py:685
  874.6 70.0 %collective-permute-start.50 = (f32[8,1472]{1,0:T(8,128)S(1)}, f32[8,1472]{1,0:T(8,128)S(1)}, u32[]{:S(2)}, u32[]{:S(2)}) collective-permute-start(f32[8,1472]{1,0:T(8,128)S(1)} %get-tuple-element.112), channel_id=1, source_target_pairs={{0,16},{4,20},{8,24},{12,28},{16,0},{20,4},{24,8},{28,12},{1,17},{... | collective-permute-start | bytes 141320 | tf_op jit(solution)/shard_map/ppermute | solution.py:685
  975.2 42.7 %collective-permute-done.55 = f32[1,1472]{1,0:T(1,128)S(1)} collective-permute-done((f32[1,1472]{1,0:T(1,128)S(1)}, f32[1,1472]{1,0:T(1,128)S(1)}, u32[]{:S(2)}, u32[]{:S(2)}) %collective-permute-start.55) | collective-permute-done | bytes 5920 | tf_op jit(solution)/shard_map/ppermute | solution.py:685
  1055.3 18.6 %reduce-scatter.11.cloned.1.call-done = bf16[256,2048]{1,0:T(8,128)(2,1)} async-done(((bf16[2048,2048]{1,0:T(8,128)(2,1)}), bf16[256,2048]{1,0:T(8,128)(2,1)}) %reduce-scatter.11.cloned.1.call-update) | async-done | bytes 1048592 | tf_op jit(solution)/shard_map/reduce_scatter | solution.py:788
  (399 shorter events, 371.8 us)
Async XLA Ops:
  7.2 153.6 %all-gather.5.cloned.1.call-start = ((), (), s32[]{:S(2)}) async-start(), calls=%async_computation.8 | async-start | bytes 7077888 | tf_op jit(solution)/shard_map/all_gather | solution.py:736
  25.9 184.6 %all-gather.7.cloned.1.call-start = ((), (), s32[]{:S(2)}) async-start(), calls=%async_computation.9 | async-start | bytes 2359296 | tf_op jit(solution)/shard_map/all_gather | solution.py:755
  37.0 377.5 %all-gather.11.cloned.1.call-start = ((), (), s32[]{:S(2)}) async-start(), calls=%async_computation.11 | async-start | bytes 9437184 | tf_op jit(solution)/shard_map/all_gather | solution.py:757
  59.5 355.0 %all-gather.9.cloned.1.call-start = ((), (), s32[]{:S(2)}) async-start(), calls=%async_computation.10 | async-start | bytes 9437184 | tf_op jit(solution)/shard_map/all_gather | solution.py:758
  104.0 862.7 %reduce-scatter.9.cloned.1.call-start = ((), (), s32[]{:S(2)}) async-start(), calls=%async_computation.14 | async-start | bytes 9437184 | tf_op jit(solution)/shard_map/reduce_scatter | solution.py:787
  232.2 50.5 %collective-permute-start.23 = (bf16[256,2048]{1,0:T(8,128)(2,1)}, bf16[256,2048]{1,0:T(8,128)(2,1)}, u32[]{:S(2)}, u32[]{:S(2)}) collective-permute-start(bf16[256,2048]{1,0:T(8,128)(2,1)} %get-tuple-element.104), channel_id=1, source_target_pairs={{0,1},{1,0},{2,3},{3,2},{4,5},{5,4},{6,7},{7,6},{8,9},{9,8},{10,11... | collective-permute-start | bytes 3145736 | tf_op jit(solution)/shard_map/ppermute | solution.py:619
  266.4 50.2 %collective-permute-start.25 = (bf16[256,2048]{1,0:T(8,128)(2,1)}, bf16[256,2048]{1,0:T(8,128)(2,1)S(1)}, u32[]{:S(2)}, u32[]{:S(2)}) collective-permute-start(bf16[256,2048]{1,0:T(8,128)(2,1)} %get-tuple-element.103), channel_id=1, source_target_pairs={{0,2},{1,3},{2,0},{3,1},{4,6},{5,7},{6,4},{7,5},{8,10},{9,11},{10,... | collective-permute-start | bytes 3145736 | tf_op jit(solution)/shard_map/ppermute | solution.py:619
  285.8 55.3 %collective-permute-start.24 = (bf16[512,2048]{1,0:T(8,128)(2,1)}, bf16[512,2048]{1,0:T(8,128)(2,1)}, u32[]{:S(2)}, u32[]{:S(2)}) collective-permute-start(bf16[512,2048]{1,0:T(8,128)(2,1)} %pad_maximum_fusion.4), channel_id=1, source_target_pairs={{0,2},{1,3},{2,0},{3,1},{4,6},{5,7},{6,4},{7,5},{8,10},{9,11},{10,... | collective-permute-start | bytes 6291464 | tf_op jit(solution)/shard_map/ppermute | solution.py:619
  318.1 53.6 %collective-permute-start.26 = (bf16[512,2048]{1,0:T(8,128)(2,1)S(1)}, bf16[512,2048]{1,0:T(8,128)(2,1)S(1)}, u32[]{:S(2)}, u32[]{:S(2)}) collective-permute-start(bf16[512,2048]{1,0:T(8,128)(2,1)S(1)} %pad_maximum_fusion.5), channel_id=1, source_target_pairs={{0,1},{1,0},{2,3},{3,2},{4,5},{5,4},{6,7},{7,6},{8,9},{9,8},{10,11... | collective-permute-start | bytes 6291464 | tf_op jit(solution)/shard_map/ppermute | solution.py:619
  336.1 72.5 %collective-permute-start.20 = (bf16[512,2048]{1,0:T(8,128)(2,1)S(1)}, bf16[512,2048]{1,0:T(8,128)(2,1)S(1)}, u32[]{:S(2)}, u32[]{:S(2)}) collective-permute-start(bf16[512,2048]{1,0:T(8,128)(2,1)S(1)} %pad_maximum_fusion.2), channel_id=1, source_target_pairs={{0,2},{1,3},{2,0},{3,1},{4,6},{5,7},{6,4},{7,5},{8,10},{9,11},{10,... | collective-permute-start | bytes 6291464 | tf_op jit(solution)/shard_map/ppermute | solution.py:619
  364.0 49.0 %collective-permute-start.22 = (bf16[512,2048]{1,0:T(8,128)(2,1)S(1)}, bf16[512,2048]{1,0:T(8,128)(2,1)S(1)}, u32[]{:S(2)}, u32[]{:S(2)}) collective-permute-start(bf16[512,2048]{1,0:T(8,128)(2,1)S(1)} %pad_maximum_fusion.3), channel_id=1, source_target_pairs={{0,1},{1,0},{2,3},{3,2},{4,5},{5,4},{6,7},{7,6},{8,9},{9,8},{10,11... | collective-permute-start | bytes 6291464 | tf_op jit(solution)/shard_map/ppermute | solution.py:619
  548.9 474.9 %reduce-scatter.7.cloned.1.call-start = ((), (), s32[]{:S(2)}) async-start(), calls=%async_computation.13 | async-start | bytes 2359296 | tf_op jit(solution)/shard_map/reduce_scatter | solution.py:809
  706.3 322.9 %reduce-scatter.5.cloned.1.call-start = ((), (), s32[]{:S(2)}) async-start(), calls=%async_computation.12 | async-start | bytes 7077888 | tf_op jit(solution)/shard_map/reduce_scatter | solution.py:819
  796.5 277.4 %reduce-scatter.11.cloned.1.call-start = ((), (), s32[]{:S(2)}) async-start(), calls=%async_computation.15 | async-start | bytes 9437184 | tf_op jit(solution)/shard_map/reduce_scatter | solution.py:788
  802.7 151.9 %collective-permute-start.38 = (bf16[512,2048]{1,0:T(8,128)(2,1)}, bf16[512,2048]{1,0:T(8,128)(2,1)S(1)}, u32[]{:S(2)}, u32[]{:S(2)}) collective-permute-start(bf16[512,2048]{1,0:T(8,128)(2,1)} %get-tuple-element.92), channel_id=1, source_target_pairs={{0,2},{1,3},{2,0},{3,1},{4,6},{5,7},{6,4},{7,5},{8,10},{9,11},{10,... | collective-permute-start | bytes 6291464 | tf_op jit(solution)/shard_map/ppermute | solution.py:619
  802.8 151.8 %collective-permute-start.40 = (bf16[512,2048]{1,0:T(8,128)(2,1)}, bf16[512,2048]{1,0:T(8,128)(2,1)}, u32[]{:S(2)}, u32[]{:S(2)}) collective-permute-start(bf16[512,2048]{1,0:T(8,128)(2,1)} %get-tuple-element.91), channel_id=1, source_target_pairs={{0,1},{1,0},{2,3},{3,2},{4,5},{5,4},{6,7},{7,6},{8,9},{9,8},{10,11... | collective-permute-start | bytes 6291464 | tf_op jit(solution)/shard_map/ppermute | solution.py:619
  831.0 129.5 %collective-permute-start.45 = (bf16[512,2048]{1,0:T(8,128)(2,1)}, bf16[512,2048]{1,0:T(8,128)(2,1)}, u32[]{:S(2)}, u32[]{:S(2)}) collective-permute-start(bf16[512,2048]{1,0:T(8,128)(2,1)} %get-tuple-element.88), channel_id=1, source_target_pairs={{0,2},{1,3},{2,0},{3,1},{4,6},{5,7},{6,4},{7,5},{8,10},{9,11},{10,... | collective-permute-start | bytes 6291464 | tf_op jit(solution)/shard_map/ppermute | solution.py:619
  832.3 128.3 %collective-permute-start.47 = (bf16[512,2048]{1,0:T(8,128)(2,1)}, bf16[512,2048]{1,0:T(8,128)(2,1)}, u32[]{:S(2)}, u32[]{:S(2)}) collective-permute-start(bf16[512,2048]{1,0:T(8,128)(2,1)} %get-tuple-element.87), channel_id=1, source_target_pairs={{0,1},{1,0},{2,3},{3,2},{4,5},{5,4},{6,7},{7,6},{8,9},{9,8},{10,11... | collective-permute-start | bytes 6291464 | tf_op jit(solution)/shard_map/ppermute | solution.py:619
  874.6 73.7 %collective-permute-start.50 = (f32[8,1472]{1,0:T(8,128)S(1)}, f32[8,1472]{1,0:T(8,128)S(1)}, u32[]{:S(2)}, u32[]{:S(2)}) collective-permute-start(f32[8,1472]{1,0:T(8,128)S(1)} %get-tuple-element.112), channel_id=1, source_target_pairs={{0,16},{4,20},{8,24},{12,28},{16,0},{20,4},{24,8},{28,12},{1,17},{... | collective-permute-start | bytes 141320 | tf_op jit(solution)/shard_map/ppermute | solution.py:685
  959.4 81.7 %collective-permute-start.39 = (bf16[256,2048]{1,0:T(8,128)(2,1)}, bf16[256,2048]{1,0:T(8,128)(2,1)}, u32[]{:S(2)}, u32[]{:S(2)}) collective-permute-start(bf16[256,2048]{1,0:T(8,128)(2,1)} %get-tuple-element.90), channel_id=1, source_target_pairs={{0,1},{1,0},{2,3},{3,2},{4,5},{5,4},{6,7},{7,6},{8,9},{9,8},{10,11... | collective-permute-start | bytes 3145736 | tf_op jit(solution)/shard_map/ppermute | solution.py:619
  960.5 80.6 %collective-permute-start.41 = (bf16[256,2048]{1,0:T(8,128)(2,1)}, bf16[256,2048]{1,0:T(8,128)(2,1)}, u32[]{:S(2)}, u32[]{:S(2)}) collective-permute-start(bf16[256,2048]{1,0:T(8,128)(2,1)} %get-tuple-element.89), channel_id=1, source_target_pairs={{0,2},{1,3},{2,0},{3,1},{4,6},{5,7},{6,4},{7,5},{8,10},{9,11},{10,... | collective-permute-start | bytes 3145736 | tf_op jit(solution)/shard_map/ppermute | solution.py:619
  965.0 81.8 %collective-permute-start.46 = (bf16[256,2048]{1,0:T(8,128)(2,1)}, bf16[256,2048]{1,0:T(8,128)(2,1)}, u32[]{:S(2)}, u32[]{:S(2)}) collective-permute-start(bf16[256,2048]{1,0:T(8,128)(2,1)} %get-tuple-element.86), channel_id=1, source_target_pairs={{0,1},{1,0},{2,3},{3,2},{4,5},{5,4},{6,7},{7,6},{8,9},{9,8},{10,11... | collective-permute-start | bytes 3145736 | tf_op jit(solution)/shard_map/ppermute | solution.py:619
  965.4 81.5 %collective-permute-start.48 = (bf16[256,2048]{1,0:T(8,128)(2,1)}, bf16[256,2048]{1,0:T(8,128)(2,1)}, u32[]{:S(2)}, u32[]{:S(2)}) collective-permute-start(bf16[256,2048]{1,0:T(8,128)(2,1)} %get-tuple-element.85), channel_id=1, source_target_pairs={{0,2},{1,3},{2,0},{3,1},{4,6},{5,7},{6,4},{7,5},{8,10},{9,11},{10,... | collective-permute-start | bytes 3145736 | tf_op jit(solution)/shard_map/ppermute | solution.py:619
  969.3 63.7 %all-to-all-start.3 = ((bf16[4,64,8,1,256]{4,2,1,3,0:T(8,128)(2,1)}), bf16[4,64,8,1,256]{4,2,1,3,0:T(8,128)(2,1)S(1)}, u32[]{:S(2)}, u32[]{:S(2)}) async-start(bf16[4,64,8,1,256]{4,2,1,3,0:T(8,128)(2,1)} %bitcast.43), calls=%async_computation.6 | async-start | bytes 2097152 | tf_op jit(solution)/shard_map/all_to_all | solution.py:855
  (86 other events, 1538.5 us)
Sparse Core Ops, SparseCore 0:
  26.0 69.9 all-gather.4
  98.1 27.7 all-gather.6
  127.5 81.6 all-gather.10
  210.7 80.5 all-gather.8
  549.0 124.7 reduce-scatter.8
  706.4 101.6 reduce-scatter.6
  810.4 155.0 reduce-scatter.4
  967.8 106.0 reduce-scatter.10

commit v2 on v1

--- a/solution.py
+++ b/solution.py
@@ -28,7 +28,27 @@
     return jnp.dot(a, b, preferred_element_type=jnp.float32)
 
 
-def launch(body, grid, ins, outs, scratch=(), prefetch=(), after=(), name=None, flops=0, moved=0):
+TAKES = {
+    "enter_attention": 12,
+    "qkv_project": 19,
+    "attention_forward": 41,
+    "out_project": 14,
+    "down_project": 200,
+    "add_rows": 30,
+    "ffn_up": 54,
+    "ffn_mid": 47,
+    "branch_back": 150,
+    "attn_grad": 38.0,
+    "attention_backward": 200.0,
+    "input_back": 112.0,
+    "enter_ffn": 7,
+    "leave_ffn": 100,
+    "finish": 6,
+    "end": 8,
+}
+
+
+def launch(body, grid, ins, outs, scratch=(), prefetch=(), after=(), name=None):
     n_pre, n_in, n_after = len(prefetch), len(ins), len(after)
 
     def kernel(*refs):
@@ -45,7 +65,7 @@
             scratch_shapes=list(scratch),
         ),
         compiler_params=pltpu.CompilerParams(vmem_limit_bytes=58 << 20),
-        cost_estimate=pl.CostEstimate(flops=flops, bytes_accessed=moved, transcendentals=0),
+        cost_estimate=pl.CostEstimate(flops=int(TAKES[name] * 1e9), bytes_accessed=int(TAKES[name] * 2e6), transcendentals=0),
         name=name,
     )(*prefetch, *(a for a, _ in ins), *after)
 
@@ -57,6 +77,46 @@
 def fixed(array):
     zeros = (0,) * array.ndim
     return (array, pl.BlockSpec(array.shape, lambda *_: zeros, pipeline_mode=pl.Buffered(1)))
+
+
+def arrivals(pieces, width):
+    counts = [p.shape[0] // BLK for p in pieces]
+    starts = [sum(counts[:a]) for a in range(len(counts))]
+    inputs = []
+    for piece, start, count in zip(pieces, starts, counts):
+        if count == 1:
+            inputs.append(fixed(piece))
+        else:
+            spec = pl.BlockSpec((BLK, width), lambda i, *_, s=start, c=count: (jnp.clip(i - s, 0, c - 1), 0))
+            inputs.append((piece, spec))
+
+    def read(refs, buffer):
+        step = pl.program_id(0)
+        for ref, start, count in zip(refs, starts, counts):
+
+            @pl.when((step >= start) & (step < start + count))
+            def _():
+                buffer[...] = ref[...]
+
+    return inputs, read
+
+
+def departures(rows, width, groups):
+    count = rows // BLK // groups
+    outs = []
+    for a in range(groups):
+        spec = pl.BlockSpec((BLK, width), lambda i, *_, s=a * count: (jnp.clip(i - s, 0, count - 1), 0))
+        outs.append(((rows // groups, width), jnp.bfloat16, spec))
+
+    def write(refs, value):
+        step = pl.program_id(0)
+        for a, ref in enumerate(refs):
+
+            @pl.when(step // count == a)
+            def _():
+                ref[...] = value
+
+    return outs, write
 
 
 def columns(lines):
@@ -79,7 +139,31 @@
     return value * straight + turned if sign > 0 else value * straight - turned
 
 
-def qkv_project(low, weight, bias, tables):
+def enter_attention(pieces, gain, shift):
+    rows, wide = sum(p.shape[0] for p in pieces), pieces[0].shape[1]
+    inputs, read = arrivals(pieces, wide)
+
+    def body(g_ref, s_ref, *rest):
+        piece_refs, (x_ref, low_ref, stat_ref) = rest[: len(pieces)], rest[len(pieces) :]
+        read(piece_refs, x_ref)
+        spread = x_ref[...].astype(jnp.float32)
+        center = jnp.mean(spread, axis=-1, keepdims=True)
+        spread = spread - center
+        inverse = lax.rsqrt(jnp.mean(spread * spread, axis=-1, keepdims=True) + NORM_EPS)
+        low_ref[...] = (spread * inverse * g_ref[...] + s_ref[...]).astype(jnp.bfloat16)
+        lane = lax.broadcasted_iota(jnp.int32, (BLK, 128), 1)
+        stat_ref[...] = jnp.where(lane == 0, center, inverse)
+
+    return launch(
+        body,
+        (rows // BLK,),
+        [fixed(gain), fixed(shift)] + inputs,
+        [((rows, wide), jnp.bfloat16, tile(BLK, wide))] * 2 + [((rows, 128), jnp.float32, tile(BLK, 128))],
+        name="enter_attention",
+    )
+
+
+def qkv_project(low, weight, bias, tables, after=()):
     rows, width = low.shape
     cols = weight.shape[1] // 3
 
@@ -100,13 +184,12 @@
         (rows // BLK,),
         [(low, tile(BLK, width)), fixed(weight), fixed(bias)] + [(t, tile(BLK, 128)) for t in tables],
         [((rows, cols), jnp.bfloat16, tile(BLK, cols))] * 3,
+        after=after,
         name="qkv_project",
-        flops=2 * rows * width * 3 * cols,
-        moved=rows * width * 4,
-    )
-
-
-def attention_fwd(q, k, v, lo, hi, slots, first, last):
+    )
+
+
+def attention_fwd(q, k, v, lo, hi, slots, first, last, after=()):
     rows, width = q.shape
     blocks = rows // BLK
     heads = width // HEAD_DIM
@@ -186,55 +269,101 @@
             pltpu.VMEM((blocks, heads, BLK, BLK), jnp.float32),
         ],
         prefetch=(slots, first, last),
+        after=after,
         name="attention_forward",
-        flops=4 * rows * rows * width,
-        moved=rows * width * 12,
-    )
-
-
-def out_project(attn, stats, gain, shift, weight):
+    )
+
+
+def out_project(attn, stats, gain, shift, weight, groups, after=()):
     rows, width = attn.shape
     wide = weight.shape[1]
+    outs, write = departures(rows, wide, groups)
 
     def body(a_ref, g_ref, s_ref, w_ref, *rest):
-        stat_refs, (low_ref, part_ref) = rest[: len(stats)], rest[len(stats) :]
+        stat_refs, (low_ref, *part_refs) = rest[: len(stats)], rest[len(stats) :]
         center, inverse = columns(joined([r[0:1] for r in stat_refs], [r[1:2] for r in stat_refs], width))
         low = ((a_ref[...] - center) * inverse * g_ref[...] + s_ref[...]).astype(jnp.bfloat16)
         low_ref[...] = low
-        part_ref[...] = nn(low, w_ref[...]).astype(jnp.bfloat16)
+        write(part_refs, nn(low, w_ref[...]).astype(jnp.bfloat16))
+
+    low, *parts = launch(
+        body,
+        (rows // BLK,),
+        [(attn, tile(BLK, width)), fixed(gain), fixed(shift), fixed(weight)] + list(stats),
+        [((rows, width), jnp.bfloat16, tile(BLK, width))] + outs,
+        after=after,
+        name="out_project",
+    )
+    return low, parts
+
+
+def down_project(low, weight, groups, after=()):
+    rows, width = low.shape
+    wide = weight.shape[1]
+    outs, write = departures(rows, wide, groups)
+
+    def body(l_ref, w_ref, *part_refs):
+        write(part_refs, nn(l_ref[...], w_ref[...]).astype(jnp.bfloat16))
 
     return launch(
         body,
         (rows // BLK,),
-        [(attn, tile(BLK, width)), fixed(gain), fixed(shift), fixed(weight)] + list(stats),
-        [((rows, width), jnp.bfloat16, tile(BLK, width)), ((rows, wide), jnp.bfloat16, tile(BLK, wide))],
-        name="out_project",
-        flops=2 * rows * width * wide,
-        moved=rows * (width * 6 + wide * 2),
+        [(low, tile(BLK, width)), fixed(weight)],
+        outs,
+        after=after,
+        name="down_project",
+    )
+
+
+def add_rows(pairs, after=()):
+    wide = pairs[0][0].shape[1]
+    half = pairs[0][0].shape[0] // 2
+    piece = min(128, half)
+
+    def body(*refs):
+        ins, outs = refs[: 2 * len(pairs)], refs[2 * len(pairs) :]
+        for i, ref in enumerate(outs):
+            ref[...] = (ins[2 * i][...].astype(jnp.float32) + ins[2 * i + 1][...].astype(jnp.float32)).astype(jnp.bfloat16)
+
+    spec = pl.BlockSpec((piece, wide), lambda i: (half // piece + i, 0))
+    return launch(
+        body,
+        (half // piece,),
+        [(x, spec) for pair in pairs for x in pair],
+        [((half, wide), jnp.bfloat16, tile(piece, wide))] * len(pairs),
+        after=after,
+        name="add_rows",
     )
 
 
 def own_rows(body, wholes, rows_in, terms, outs, sums=0, after=(), name=None):
-    two, half, wide = rows_in[0].shape
+    half, wide = rows_in[0][0].shape
     piece = min(128, half)
     count = len(terms[0])
 
     def kernel(*refs):
         whole_refs, refs = refs[: len(wholes)], refs[len(wholes) :]
-        row_refs, refs = refs[: len(rows_in)], refs[len(rows_in) :]
-        term_refs, out_refs = refs[: 2 * count], refs[2 * count :]
+        row_refs, refs = refs[: 2 * len(rows_in)], refs[2 * len(rows_in) :]
+        term_refs, out_refs = refs[: 2 * count], list(refs[2 * count :])
+        targets = []
+        for _, stacked in outs:
+            if stacked:
+                ref = out_refs.pop(0)
+                targets.append((ref.at[0], ref.at[1]))
+            else:
+                targets.append((out_refs.pop(0), out_refs.pop(0)))
         vectors = [r[...] for r in whole_refs]
         added = [0.0] * sums
         for side in range(2):
             total = term_refs[side * count][...].astype(jnp.float32)
             for r in term_refs[side * count + 1 : (side + 1) * count]:
                 total = total + r[...].astype(jnp.float32)
-            values = body(vectors, [r[side] for r in row_refs], total)
-            for ref, value in zip(out_refs, values[: len(outs)]):
-                ref[side] = value.astype(ref.dtype)
+            values = body(vectors, [r[...] for r in row_refs[side::2]], total)
+            for target, value in zip(targets, values[: len(outs)]):
+                target[side][...] = value.astype(target[side].dtype)
             added = [a + jnp.sum(v, axis=0, keepdims=True) for a, v in zip(added, values[len(outs) :])]
         if sums:
-            sum_ref = out_refs[len(outs)]
+            sum_ref = out_refs[0]
 
             @pl.when(pl.program_id(0) == 0)
             def _():
@@ -243,23 +372,25 @@
             for i, a in enumerate(added):
                 sum_ref[i : i + 1, :] += a
 
-    own = pl.BlockSpec((2, piece, wide), lambda i: (0, i, 0))
     pieces = []
     for side in range(2):
         for array, start in terms[side]:
             pieces.append((array, pl.BlockSpec((piece, wide), lambda i, at=start // piece: (at + i, 0))))
-    results = [((2, half, wide), d, own) for d in outs]
+    results = []
+    for d, stacked in outs:
+        if stacked:
+            results.append(((2, half, wide), d, pl.BlockSpec((2, piece, wide), lambda i: (0, i, 0))))
+        else:
+            results += [((half, wide), d, tile(piece, wide))] * 2
     if sums:
         results.append(((8, wide), jnp.float32, pl.BlockSpec((8, wide), lambda i: (0, 0))))
     return launch(
         kernel,
         (half // piece,),
-        [fixed(w) for w in wholes] + [(r, own) for r in rows_in] + pieces,
+        [fixed(w) for w in wholes] + [(r, tile(piece, wide)) for pair in rows_in for r in pair] + pieces,
         results,
         after=after,
         name=name,
-        flops=40 * half * wide,
-        moved=half * wide * 16,
     )
 
 
@@ -281,12 +412,15 @@
 GELU_C = 0.7978845608028654
 
 
-def ffn_up(mid, cot, w_up, w_down, bias, gain, after=()):
-    rows, wide = mid.shape
+def ffn_up(pieces, cot, w_up, w_down, bias, gain, after=()):
+    rows, wide = cot.shape
+    inputs, read = arrivals(pieces, wide)
     units = w_up.shape[1]
     chunk = min(512, units)
 
-    def body(m_ref, c_ref, u_w, d_w, b_ref, g_ref, up_ref, grad_ref, stat_ref, gel_ref):
+    def body(c_ref, u_w, d_w, b_ref, g_ref, *rest):
+        m_ref, up_ref, grad_ref, stat_ref, gel_ref = rest[len(pieces) :]
+        read(rest[: len(pieces)], m_ref)
         total = scaled_total = 0.0
         for at in range(0, units, chunk):
             span = slice(at, at + chunk)
@@ -314,8 +448,9 @@
     return launch(
         body,
         (rows // BLK,),
-        [(mid, tile(BLK, wide)), (cot, tile(BLK, wide)), fixed(w_up), fixed(w_down), fixed(bias), fixed(gain)],
+        [(cot, tile(BLK, wide)), fixed(w_up), fixed(w_down), fixed(bias), fixed(gain)] + inputs,
         [
+            ((rows, wide), jnp.bfloat16, tile(BLK, wide)),
             ((rows, units), jnp.float32, tile(BLK, units)),
             ((rows, units), jnp.float32, tile(BLK, units)),
             ((8, rows), jnp.float32, pl.BlockSpec((8, BLK), lambda i, *_: (0, i))),
@@ -323,19 +458,18 @@
         scratch=[pltpu.VMEM((BLK, units), jnp.float32)],
         after=after,
         name="ffn_up",
-        flops=4 * rows * wide * units,
-        moved=rows * (wide * 4 + units * 8),
-    )
-
-
-def ffn_mid(up, grad, stats, gain, shift, w_up):
+    )
+
+
+def ffn_mid(up, grad, stats, gain, shift, w_up, groups):
     rows, units = up.shape
     wide = w_up.shape[0]
     chunk = min(512, units)
     ranks = len(stats)
+    outs, write = departures(rows, wide, groups)
 
     def body(u_ref, f_ref, g_ref, s_ref, w_ref, *rest):
-        stat_refs, (low_ref, gup_ref, part_ref, sum_ref) = rest[:ranks], rest[ranks:]
+        stat_refs, (low_ref, gup_ref, sum_ref, *part_refs) = rest[:ranks], rest[ranks:]
         centers = [r[0:1] for r in stat_refs]
         center, inverse = joined(centers, [r[1:2] for r in stat_refs], units)
         share = 1.0 / (units * ranks)
@@ -362,31 +496,33 @@
             sum_ref[0:1, span] += jnp.sum(f * normed, axis=0, keepdims=True)
             sum_ref[1:2, span] += jnp.sum(f, axis=0, keepdims=True)
             sum_ref[2:3, span] += jnp.sum(gup.astype(jnp.float32), axis=0, keepdims=True)
-        part_ref[...] = nt(gup_ref[...], w_ref[...]).astype(jnp.bfloat16)
-
-    return launch(
+        write(part_refs, nt(gup_ref[...], w_ref[...]).astype(jnp.bfloat16))
+
+    low, gup, sums, *parts = launch(
         body,
         (rows // BLK,),
         [(up, tile(BLK, units)), (grad, tile(BLK, units)), fixed(gain), fixed(shift), fixed(w_up)] + list(stats),
         [
             ((rows, units), jnp.bfloat16, tile(BLK, units)),
             ((rows, units), jnp.bfloat16, tile(BLK, units)),
-            ((rows, wide), jnp.bfloat16, tile(BLK, wide)),
             ((8, units), jnp.float32, pl.BlockSpec((8, units), lambda i, *_: (0, 0))),
-        ],
+        ]
+        + outs,
         name="ffn_mid",
-        flops=2 * rows * wide * units,
-        moved=rows * (wide * 2 + units * 12),
-    )
-
-
-def branch_back(resid, w_out, attn, stats, gain, after=()):
-    rows, wide = resid.shape
-    width = attn.shape[1]
+    )
+    return low, gup, sums, parts
+
+
+def branch_back(pieces, w_out, attn, stats, gain, after=()):
+    rows, width = attn.shape
+    wide = w_out.shape[1]
     ranks = len(stats)
-
-    def body(r_ref, w_ref, a_ref, g_ref, *rest):
-        stat_refs, (grad_ref, stat_ref, sum_ref) = rest[:ranks], rest[ranks:]
+    inputs, read = arrivals(pieces, wide)
+
+    def body(w_ref, a_ref, g_ref, *rest):
+        stat_refs, rest = rest[:ranks], rest[ranks:]
+        r_ref, grad_ref, stat_ref, sum_ref = rest[len(pieces) :]
+        read(rest[: len(pieces)], r_ref)
         center, inverse = columns(joined([r[0:1] for r in stat_refs], [r[1:2] for r in stat_refs], width))
 
         @pl.when(pl.program_id(0) == 0)
@@ -407,16 +543,15 @@
     return launch(
         body,
         (rows // BLK,),
-        [(resid, tile(BLK, wide)), fixed(w_out), (attn, tile(BLK, width)), fixed(gain)] + list(stats),
+        [fixed(w_out), (attn, tile(BLK, width)), fixed(gain)] + list(stats) + inputs,
         [
+            ((rows, wide), jnp.bfloat16, tile(BLK, wide)),
             ((rows, width), jnp.float32, tile(BLK, width)),
             ((8, rows), jnp.float32, pl.BlockSpec((8, BLK), lambda i, *_: (0, i))),
             ((8, width), jnp.float32, pl.BlockSpec((8, width), lambda i, *_: (0, 0))),
         ],
         after=after,
         name="branch_back",
-        flops=2 * rows * wide * width,
-        moved=rows * (wide * 2 + width * 8),
     )
 
 
@@ -451,16 +586,17 @@
         ],
         after=after,
         name="attn_grad",
-        flops=20 * rows * width,
-        moved=rows * width * 10,
-    )
-
-
-def attention_bwd(q, k, v, g, lse, dot, lo, hi, tables, slots, first, last, after=()):
+    )
+
+
+def attention_bwd(part, parts, q, k, v, g, lse, dot, lo, hi, tables, slots, first, last, after=()):
     rows, width = q.shape
+    width //= parts
     blocks = rows // BLK
     heads = width // HEAD_DIM
+    base = part * heads
     scale = HEAD_DIM**-0.5
+    own_columns = pl.BlockSpec((rows, width), lambda *_: (0, part), pipeline_mode=pl.Buffered(1))
 
     def body(slots, first, last, q_ref, k_ref, v_ref, g_ref, lse_ref, dot_ref, lo_ref, hi_ref, *rest):
         table_refs, (out_ref, dqt, qt, gt, accs) = rest[:6], rest[6:]
@@ -495,9 +631,9 @@
                     two = slice(h // 2 * 128, h // 2 * 128 + 128)
                     span = slice(h * HEAD_DIM, (h + 1) * HEAD_DIM)
                     s = nn(ks[h], qt[two, at])
-                    p = jnp.where(seen, jnp.exp(s - lse_ref[h : h + 1, at]), 0.0)
+                    p = jnp.where(seen, jnp.exp(s - lse_ref[base + h : base + h + 1, at]), 0.0)
                     dp = nn(vs[h], gt[two, at])
-                    ds = (p * (dp - dot_ref[h : h + 1, at])).astype(jnp.bfloat16)
+                    ds = (p * (dp - dot_ref[base + h : base + h + 1, at])).astype(jnp.bfloat16)
                     accs[1, h] += nn(p.astype(jnp.bfloat16), g_ref[at, two])
                     accs[0, h] += nn(ds, q_ref[at, two])
                     dqt[span, at] += nn(kts[span, :], ds)
@@ -524,7 +660,7 @@
     return launch(
         body,
         (1,),
-        [fixed(a) for a in (q, k, v, g, lse, dot, lo, hi, *tables)],
+        [(a, own_columns) for a in (q, k, v, g)] + [fixed(a) for a in (lse, dot, lo, hi, *tables)],
         [((rows, 3 * width), jnp.bfloat16, pl.BlockSpec((rows, 3 * width), lambda *_: (0, 0), pipeline_mode=pl.Buffered(1)))],
         scratch=[
             pltpu.VMEM((width, rows), jnp.float32),
@@ -535,42 +671,50 @@
         prefetch=(slots, first, last),
         after=after,
         name="attention_backward",
-        flops=10 * rows * rows * width,
-        moved=rows * width * 14,
     )[0]
 
 
-def input_back(grad, weight, x, after=()):
-    rows, cols = grad.shape
-    wide = weight.shape[0]
-
-    def body(g_ref, w_ref, x_ref, part_ref, bias_ref, sum_ref):
+def input_back(grads, weight, x, row_stats, groups, after=()):
+    rows, wide = x.shape
+    cols = weight.shape[1]
+    parts = len(grads)
+    small = cols // parts // 3
+    outs, write = departures(rows, wide, groups)
+
+    def body(w_ref, x_ref, stat_ref, *rest):
+        grad_refs, (bias_ref, sum_ref, *part_refs), g_ref = rest[:parts], rest[parts:-1], rest[-1]
+
         @pl.when(pl.program_id(0) == 0)
         def _():
             sum_ref[...] = jnp.zeros_like(sum_ref)
             bias_ref[...] = jnp.zeros_like(bias_ref)
 
-        part = nt(g_ref[...], w_ref[...])
-        part_ref[...] = part.astype(jnp.bfloat16)
+        for p, ref in enumerate(grad_refs):
+            for j in range(3):
+                at = (j * parts + p) * small
+                g_ref[:, at : at + small] = ref[:, j * small : (j + 1) * small]
+        value = nt(g_ref[...], w_ref[...])
+        write(part_refs, value.astype(jnp.bfloat16))
         bias_ref[0:1, :] += jnp.sum(g_ref[...].astype(jnp.float32), axis=0, keepdims=True)
-        normed, _ = norm_parts(x_ref[...].astype(jnp.float32))
-        sum_ref[0:1, :] += jnp.sum(part * normed, axis=0, keepdims=True)
-        sum_ref[1:2, :] += jnp.sum(part, axis=0, keepdims=True)
-
-    return launch(
+        normed = (x_ref[...].astype(jnp.float32) - stat_ref[:, 0:1]) * stat_ref[:, 1:2]
+        sum_ref[0:1, :] += jnp.sum(value * normed, axis=0, keepdims=True)
+        sum_ref[1:2, :] += jnp.sum(value, axis=0, keepdims=True)
+
+    bias_sums, sums, *parts_out = launch(
         body,
         (rows // BLK,),
-        [(grad, tile(BLK, cols)), fixed(weight), (x, tile(BLK, wide))],
+        [fixed(weight), (x, tile(BLK, wide)), (row_stats, tile(BLK, 128))]
+        + [(g, tile(BLK, cols // parts)) for g in grads],
         [
-            ((rows, wide), jnp.bfloat16, tile(BLK, wide)),
             ((8, cols), jnp.float32, pl.BlockSpec((8, cols), lambda i, *_: (0, 0))),
             ((8, wide), jnp.float32, pl.BlockSpec((8, wide), lambda i, *_: (0, 0))),
-        ],
+        ]
+        + outs,
+        scratch=[pltpu.VMEM((BLK, cols), jnp.bfloat16)],
         after=after,
         name="input_back",
-        flops=2 * rows * cols * wide,
-        moved=rows * (wide * 4 + cols * 2),
-    )
+    )
+    return bias_sums, sums, parts_out
 
 
 def key_limits(bounds, spans, kind, total):
@@ -600,6 +744,8 @@
         self.ranks, self.batches, self.rows, self.me = ranks, batches, rows, me
         self.square = ranks == 4 and rows == 2 * BLK
         self.half = rows // 2
+        self.groups = 4 if self.square else 1
+        self.forwarded = ()
         self.order = ((0, 1, 2, 3), (0, 2, 1, 3))
         total = ranks * rows
         block = jnp.arange(total // BLK, dtype=jnp.int32)
@@ -618,25 +764,44 @@
     def swap(self, value, bit):
         return lax.ppermute(value, "seq", [(r, r ^ bit) for r in range(self.ranks)])
 
-    def gather(self, upper, lower):
+    def gather(self, upper, lower, late=None):
         if not self.square:
-            return lax.all_gather(jnp.concatenate([upper, lower], axis=0), "seq", axis=0, tiled=True)
-        upper = jnp.concatenate([upper, self.swap(upper, 1)], axis=0)
-        lower = jnp.concatenate([lower, self.swap(lower, 2)], axis=0)
-        return jnp.concatenate([upper, self.swap(upper, 2), lower, self.swap(lower, 1)], axis=0)
-
-    def scatter(self, low):
-        n = self.half
+            return [lax.all_gather(jnp.concatenate([upper, lower], axis=0), "seq", axis=0, tiled=True)]
+        near_upper, near_lower = self.swap(upper, 1), self.swap(lower, 2)
+        again = (upper, lower, near_upper, near_lower)
+        if late is not None:
+            again, _ = lax.optimization_barrier((again, late))
+        return [upper, near_upper, self.swap(again[0], 2), self.swap(again[2], 2)] + [
+            lower,
+            near_lower,
+            self.swap(again[1], 1),
+            self.swap(again[3], 1),
+        ]
+
+    def scatter(self, parts, after=()):
         if not self.square:
-            own = lax.psum_scatter(low, "seq", scatter_dimension=0, tiled=True)
-            return [[(own, 0)], [(own, n)]]
-        out = []
-        for at, bits in ((0, (2, 1)), (4 * n, (1, 2))):
-            near = self.swap(low[at + 2 * n : at + 4 * n], bits[0])
-            far = low[at + n : at + 2 * n].astype(jnp.float32) + near[n:].astype(jnp.float32)
-            far = self.swap(far.astype(jnp.bfloat16), bits[1])
-            out.append([(low, at), (near, 0), (far, 0)])
-        return out
+            own = lax.psum_scatter(parts[0], "seq", scatter_dimension=0, tiled=True)
+            return [[(own, 0)], [(own, self.half)]]
+        keep_upper, send_upper, keep_lower, send_lower = parts
+        near_upper, near_lower = self.swap(send_upper, 2), self.swap(send_lower, 1)
+        far_upper, far_lower = add_rows([(keep_upper, near_upper), (keep_lower, near_lower)], after)
+        sums = (far_upper, far_lower)
+        far_upper, far_lower = self.swap(far_upper, 1), self.swap(far_lower, 2)
+        self.forwarded = sums
+        return [[(keep_upper, 0), (near_upper, 0), (far_upper, 0)], [(keep_lower, 0), (near_lower, 0), (far_lower, 0)]]
+
+    def picked(self, value, axis):
+        if not self.square:
+            return [jnp.moveaxis(value, axis, 0)]
+        return [lax.dynamic_index_in_dim(value, self.me ^ r, axis, False) for r in range(self.ranks)]
+
+    def sent(self, pieces):
+        if not self.square:
+            return [lax.all_to_all(pieces[0], "seq", 0, 0)]
+        return [pieces[0]] + [self.swap(pieces[r], r) for r in range(1, self.ranks)]
+
+    def ordered(self, pieces):
+        return flipped(jnp.stack(pieces), self.me, 2) if self.square else pieces[0]
 
     def spread(self, value):
         lines = value.shape[0]
@@ -652,8 +817,7 @@
         return out
 
 
-def flipped(value, batch, me, bits):
-    device = batch * 4 + me
+def flipped(value, device, bits):
     shape = value.shape
     for bit in range(bits):
         two = value.reshape((-1, 2, 1 << bit) + shape[1:])
@@ -670,15 +834,17 @@
         parts = jnp.concatenate(
             [parts] + [lax.ppermute(parts, axis, [(r, r ^ s) for r in range(count)]) for s in steps], axis=0
         )
-    return flipped(parts, batch, me, 5)
-
-
-def sum_small(value, batches, ranks):
+    return flipped(parts, batch * ranks + me, 5)
+
+
+def sum_small(value, batches, ranks, late):
     if (batches, ranks) != (8, 4):
         return lax.psum_scatter(value, EVERY, scatter_dimension=0, tiled=True)[0]
     batch, me = lax.axis_index("batch"), lax.axis_index("seq")
-    value = flipped(value, batch, me, 5)
+    value = flipped(value, batch * ranks + me, 5)
     for axis, count, steps, left in (("batch", batches, (2, 4, 6), 8), ("batch", batches, (1,), 4), ("seq", ranks, (1, 2, 3), 1)):
+        if axis == "seq":
+            value, _ = lax.optimization_barrier((value, late))
         total = value[:left]
         for i, s in enumerate(steps):
             at = (i + 1) * left
@@ -730,15 +896,24 @@
     strip, d_rows = w_down.shape[0], w_up.shape[0]
     units = strip * batches
     f32, bf16 = jnp.float32, jnp.bfloat16
-    x_own, cot_own = layer_input.reshape(2, half, D), cotangent.reshape(2, half, D)
-
-    part_qkv = lax.all_to_all(w_qkv.reshape(d_rows, 3, ranks, cols), "seq", 2, 0).reshape(d_rows * ranks, 3 * cols)
-    full_qkv = lax.all_gather(part_qkv, "batch", axis=0, tiled=True)
-    x_full = move.gather(x_own[0], x_own[1])
+    x_own = [layer_input.reshape(2, half, D)[i] for i in range(2)]
+    cot_own = [cotangent.reshape(2, half, D)[i] for i in range(2)]
+
+    x_pieces = move.gather(*x_own, late=())
     small = jnp.concatenate(
         [bias_qkv.reshape(-1), gains_d.reshape(-1), biases_d.reshape(-1), gain_ff, biases_ff.reshape(-1)]
     )
     small = share_small(small, batches, ranks)
+
+    w_qkv, _ = lax.optimization_barrier((w_qkv, x_own))
+    part_qkv = move.ordered(move.sent(move.picked(w_qkv.reshape(d_rows, 3, ranks, cols), 2)))
+    up_pieces = move.picked(w_up.reshape(d_rows, batches, ranks, strip), 2)
+    order = [(i, (i % batches) * ranks + i // batches) for i in range(batches * ranks)]
+    part_out = lax.ppermute(w_out, EVERY, order)
+    tables = rot_tables(move.places)
+    early = (small, part_out, up_pieces, tables, x_pieces[1:2] + x_pieces[5:6])
+    part_qkv, (small, part_out, up_pieces, tables, _) = lax.optimization_barrier((part_qkv, early))
+    full_qkv = lax.all_gather(part_qkv.reshape(d_rows * ranks, 3 * cols), "batch", axis=0, tiled=True)
     cut = 11 * d_rows
     rows_d = small[:, :cut].reshape(-1, 11, d_rows).swapaxes(0, 1).reshape(11, D).astype(f32)
     rows_f = small[:, cut:].reshape(batches, ranks, 3, strip)
@@ -750,42 +925,51 @@
     gain_branch, shift_branch = branch[1:2], branch[4:5]
     gain_ffn, shift_ffn, shift_up = rows_f[0:1], rows_f[1:2], rows_f[2:3]
 
-    order = [(i, (i % batches) * ranks + i // batches) for i in range(batches * ranks)]
-    part_out = lax.ppermute(w_out, EVERY, order)
+    (up_pieces, *cot_send), _ = lax.optimization_barrier(((up_pieces, *cot_own), x_pieces))
     full_out = lax.all_gather(part_out, "batch", axis=0, tiled=True)
-    part_up = lax.all_to_all(w_up.reshape(d_rows, batches, ranks, strip), "seq", 2, 0).reshape(d_rows * ranks, units)
     full_down = lax.all_gather(w_down, "batch", axis=0, tiled=True)
-    full_up = lax.all_gather(part_up, "batch", axis=0, tiled=True)
-    cot_full = move.gather(cot_own[0], cot_own[1])
-
-    normed_all, _ = norm_parts(x_full.astype(f32))
-    input_low = (normed_all * gain_in + shift_in).astype(bf16)
-    tables = rot_tables(move.places)
+    up_pieces = move.sent(up_pieces)
+
+    x_full, input_low, row_stats = enter_attention(x_pieces, gain_in, shift_in)
     query_rot, key_rot, value_low = qkv_project(input_low, full_qkv, qkv_shift, tables)
+    cot_pieces = move.gather(*cot_send, late=(query_rot,))
+    up_pieces, _ = lax.optimization_barrier((up_pieces, query_rot))
+    full_up = lax.all_gather(move.ordered(up_pieces).reshape(d_rows * ranks, units), "batch", axis=0, tiled=True)
     lo, hi, q_lo, q_hi = key_limits(doc_bounds[0], span_starts[0], data_type[0], tokens)
     k_first, k_last, q_first, q_last = block_limits(lo, hi, q_lo, q_hi)
     lo, hi = lo[None], hi[None]
-    attn, lse, stat = attention_fwd(query_rot, key_rot, value_low, lo, hi, move.slots, k_first, k_last)
+    attn, lse, stat = attention_fwd(
+        query_rot, key_rot, value_low, lo, hi, move.slots, k_first, k_last, after=cot_pieces[1:2] + cot_pieces[5:6]
+    )
+    stat, _ = lax.optimization_barrier((stat, cot_pieces))
     stats2 = move.spread(stat)
-    branch_low, part = out_project(attn, stats2, gain_branch, shift_branch, full_out)
+    branch_low, parts = out_project(attn, stats2, gain_branch, shift_branch, full_out, move.groups, after=cot_pieces)
 
     def enter(vectors, values, arrived):
         resid = values[0].astype(f32) + (arrived + vectors[0])
         normed, _ = norm_parts(resid)
         return resid, normed * vectors[1] + vectors[2]
 
-    resid, mid_own = own_rows(
-        enter, [shift_out, gain_mid, shift_mid], [x_own], move.scatter(part), [f32, bf16], name="enter_ffn"
-    )
-    mid_low = move.gather(mid_own[0], mid_own[1])
-    up_proj, grad_ffn, stat = ffn_up(mid_low, cot_full, full_up, full_down, shift_up, gain_ffn)
+    cot_full = jnp.concatenate(cot_pieces, axis=0)
+    *resid, mid_upper, mid_lower = own_rows(
+        enter,
+        [shift_out, gain_mid, shift_mid],
+        [x_own],
+        move.scatter(parts),
+        [(f32, False), (bf16, False)],
+        after=(cot_full,),
+        name="enter_ffn",
+    )
+    mid_pieces = move.gather(mid_upper, mid_lower)
+    mid_low, up_proj, grad_ffn, stat = ffn_up(mid_pieces, cot_full, full_up, full_down, shift_up, gain_ffn)
     stats4 = move.spread(stat)
-    ffn_low, grad_up, part, sums_ff = ffn_mid(up_proj, grad_ffn, stats4, gain_ffn, shift_ffn, full_up)
-    arriving = move.scatter(part)
+    ffn_low, grad_up, sums_ff, parts = ffn_mid(up_proj, grad_ffn, stats4, gain_ffn, shift_ffn, full_up, move.groups)
+    g_down = tn(ffn_low, cot_full).astype(bf16)
+    sum_down = lax.psum_scatter(g_down, "batch", scatter_dimension=0, tiled=True)
+    arriving = move.scatter(parts, (g_down,))
+    grad_up, _ = lax.optimization_barrier((grad_up, move.forwarded))
     g_up = tn(mid_low, grad_up).astype(bf16)
-    g_down = tn(ffn_low, cot_full).astype(bf16)
     sum_up = lax.psum_scatter(g_up, "batch", scatter_dimension=0, tiled=True)
-    sum_down = lax.psum_scatter(g_down, "batch", scatter_dimension=0, tiled=True)
 
     def leave(vectors, values, arrived):
         normed, inverse = norm_parts(values[0])
@@ -794,31 +978,63 @@
         low = grad.astype(bf16)
         return grad, low, arrived * normed, arrived, low.astype(f32), cot
 
-    grad_resid, resid_own, sums_mid = own_rows(
-        leave, [gain_mid], [resid, cot_own], arriving, [f32, bf16], sums=4, after=(g_up, g_down), name="leave_ffn"
-    )
-    resid_low = move.gather(resid_own[0], resid_own[1])
-    down = nn(ffn_low, full_down).astype(bf16)
-
-    grad_branch, stat, sums_branch = branch_back(resid_low, full_out, attn, stats2, gain_branch, after=(down,))
-    down, _ = lax.optimization_barrier((down, stat))
-    arriving = move.scatter(down)
+    *grad_resid, resid_upper, resid_lower, sums_mid = own_rows(
+        leave,
+        [gain_mid],
+        [resid, cot_own],
+        arriving,
+        [(f32, False), (bf16, False)],
+        sums=4,
+        after=(g_up,),
+        name="leave_ffn",
+    )
+    resid_pieces = move.gather(resid_upper, resid_lower)
+    down_parts = down_project(ffn_low, full_down, move.groups, after=(resid_upper,))
+
+    resid_low, grad_branch, stat, sums_branch = branch_back(
+        resid_pieces, full_out, attn, stats2, gain_branch, after=down_parts
+    )
+    down_parts, _ = lax.optimization_barrier((down_parts, resid_pieces))
     stats3 = move.spread(stat)
     g_out = tn(branch_low, resid_low).astype(bf16)
     attn_low, dots = attn_grad(grad_branch, attn, stats2, stats3, gain_branch, after=(g_out,))
+
+    def back(part, after):
+        return attention_bwd(
+            part, 2, query_rot, key_rot, value_low, attn_low, lse, dots, lo, hi, tables, move.slots, q_first, q_last, after
+        )
+
+    grad_first = back(0, (sum_down,))
+    arriving = move.scatter(down_parts, (grad_first,))
+    forwarded = move.forwarded
+    g_first = tn(input_low, grad_first).astype(bf16)
+    sum_first = lax.psum_scatter(g_first, "batch", scatter_dimension=0, tiled=True)
+    g_out, _ = lax.optimization_barrier((g_out, sum_down))
     sum_out = lax.psum_scatter(g_out, "batch", scatter_dimension=0, tiled=True)
-    grad_qkv = attention_bwd(
-        query_rot, key_rot, value_low, attn_low, lse, dots, lo, hi, tables, move.slots, q_first, q_last
+    grad_second = back(1, (g_first, sum_up, sum_out, *forwarded))
+    up_rows = move.sent(move.picked(sum_up.reshape(ranks, d_rows, batches, strip), 0))
+    out_rows = lax.ppermute(sum_out, EVERY, [(b, a) for a, b in order])
+    bias_sums, sums_in, parts = input_back(
+        (grad_first, grad_second),
+        full_qkv,
+        x_full,
+        row_stats,
+        move.groups,
+        after=[terms[-1][0] for terms in arriving] + up_rows + [out_rows],
     )
 
     def finish(vectors, values, arrived):
         return (values[0] + (arrived + vectors[0]),)
 
-    result = own_rows(finish, [shift_down], [resid], arriving, [bf16], after=(grad_qkv,), name="finish")[0]
-    g_qkv = tn(input_low, grad_qkv).astype(bf16)
-    sum_qkv = lax.psum_scatter(g_qkv, "batch", scatter_dimension=0, tiled=True)
-    part, sums_qkv, sums_in = input_back(grad_qkv, full_qkv, x_full, after=(g_qkv,))
-    arriving = move.scatter(part)
+    result = own_rows(
+        finish, [shift_down], [resid], arriving, [(bf16, True)], after=(parts[0],), name="finish"
+    )[0]
+    out_up = jnp.moveaxis(move.ordered(up_rows), 0, 2).reshape(d_rows, batches * ranks * strip).astype(f32)
+    first_rows = move.sent(move.picked(sum_first.reshape(ranks, d_rows, 3, cols // 2), 0))
+    arriving = move.scatter(parts, (sum_first, result, out_up))
+    grad_second, _ = lax.optimization_barrier((grad_second, parts))
+    g_second = tn(input_low, grad_second).astype(bf16)
+    sum_second = lax.psum_scatter(g_second, "batch", scatter_dimension=0, tiled=True)
 
     def end(vectors, values, arrived):
         normed, inverse = norm_parts(values[0].astype(f32))
@@ -830,7 +1046,7 @@
     branch_rows = placed(sums_branch[:2])
     vector_d = jnp.concatenate(
         [
-            placed(sums_qkv[0].reshape(3, cols)),
+            placed(bias_sums[0].reshape(3, cols)),
             sums_in[:1],
             branch_rows[:1],
             sums_mid[:1],
@@ -848,16 +1064,16 @@
         ],
         axis=1,
     )
-    vector = sum_small(vector, batches, ranks)
-    grad_total = own_rows(end, [gain_in], [x_own, grad_resid], arriving, [f32], name="end")[0]
-
-    def to_rows(value, groups, wide):
-        value = lax.all_to_all(value.reshape(ranks, d_rows, groups, wide), "seq", 0, 2)
-        return value.reshape(d_rows, groups * ranks * wide).astype(f32)
-
-    out_qkv = to_rows(sum_qkv, 3, cols)
-    out_up = to_rows(sum_up, batches, strip)
-    out_out = lax.ppermute(sum_out, EVERY, [(b, a) for a, b in order]).astype(f32)
+    vector = sum_small(vector, batches, ranks, [terms[-1][0] for terms in arriving])
+    second_rows = move.picked(sum_second.reshape(ranks, d_rows, 3, cols // 2), 0)
+    grad_total = own_rows(
+        end, [gain_in], [x_own, grad_resid], arriving, [(f32, True)], after=second_rows, name="end"
+    )[0]
+
+    second_rows = move.sent(second_rows)
+    halves = [jnp.moveaxis(move.ordered(r), 0, 2) for r in (first_rows, second_rows)]
+    out_qkv = jnp.stack(halves, axis=3).reshape(d_rows, 3 * D).astype(f32)
+    out_out = out_rows.astype(f32)
     out_down = sum_down.astype(f32)
     own_d = vector[:cut].reshape(11, d_rows)
     own_f = vector[cut:].reshape(3, strip)

time: 1090 us -> 944 us (0.87); the launches traced: 1090 us -> 929 us
  Pallas kernels: 300 us -> 363 us
  starting transfers between devices: 194 us -> 132 us
  waiting for transfers between devices: 295 us -> 236 us
  local copies, waits for them, and re-layouts: 112 us -> 72.1 us
  other arithmetic: 59.6 us -> 21.4 us
  blocking collectives: 14.3 us -> 0 us
  matrix products: 100 us -> 88.1 us
    ppermute x7, starting transfers between devices: 112 us -> 38.4 us  [sum_small(): lax.ppermute(value[at:at + left], axis, [(r, r ^ s) for r in range(count)])]
    pallas_call x13 -> x20, Pallas kernels: 300 us -> 363 us  [launch(): pl.pallas_call(kernel, out_shape=tuple((jax.ShapeDtypeStruct(s, d) for s,...]
    ppermute x7, waiting for transfers between devices: 54.1 us -> 2.63 us  [sum_small(): lax.ppermute(value[at:at + left], axis, [(r, r ^ s) for r in range(count)])]
    ppermute x41 -> x64, starting transfers between devices: 35.8 us -> 71.2 us  [swap(): return lax.ppermute(value, 'seq', [(r, r ^ bit) for r in range(self.ranks)])]
    reduce_scatter x1, waiting for transfers between devices: 0.01 us -> 28.5 us  [local(): sum_up = lax.psum_scatter(g_up, 'batch', scatter_dimension=0, tiled=True)]
    ppermute x41 -> x64, waiting for transfers between devices: 214 us -> 186 us  [swap(): return lax.ppermute(value, 'seq', [(r, r ^ bit) for r in range(self.ranks)])]
    dot_general x1 -> x0, matrix products: 23.9 us -> none  [nn(): return jnp.dot(a, b, preferred_element_type=jnp.float32)]
    convert_element_type x8 -> x3, other arithmetic: 23.8 us -> 2.13 us  [the longest x1 1.78 us: local(): out_out = out_rows.astype(f32)]
  transfers between devices with their start and end apart: 68 -> 89, of which waited for: 31 -> 34; matrix products, arithmetic and copies ran while one was open for 21% -> 17% of each run, Pallas kernels for 18% -> 28%
where the time goes in v2:
time: 944 us; the launch traced here: 929 us
  Pallas kernels  363 us (38%)
  waiting for transfers between devices  236 us (25%)
  starting transfers between devices  132 us (14%)
  matrix products  88.1 us (9%)
  local copies, waits for them, and re-layouts  72.1 us (8%)
  other arithmetic  21.4 us (2%)
  between operations  16.1 us (2%)
    pallas_call x20, Pallas kernels, launch(): pl.pallas_call(kernel, out_shape=tuple((jax.ShapeDtypeStruct(s, d) for s,...  363 us
    ppermute x64, waiting for transfers between devices, swap(): return lax.ppermute(value, 'seq', [(r, r ^ bit) for r in range(self.ranks)])  186 us
    dot_general x5, matrix products, tn(): lax.dot_general(a, b, (((0,), (0,)), ((), ())), preferred_element_type=jn...  88.1 us
    ppermute x64, starting transfers between devices, swap(): return lax.ppermute(value, 'seq', [(r, r ^ bit) for r in range(self.ranks)])  71.2 us
    ppermute x7, starting transfers between devices, sum_small(): lax.ppermute(value[at:at + left], axis, [(r, r ^ s) for r in range(count)])  38.4 us
    reduce_scatter x1, waiting for transfers between devices, local(): sum_up = lax.psum_scatter(g_up, 'batch', scatter_dimension=0, tiled=True)  28.5 us
    unnamed x154, local copies, waits for them, and re-layouts  25.8 us
  transfers between devices with their start and end apart: 89, of which 34 were waited for; matrix products, arithmetic and copies ran while one was open for 17% of the time, Pallas kernels for 28%

profile of v2, /device:TPU:1, one launch (start us, length us, event | category | flops | bytes accessed | tf_op | source)
XLA Modules:
  0.0 928.9 jit_solution(8416103802722315917)
XLA Ops:
  91.2 22.5 %collective-permute-done.14.refs_5_ = bf16[256,2048]{1,0:T(8,128)(2,1)} collective-permute-done((bf16[256,2048]{1,0:T(8,128)(2,1)}, bf16[256,2048]{1,0:T(8,128)(2,1)}, u32[]{:S(2)}, u32[]{:S(2)}) %collective-permute-start.14) | collective-permute-done | bytes 1048608 | tf_op jit(solution)/shard_map/ppermute | solution.py:765
  118.2 12.0 %enter_attention.1 = (bf16[2048,2048]{1,0:T(8,128)(2,1)}, bf16[2048,2048]{1,0:T(8,128)(2,1)}, f32[2048,128]{1,0:T(8,128)}) custom-call(f32[1,2048]{1,0:T(1,128)} %slice.214.refs_0_, f32[1,2048]{1,0:T(1,128)} %slice.216.refs_1_, bf16[256,2048]{1,0:T(8,128)(2,1)} %get-tuple-element.112.refs_2_.refs_3_.refs_1_, ...), custom_call_target="tpu_custom_call" | custom-call | flops 12000000000 | bytes 24000000 | tf_op jit(solution)/shard_map/enter_attention/pallas_call | solution.py:57
  131.4 19.0 %qkv_project.1 = (bf16[2048,512]{1,0:T(8,128)(2,1)}, bf16[2048,512]{1,0:T(8,128)(2,1)}, bf16[2048,512]{1,0:T(8,128)(2,1)}) custom-call(bf16[2048,2048]{1,0:T(8,128)(2,1)} %get-tuple-element.116.refs_0_, bf16[2048,1536]{1,0:T(8,128)(2,1)} %all-gather.5.cloned.1.call-done.refs_1_.refs_0_, f32[1,1536]{1,0:T(1,128)} %bitcast.219, ...), custom_call_target="tpu_custom_call" | custom-call | flops 19000000512 | bytes 38000000 | tf_op jit(solution)/shard_map/qkv_project/pallas_call | solution.py:57
  158.0 25.4 %attention_forward.1 = (f32[2048,512]{1,0:T(8,128)}, f32[8,2048]{1,0:T(8,128)}, f32[8,2048]{1,0:T(8,128)}) custom-call(s32[8]{0:T(128)} %fusion.19.refs_0_, s32[8]{0:T(128)} %get-tuple-element.279.refs_1_, s32[8]{0:T(128)} %get-tuple-element.280.refs_2_, bf16[2048,512]{1,0:T(8,128)(2,1)} %get-tuple-element.124.refs_3_, ...), custom_call_target="tpu_custom_call" | custom-call | flops 41000001536 | bytes 82000000 | tf_op jit(solution)/shard_map/attention_forward/pallas_call | solution.py:57
  183.4 14.6 %collective-permute-done.20.refs_11_ = bf16[256,2048]{1,0:T(8,128)(2,1)} collective-permute-done((bf16[256,2048]{1,0:T(8,128)(2,1)}, bf16[256,2048]{1,0:T(8,128)(2,1)}, u32[]{:S(2)}, u32[]{:S(2)}) %collective-permute-start.20) | collective-permute-done | bytes 1048608 | tf_op jit(solution)/shard_map/ppermute | solution.py:765
  208.5 14.6 %out_project.1 = (bf16[2048,512]{1,0:T(8,128)(2,1)}, bf16[512,2048]{1,0:T(8,128)(2,1)}, bf16[512,2048]{1,0:T(8,128)(2,1)}, bf16[512,2048]{1,0:T(8,128)(2,1)}, bf16[512,2048]{1,0:T(8,128)(2,1)}) custom-call(f32[2048,512]{1,0:T(8,128)} %get-tuple-element.133.refs_0_.refs_1_, f32[1,512]{1,0:T(1,128)} %get-tuple-element.255.refs_1_.refs_2_, ...), custom_call_target="tpu_custom_call" | custom-call | flops 14000000000 | bytes 28000000 | tf_op jit(solution)/shard_map/out_project/pallas_call | solution.py:57
  228.1 34.7 %collective-permute-done.26.refs_1_.refs_6_ = bf16[512,2048]{1,0:T(8,128)(2,1)S(1)} collective-permute-done((bf16[512,2048]{1,0:T(8,128)(2,1)}, bf16[512,2048]{1,0:T(8,128)(2,1)S(1)}, u32[]{:S(2)}, u32[]{:S(2)}) %collective-permute-start.26) | collective-permute-done | bytes 2097184 | tf_op jit(solution)/shard_map/ppermute | solution.py:765
  296.7 13.1 %collective-permute-done.33.refs_6_ = bf16[256,2048]{1,0:T(8,128)(2,1)S(1)} collective-permute-done((bf16[256,2048]{1,0:T(8,128)(2,1)}, bf16[256,2048]{1,0:T(8,128)(2,1)S(1)}, u32[]{:S(2)}, u32[]{:S(2)}) %collective-permute-start.33) | collective-permute-done | bytes 1048608 | tf_op jit(solution)/shard_map/ppermute | solution.py:765
  311.7 21.0 %collective-permute-done.34.refs_7_ = bf16[256,2048]{1,0:T(8,128)(2,1)S(1)} collective-permute-done((bf16[256,2048]{1,0:T(8,128)(2,1)}, bf16[256,2048]{1,0:T(8,128)(2,1)S(1)}, u32[]{:S(2)}, u32[]{:S(2)}) %collective-permute-start.34) | collective-permute-done | bytes 1048608 | tf_op jit(solution)/shard_map/ppermute | solution.py:765
  332.7 22.5 %collective-permute-done.35.refs_8_ = bf16[256,2048]{1,0:T(8,128)(2,1)} collective-permute-done((bf16[256,2048]{1,0:T(8,128)(2,1)S(1)}, bf16[256,2048]{1,0:T(8,128)(2,1)}, u32[]{:S(2)}, u32[]{:S(2)}) %collective-permute-start.35) | collective-permute-done | bytes 1048608 | tf_op jit(solution)/shard_map/ppermute | solution.py:765
  355.2 54.6 %ffn_up.1 = (bf16[2048,2048]{1,0:T(8,128)(2,1)}, f32[2048,2048]{1,0:T(8,128)}, f32[2048,2048]{1,0:T(8,128)}, f32[8,2048]{1,0:T(8,128)}) custom-call(bf16[2048,2048]{1,0:T(8,128)(2,1)} %constant_dynamic-update-slice_fusion.refs_11_.refs_0_, bf16[2048,2048]{1,0:T(8,128)(2,1)} %all-gather.9.cloned.1.call-done.refs_1_.refs_4_, ...), custom_call_target="tpu_custom_call" | custom-call | flops 54000001024 | bytes 108000000 | tf_op jit(solution)/shard_map/ffn_up/pallas_call | solution.py:57
  416.0 47.1 %ffn_mid.1 = (bf16[2048,2048]{1,0:T(8,128)(2,1)}, bf16[2048,2048]{1,0:T(8,128)(2,1)}, f32[8,2048]{1,0:T(8,128)}, bf16[512,2048]{1,0:T(8,128)(2,1)}, bf16[512,204...) custom-call(f32[2048,2048]{1,0:T(8,128)} %get-tuple-element.159.refs_0_, ...), custom_call_target="tpu_custom_call" | custom-call | flops 46999998464 | bytes 94000000 | tf_op jit(solution)/shard_map/ffn_mid/pallas_call | solution.py:57
  464.8 33.2 %convolution_convert_fusion.1.refs_4_ = bf16[2048,2048]{1,0:T(8,128)(2,1)} fusion(bf16[2048,2048]{1,0:T(8,128)(2,1)} %get-tuple-element.162.refs_0_, bf16[2048,2048]{1,0:T(8,128)(2,1)} %constant_dynamic-update-slice_fusion.refs_11_.refs_0_), kind=kOutput, calls=%fused_computation.1 | convolution fusion | flops 17184063488 | bytes 25165824 | tf_op jit(solution)/shard_map/dot_general | solution.py:24
  505.4 23.8 %convolution_convert_fusion.refs_11_ = bf16[2048,2048]{1,0:T(8,128)(2,1)} fusion(bf16[2048,2048]{1,0:T(8,128)(2,1)} %get-tuple-element.169, bf16[2048,2048]{1,0:T(8,128)(2,1)} %get-tuple-element.171), kind=kOutput, calls=%fused_computation | convolution fusion | flops 17184063488 | bytes 25165824 | tf_op jit(solution)/shard_map/dot_general | solution.py:24
  530.5 11.6 %leave_ffn.1 = (f32[256,2048]{1,0:T(8,128)}, f32[256,2048]{1,0:T(8,128)}, bf16[256,2048]{1,0:T(8,128)(2,1)}, bf16[256,2048]{1,0:T(8,128)(2,1)}, f32[8,2048]{1,0:T(8,128)}) custom-call(f32[1,2048]{1,0:T(1,128)} %slice.208.refs_1_.refs_0_, f32[256,2048]{1,0:T(8,128)} %get-tuple-element.147.refs_1_, f32[256,2048]{1,0:T(8,128)} %get-tuple-element.148.refs_2_, ...), custom_call_target="tpu_custom_call" | custom-call | flops 99999997952 | bytes 200000000 | tf_op jit(solution)/shard_map/leave_ffn/pallas_call | solution.py:57
  557.9 26.1 %down_project.1 = (bf16[512,2048]{1,0:T(8,128)(2,1)}, bf16[512,2048]{1,0:T(8,128)(2,1)}, bf16[512,2048]{1,0:T(8,128)(2,1)}, bf16[512,2048]{1,0:T(8,128)(2,1)}) custom-call(bf16[2048,2048]{1,0:T(8,128)(2,1)} %get-tuple-element.162.refs_0_, bf16[2048,2048]{1,0:T(8,128)(2,1)} %all-gather.11.cloned.1.call-done.refs_2_.refs_1_, ...), custom_call_target="tpu_custom_call" | custom-call | flops 199999995904 | bytes 400000000 | tf_op jit(solution)/shard_map/down_project/pallas_call | solution.py:57
  594.7 15.9 %branch_back.1 = (bf16[2048,2048]{1,0:T(8,128)(2,1)}, f32[2048,512]{1,0:T(8,128)}, f32[8,2048]{1,0:T(8,128)}, f32[8,512]{1,0:T(8,128)}) custom-call(bf16[512,2048]{1,0:T(8,128)(2,1)} %all-gather.7.cloned.1.call-done.refs_3_.refs_0_, f32[2048,512]{1,0:T(8,128)} %get-tuple-element.133.refs_0_.refs_1_, f32[1,512]{1,0:T(1,128)} %get-tuple-element.255.refs_1_.refs_2_, ...), custom_call_target="tpu_custom_call" | custom-call | flops 149999992832 | bytes 300000000 | tf_op jit(solution)/shard_map/branch_back/pallas_call | solution.py:57
  635.2 32.8 %attention_backward.2.refs_4_.refs_3_ = bf16[2048,768]{1,0:T(8,128)(2,1)} custom-call(s32[8]{0:T(128)} %fusion.19.refs_0_, s32[8]{0:T(128)} %get-tuple-element.277.refs_1_, s32[8]{0:T(128)} %get-tuple-element.278.refs_2_, bf16[2048,512]{1,0:T(8,128)(2,1)} %get-tuple-element.124.refs_3_, bf16[2048,512]{1,0:T(8,128)(2,1)} %get-tuple-element.125.refs_4_, ...), custom_call_target="tpu_custom_call" | custom-call | flops 199999995904 | bytes 400000000 | tf_op jit(solution)/shard_map/attention_backward/pallas_call | solution.py:57
  671.3 28.5 %reduce-scatter.8.cloned.1.call-done.refs_18_ = bf16[256,2048]{1,0:T(8,128)(2,1)} async-done(((bf16[2048,2048]{1,0:T(8,128)(2,1)}), bf16[256,2048]{1,0:T(8,128)(2,1)}) %reduce-scatter.8.cloned.1.call-update) | async-done | bytes 1048592 | tf_op jit(solution)/shard_map/reduce_scatter | solution.py:972
  723.1 12.5 %reduce-scatter.10.cloned.1.call-done.refs_19_ = bf16[64,2048]{1,0:T(8,128)(2,1)} async-done(((bf16[512,2048]{1,0:T(8,128)(2,1)}), bf16[64,2048]{1,0:T(8,128)(2,1)}) %reduce-scatter.10.cloned.1.call-update) | async-done | bytes 262160 | tf_op jit(solution)/shard_map/reduce_scatter | solution.py:1013
  742.1 32.5 %attention_backward.3.refs_4_ = bf16[2048,768]{1,0:T(8,128)(2,1)} custom-call(s32[8]{0:T(128)} %fusion.19.refs_0_, s32[8]{0:T(128)} %get-tuple-element.277.refs_1_, s32[8]{0:T(128)} %get-tuple-element.278.refs_2_, bf16[2048,512]{1,0:T(8,128)(2,1)} %get-tuple-element.124.refs_3_, bf16[2048,512]{1,0:T(8,128)(2,1)} %get-tuple-element.125.refs_4_, ...), custom_call_target="tpu_custom_call" | custom-call | flops 199999995904 | bytes 400000000 | tf_op jit(solution)/shard_map/attention_backward/pallas_call | solution.py:57
  774.6 27.7 %input_back.1 = (f32[8,1536]{1,0:T(8,128)}, f32[8,2048]{1,0:T(8,128)}, bf16[512,2048]{1,0:T(8,128)(2,1)}, bf16[512,2048]{1,0:T(8,128)(2,1)}, bf16[512,2048]{1,0:T(8,128)(2,1)}, /*index=5*/bf16[512,2048]{1,0:T(8,128)(2,1)}) custom-call(bf16[2048,1536]{1,0:T(8,128)(2,1)} %all-gather.5.cloned.1.call-done.refs_1_.refs_0_, ...), custom_call_target="tpu_custom_call" | custom-call | flops 112000000000 | bytes 224000000 | tf_op jit(solution)/shard_map/input_back/pallas_call | solution.py:57
  802.3 18.0 %collective-permute-start.63 = (bf16[512,2048]{1,0:T(8,128)(2,1)}, bf16[512,2048]{1,0:T(8,128)(2,1)S(1)}, u32[]{:S(2)}, u32[]{:S(2)}) collective-permute-start(bf16[512,2048]{1,0:T(8,128)(2,1)} %get-tuple-element.197), channel_id=1, source_target_pairs={{0,2},{1,3},{2,0},{3,1},{4,6},{5,7},{6,4},{7,5},{8,10},{9,11},{10,... | collective-permute-start | bytes 6291464 | tf_op jit(solution)/shard_map/ppermute | solution.py:765
  854.4 30.5 %collective-permute-start.76 = (f32[4,1472]{1,0:T(4,128)S(1)}, f32[4,1472]{1,0:T(4,128)S(1)}, u32[]{:S(2)}, u32[]{:S(2)}) collective-permute-start(f32[4,1472]{1,0:T(4,128)S(1)} %slice.288), channel_id=1, source_target_pairs={{0,4},{4,0},{8,12},{12,8},{16,20},{20,16},{24,28},{28,24},{1,5},{5... | collective-permute-start | bytes 70664 | tf_op jit(solution)/shard_map/ppermute | solution.py:851
  (488 shorter events, 318.8 us)
Async XLA Ops:
  7.2 124.2 %all-gather.5.cloned.1.call-start = ((), (), s32[]{:S(2)}) async-start(), calls=%async_computation.5 | async-start | bytes 7077888 | tf_op jit(solution)/shard_map/all_gather | solution.py:916
  17.1 43.3 %collective-permute-start.11 = (bf16[256,2048]{1,0:T(8,128)(2,1)}, bf16[256,2048]{1,0:T(8,128)(2,1)}, u32[]{:S(2)}, u32[]{:S(2)}) collective-permute-start(bf16[256,2048]{1,0:T(8,128)(2,1)} %get-tuple-element.112.refs_2_.refs_3_.refs_1_), channel_id=1, source_target_pairs={{0,1},{1,0},{2,3},{3,2},{4,5},{5,4},{6,7},{7,6},{8,9},{9,8},{10,11... | collective-permute-start | bytes 3145736 | tf_op jit(solution)/shard_map/ppermute | solution.py:765
  18.5 41.9 %collective-permute-start.12 = (bf16[256,2048]{1,0:T(8,128)(2,1)S(1)}, bf16[256,2048]{1,0:T(8,128)(2,1)}, u32[]{:S(2)}, u32[]{:S(2)}) collective-permute-start(bf16[256,2048]{1,0:T(8,128)(2,1)S(1)} %get-tuple-element.114.refs_6_.refs_4_.refs_2_), channel_id=1, source_target_pairs={{0,2},{1,3},{2,0},{3,1},{4,6},{5,7},{6,4},{7,5},{8,10},{9,11},{10,... | collective-permute-start | bytes 3145736 | tf_op jit(solution)/shard_map/ppermute | solution.py:765
  61.5 142.4 %all-gather.7.cloned.1.call-start = ((), (), s32[]{:S(2)}) async-start(), calls=%async_computation.6 | async-start | bytes 2359296 | tf_op jit(solution)/shard_map/all_gather | solution.py:929
  62.3 249.4 %all-gather.11.cloned.1.call-start = ((), (), s32[]{:S(2)}) async-start(), calls=%async_computation.8 | async-start | bytes 9437184 | tf_op jit(solution)/shard_map/all_gather | solution.py:930
  63.0 292.1 %all-gather.9.cloned.1.call-start = ((), (), s32[]{:S(2)}) async-start(), calls=%async_computation.7 | async-start | bytes 9437184 | tf_op jit(solution)/shard_map/all_gather | solution.py:937
  68.8 44.9 %collective-permute-start.14 = (bf16[256,2048]{1,0:T(8,128)(2,1)}, bf16[256,2048]{1,0:T(8,128)(2,1)}, u32[]{:S(2)}, u32[]{:S(2)}) collective-permute-start(bf16[256,2048]{1,0:T(8,128)(2,1)} %collective-permute-done.11.refs_3_), channel_id=1, source_target_pairs={{0,2},{1,3},{2,0},{3,1},{4,6},{5,7},{6,4},{7,5},{8,10},{9,11},{10,... | collective-permute-start | bytes 3145736 | tf_op jit(solution)/shard_map/ppermute | solution.py:765
  68.8 44.8 %collective-permute-start.15 = (bf16[256,2048]{1,0:T(8,128)(2,1)S(1)}, bf16[256,2048]{1,0:T(8,128)(2,1)}, u32[]{:S(2)}, u32[]{:S(2)}) collective-permute-start(bf16[256,2048]{1,0:T(8,128)(2,1)S(1)} %get-tuple-element.114.refs_6_.refs_4_.refs_2_), channel_id=1, source_target_pairs={{0,1},{1,0},{2,3},{3,2},{4,5},{5,4},{6,7},{7,6},{8,9},{9,8},{10,11... | collective-permute-start | bytes 3145736 | tf_op jit(solution)/shard_map/ppermute | solution.py:765
  70.8 42.9 %collective-permute-start.16 = (bf16[256,2048]{1,0:T(8,128)(2,1)}, bf16[256,2048]{1,0:T(8,128)(2,1)}, u32[]{:S(2)}, u32[]{:S(2)}) collective-permute-start(bf16[256,2048]{1,0:T(8,128)(2,1)} %collective-permute-done.12.refs_7_), channel_id=1, source_target_pairs={{0,1},{1,0},{2,3},{3,2},{4,5},{5,4},{6,7},{7,6},{8,9},{9,8},{10,11... | collective-permute-start | bytes 3145736 | tf_op jit(solution)/shard_map/ppermute | solution.py:765
  153.4 481.7 %reduce-scatter.6.cloned.1.call-start = ((), (), s32[]{:S(2)}) async-start(), calls=%async_computation.9 | async-start | bytes 9437184 | tf_op jit(solution)/shard_map/reduce_scatter | solution.py:968
  156.2 41.7 %collective-permute-start.20 = (bf16[256,2048]{1,0:T(8,128)(2,1)}, bf16[256,2048]{1,0:T(8,128)(2,1)}, u32[]{:S(2)}, u32[]{:S(2)}) collective-permute-start(bf16[256,2048]{1,0:T(8,128)(2,1)} %collective-permute-done.17.refs_8_.refs_9_), channel_id=1, source_target_pairs={{0,2},{1,3},{2,0},{3,1},{4,6},{5,7},{6,4},{7,5},{8,10},{9,11},{10,... | collective-permute-start | bytes 3145736 | tf_op jit(solution)/shard_map/ppermute | solution.py:765
  156.5 41.4 %collective-permute-start.21 = (bf16[256,2048]{1,0:T(8,128)(2,1)S(1)}, bf16[256,2048]{1,0:T(8,128)(2,1)S(1)}, u32[]{:S(2)}, u32[]{:S(2)}) collective-permute-start(bf16[256,2048]{1,0:T(8,128)(2,1)S(1)} %get-tuple-element.138.refs_12_.refs_4_), channel_id=1, source_target_pairs={{0,1},{1,0},{2,3},{3,2},{4,5},{5,4},{6,7},{7,6},{8,9},{9,8},{10,11... | collective-permute-start | bytes 3145736 | tf_op jit(solution)/shard_map/ppermute | solution.py:765
  309.8 45.4 %collective-permute-start.35 = (bf16[256,2048]{1,0:T(8,128)(2,1)S(1)}, bf16[256,2048]{1,0:T(8,128)(2,1)}, u32[]{:S(2)}, u32[]{:S(2)}) collective-permute-start(bf16[256,2048]{1,0:T(8,128)(2,1)S(1)} %collective-permute-done.33.refs_6_), channel_id=1, source_target_pairs={{0,2},{1,3},{2,0},{3,1},{4,6},{5,7},{6,4},{7,5},{8,10},{9,11},{10,... | collective-permute-start | bytes 3145736 | tf_op jit(solution)/shard_map/ppermute | solution.py:765
  310.3 44.8 %collective-permute-start.38 = (bf16[256,2048]{1,0:T(8,128)(2,1)S(1)}, bf16[256,2048]{1,0:T(8,128)(2,1)}, u32[]{:S(2)}, u32[]{:S(2)}) collective-permute-start(bf16[256,2048]{1,0:T(8,128)(2,1)S(1)} %collective-permute-done.36.refs_10_), channel_id=1, source_target_pairs={{0,1},{1,0},{2,3},{3,2},{4,5},{5,4},{6,7},{7,6},{8,9},{9,8},{10,11... | collective-permute-start | bytes 3145736 | tf_op jit(solution)/shard_map/ppermute | solution.py:765
  498.1 201.7 %reduce-scatter.8.cloned.1.call-start = ((), (), s32[]{:S(2)}) async-start(), calls=%async_computation.10 | async-start | bytes 9437184 | tf_op jit(solution)/shard_map/reduce_scatter | solution.py:972
  545.3 190.4 %reduce-scatter.10.cloned.1.call-start = ((), (), s32[]{:S(2)}) async-start(), calls=%async_computation.11 | async-start | bytes 2359296 | tf_op jit(solution)/shard_map/reduce_scatter | solution.py:1013
  613.3 54.6 %collective-permute-start.52 = (bf16[512,2048]{1,0:T(8,128)(2,1)}, bf16[512,2048]{1,0:T(8,128)(2,1)}, u32[]{:S(2)}, u32[]{:S(2)}) collective-permute-start(bf16[512,2048]{1,0:T(8,128)(2,1)} %get-tuple-element.179.refs_16_), channel_id=1, source_target_pairs={{0,2},{1,3},{2,0},{3,1},{4,6},{5,7},{6,4},{7,5},{8,10},{9,11},{10,... | collective-permute-start | bytes 6291464 | tf_op jit(solution)/shard_map/ppermute | solution.py:765
  613.3 54.6 %collective-permute-start.53 = (bf16[512,2048]{1,0:T(8,128)(2,1)}, bf16[512,2048]{1,0:T(8,128)(2,1)}, u32[]{:S(2)}, u32[]{:S(2)}) collective-permute-start(bf16[512,2048]{1,0:T(8,128)(2,1)} %get-tuple-element.181.refs_18_), channel_id=1, source_target_pairs={{0,1},{1,0},{2,3},{3,2},{4,5},{5,4},{6,7},{7,6},{8,9},{9,8},{10,11... | collective-permute-start | bytes 6291464 | tf_op jit(solution)/shard_map/ppermute | solution.py:765
  635.1 212.7 %reduce-scatter.12.cloned.1.call-start = ((), (), s32[]{:S(2)}) async-start(), calls=%async_computation.12 | async-start | bytes 3538944 | tf_op jit(solution)/shard_map/reduce_scatter | solution.py:1011
  714.8 59.7 %collective-permute-start.57 = (bf16[256,2048]{1,0:T(8,128)(2,1)}, bf16[256,2048]{1,0:T(8,128)(2,1)}, u32[]{:S(2)}, u32[]{:S(2)}) collective-permute-start(bf16[256,2048]{1,0:T(8,128)(2,1)} %get-tuple-element.189.refs_20_), channel_id=1, source_target_pairs={{0,1},{1,0},{2,3},{3,2},{4,5},{5,4},{6,7},{7,6},{8,9},{9,8},{10,11... | collective-permute-start | bytes 3145736 | tf_op jit(solution)/shard_map/ppermute | solution.py:765
  716.0 58.6 %collective-permute-start.58 = (bf16[256,2048]{1,0:T(8,128)(2,1)}, bf16[256,2048]{1,0:T(8,128)(2,1)}, u32[]{:S(2)}, u32[]{:S(2)}) collective-permute-start(bf16[256,2048]{1,0:T(8,128)(2,1)} %get-tuple-element.190.refs_21_), channel_id=1, source_target_pairs={{0,2},{1,3},{2,0},{3,1},{4,6},{5,7},{6,4},{7,5},{8,10},{9,11},{10,... | collective-permute-start | bytes 3145736 | tf_op jit(solution)/shard_map/ppermute | solution.py:765
  717.2 186.9 %reduce-scatter.14.cloned.1.call-start = ((), (), s32[]{:S(2)}) async-start(), calls=%async_computation.13 | async-start | bytes 3538944 | tf_op jit(solution)/shard_map/reduce_scatter | solution.py:1037
  802.3 45.5 %collective-permute-start.63 = (bf16[512,2048]{1,0:T(8,128)(2,1)}, bf16[512,2048]{1,0:T(8,128)(2,1)S(1)}, u32[]{:S(2)}, u32[]{:S(2)}) collective-permute-start(bf16[512,2048]{1,0:T(8,128)(2,1)} %get-tuple-element.197), channel_id=1, source_target_pairs={{0,2},{1,3},{2,0},{3,1},{4,6},{5,7},{6,4},{7,5},{8,10},{9,11},{10,... | collective-permute-start | bytes 6291464 | tf_op jit(solution)/shard_map/ppermute | solution.py:765
  852.8 42.0 %collective-permute-start.65 = (bf16[256,2048]{1,0:T(8,128)(2,1)}, bf16[256,2048]{1,0:T(8,128)(2,1)S(1)}, u32[]{:S(2)}, u32[]{:S(2)}) collective-permute-start(bf16[256,2048]{1,0:T(8,128)(2,1)} %get-tuple-element.200), channel_id=1, source_target_pairs={{0,1},{1,0},{2,3},{3,2},{4,5},{5,4},{6,7},{7,6},{8,9},{9,8},{10,11... | collective-permute-start | bytes 3145736 | tf_op jit(solution)/shard_map/ppermute | solution.py:765
  (134 other events, 2305.8 us)
Sparse Core Ops, SparseCore 0:
  61.7 69.6 all-gather.4
  133.5 27.7 all-gather.6
  162.9 81.5 all-gather.10
  246.0 80.5 all-gather.8
  498.2 111.3 reduce-scatter.5
  611.8 87.9 reduce-scatter.7
  702.1 33.5 reduce-scatter.9
  737.9 51.6 reduce-scatter.11
  835.7 55.9 reduce-scatter.13

commit v3 on v2

--- a/solution.py
+++ b/solution.py
@@ -35,7 +35,8 @@
     "out_project": 14,
     "down_project": 200,
     "add_rows": 30,
-    "ffn_up": 54,
+    "ffn_grad": 24,
+    "ffn_up": 33,
     "ffn_mid": 47,
     "branch_back": 150,
     "attn_grad": 38.0,
@@ -412,51 +413,101 @@
 GELU_C = 0.7978845608028654
 
 
-def ffn_up(pieces, cot, w_up, w_down, bias, gain, after=()):
+def ffn_grad(cot, w_down, gain):
     rows, wide = cot.shape
+    units = w_down.shape[0]
+    chunk = min(512, units)
+
+    def body(c_ref, d_w, g_ref, grad_ref, stat_ref, sum_ref):
+        @pl.when(pl.program_id(0) == 0)
+        def _():
+            sum_ref[...] = jnp.zeros_like(sum_ref)
+
+        total = 0.0
+        for at in range(0, units, chunk):
+            span = slice(at, at + chunk)
+            grad = nt(c_ref[...], d_w[span, :])
+            scaled = grad * g_ref[:, span]
+            grad_ref[:, span] = scaled
+            sum_ref[0:1, span] += jnp.sum(grad, axis=0, keepdims=True)
+            total = total + jnp.sum(scaled, axis=1, keepdims=True)
+        lane = lax.broadcasted_iota(jnp.int32, (BLK, 128), 1)
+        stat_ref[...] = jnp.where(lane == 0, total, 0.0).T[0:8, :]
+
+    return launch(
+        body,
+        (rows // BLK,),
+        [(cot, tile(BLK, wide)), fixed(w_down), fixed(gain)],
+        [
+            ((rows, units), jnp.float32, tile(BLK, units)),
+            ((8, rows), jnp.float32, pl.BlockSpec((8, BLK), lambda i, *_: (0, i))),
+            ((8, units), jnp.float32, pl.BlockSpec((8, units), lambda i, *_: (0, 0))),
+        ],
+        name="ffn_grad",
+    )
+
+
+def ffn_up(pieces, grad, grad_sums, w_up, bias):
+    rows, units = grad.shape
+    wide = w_up.shape[0]
     inputs, read = arrivals(pieces, wide)
-    units = w_up.shape[1]
     chunk = min(512, units)
-
-    def body(c_ref, u_w, d_w, b_ref, g_ref, *rest):
-        m_ref, up_ref, grad_ref, stat_ref, gel_ref = rest[len(pieces) :]
+    share = 1.0 / chunk
+
+    def body(f_ref, t_ref, u_w, b_ref, *rest):
+        m_ref, up_ref, stat_ref = rest[len(pieces) :]
         read(rest[: len(pieces)], m_ref)
-        total = scaled_total = 0.0
+        parts = []
+
+        def figures(at, up):
+            span = slice(at, at + chunk)
+            gel = 0.5 * up * (1.0 + jnp.tanh(GELU_C * up * (1.0 + GELU_A * up * up)))
+            center = jnp.sum(gel, axis=1, keepdims=True) * share
+            spread = gel - center
+            scaled = f_ref[:, span]
+            parts.append(
+                (
+                    center,
+                    jnp.sum(spread * spread, axis=1, keepdims=True),
+                    jnp.sum(scaled * spread, axis=1, keepdims=True),
+                    jnp.sum(scaled, axis=1, keepdims=True),
+                )
+            )
+
+        last = None
         for at in range(0, units, chunk):
             span = slice(at, at + chunk)
             up = nn(m_ref[...], u_w[:, span]) + b_ref[:, span]
-            grad = nt(c_ref[...], d_w[span, :])
             up_ref[:, span] = up
-            grad_ref[:, span] = grad
-            gel = 0.5 * up * (1.0 + jnp.tanh(GELU_C * (up + GELU_A * up * up * up)))
-            gel_ref[:, span] = gel
-            total = total + jnp.sum(gel, axis=1, keepdims=True)
-            scaled_total = scaled_total + jnp.sum(grad * g_ref[:, span], axis=1, keepdims=True)
-        center = total * (1.0 / units)
-        square = product = 0.0
-        for at in range(0, units, chunk):
-            span = slice(at, at + chunk)
-            spread = gel_ref[:, span] - center
-            square = square + jnp.sum(spread * spread, axis=1, keepdims=True)
-            product = product + jnp.sum(grad_ref[:, span] * g_ref[:, span] * spread, axis=1, keepdims=True)
+            if last is not None:
+                figures(*last)
+            last = at, up
+        figures(*last)
+        center = sum(p[0] for p in parts) * (1.0 / len(parts))
+        square = sum(p[1] + chunk * (p[0] - center) ** 2 for p in parts)
+        product = sum(p[2] + (p[0] - center) * p[3] for p in parts)
         lane = lax.broadcasted_iota(jnp.int32, (BLK, 128), 1)
         flat = jnp.zeros((BLK, 128), jnp.float32)
-        for i, value in enumerate((center, square, scaled_total, product)):
+        for i, value in enumerate((center, square, product)):
             flat = jnp.where(lane == i, value, flat)
-        stat_ref[...] = flat.T[0:8, :]
+        flat = flat.T
+        stat_ref[...] = jnp.concatenate([flat[0:2], t_ref[0:1, :], flat[2:7]], axis=0)
 
     return launch(
         body,
         (rows // BLK,),
-        [(cot, tile(BLK, wide)), fixed(w_up), fixed(w_down), fixed(bias), fixed(gain)] + inputs,
+        [
+            (grad, tile(BLK, units)),
+            (grad_sums, pl.BlockSpec((8, BLK), lambda i, *_: (0, i))),
+            fixed(w_up),
+            fixed(bias),
+        ]
+        + inputs,
         [
             ((rows, wide), jnp.bfloat16, tile(BLK, wide)),
             ((rows, units), jnp.float32, tile(BLK, units)),
-            ((rows, units), jnp.float32, tile(BLK, units)),
             ((8, rows), jnp.float32, pl.BlockSpec((8, BLK), lambda i, *_: (0, i))),
         ],
-        scratch=[pltpu.VMEM((BLK, units), jnp.float32)],
-        after=after,
         name="ffn_up",
     )
 
@@ -490,12 +541,11 @@
             slope = one + 0.5 * u * (1.0 - t * t) * (GELU_C * (1.0 + 3.0 * GELU_A * squared))
             normed = (u * one - center) * inverse
             low_ref[:, span] = (normed * g_ref[:, span] + s_ref[:, span]).astype(jnp.bfloat16)
-            lower = inverse * (f * g_ref[:, span] - first - normed * second)
+            lower = inverse * (f - first - normed * second)
             gup = (lower * slope).astype(jnp.bfloat16)
             gup_ref[:, span] = gup
             sum_ref[0:1, span] += jnp.sum(f * normed, axis=0, keepdims=True)
-            sum_ref[1:2, span] += jnp.sum(f, axis=0, keepdims=True)
-            sum_ref[2:3, span] += jnp.sum(gup.astype(jnp.float32), axis=0, keepdims=True)
+            sum_ref[1:2, span] += jnp.sum(gup.astype(jnp.float32), axis=0, keepdims=True)
         write(part_refs, nt(gup_ref[...], w_ref[...]).astype(jnp.bfloat16))
 
     low, gup, sums, *parts = launch(
@@ -627,16 +677,30 @@
                 at = pl.ds(pl.multiple_of(slots[qb] * BLK, BLK), BLK)
                 here = pl.ds(pl.multiple_of(qb * BLK, BLK), BLK)
                 seen = (spot >= lo_ref[0:1, here]) & (spot <= hi_ref[0:1, here])
-                for h in range(heads):
+                def products(h):
+                    two = slice(h // 2 * 128, h // 2 * 128 + 128)
+                    return nn(ks[h], qt[two, at]), nn(vs[h], gt[two, at])
+
+                def factors(h, s, dp):
+                    p = jnp.where(seen, jnp.exp(s - lse_ref[base + h : base + h + 1, at]), 0.0)
+                    ds = (p * (dp - dot_ref[base + h : base + h + 1, at])).astype(jnp.bfloat16)
+                    return p.astype(jnp.bfloat16), ds
+
+                def add(h, p, ds):
                     two = slice(h // 2 * 128, h // 2 * 128 + 128)
                     span = slice(h * HEAD_DIM, (h + 1) * HEAD_DIM)
-                    s = nn(ks[h], qt[two, at])
-                    p = jnp.where(seen, jnp.exp(s - lse_ref[base + h : base + h + 1, at]), 0.0)
-                    dp = nn(vs[h], gt[two, at])
-                    ds = (p * (dp - dot_ref[base + h : base + h + 1, at])).astype(jnp.bfloat16)
-                    accs[1, h] += nn(p.astype(jnp.bfloat16), g_ref[at, two])
+                    accs[1, h] += nn(p, g_ref[at, two])
                     accs[0, h] += nn(ds, q_ref[at, two])
                     dqt[span, at] += nn(kts[span, :], ds)
+
+                made, ready = {}, {}
+                for h in range(heads + 2):
+                    if h < heads:
+                        made[h] = products(h)
+                    if 0 <= h - 1 < heads:
+                        ready[h - 1] = factors(h - 1, *made[h - 1])
+                    if 0 <= h - 2 < heads:
+                        add(h - 2, *ready[h - 2])
                 return 0
 
             lax.fori_loop(first[kb], last[kb], inner, 0)
@@ -903,6 +967,7 @@
     small = jnp.concatenate(
         [bias_qkv.reshape(-1), gains_d.reshape(-1), biases_d.reshape(-1), gain_ff, biases_ff.reshape(-1)]
     )
+
     small = share_small(small, batches, ranks)
 
     w_qkv, _ = lax.optimization_barrier((w_qkv, x_own))
@@ -961,9 +1026,11 @@
         name="enter_ffn",
     )
     mid_pieces = move.gather(mid_upper, mid_lower)
-    mid_low, up_proj, grad_ffn, stat = ffn_up(mid_pieces, cot_full, full_up, full_down, shift_up, gain_ffn)
+    (cot_here, *_) = lax.optimization_barrier((cot_full, mid_upper))
+    scaled_grad, grad_sums, shift_sums = ffn_grad(cot_here, full_down, gain_ffn)
+    mid_low, up_proj, stat = ffn_up(mid_pieces, scaled_grad, grad_sums, full_up, shift_up)
     stats4 = move.spread(stat)
-    ffn_low, grad_up, sums_ff, parts = ffn_mid(up_proj, grad_ffn, stats4, gain_ffn, shift_ffn, full_up, move.groups)
+    ffn_low, grad_up, sums_ff, parts = ffn_mid(up_proj, scaled_grad, stats4, gain_ffn, shift_ffn, full_up, move.groups)
     g_down = tn(ffn_low, cot_full).astype(bf16)
     sum_down = lax.psum_scatter(g_down, "batch", scatter_dimension=0, tiled=True)
     arriving = move.scatter(parts, (g_down,))
@@ -1011,16 +1078,14 @@
     sum_first = lax.psum_scatter(g_first, "batch", scatter_dimension=0, tiled=True)
     g_out, _ = lax.optimization_barrier((g_out, sum_down))
     sum_out = lax.psum_scatter(g_out, "batch", scatter_dimension=0, tiled=True)
-    grad_second = back(1, (g_first, sum_up, sum_out, *forwarded))
-    up_rows = move.sent(move.picked(sum_up.reshape(ranks, d_rows, batches, strip), 0))
-    out_rows = lax.ppermute(sum_out, EVERY, [(b, a) for a, b in order])
+    grad_second = back(1, (g_first, sum_up, *forwarded))
     bias_sums, sums_in, parts = input_back(
         (grad_first, grad_second),
         full_qkv,
         x_full,
         row_stats,
         move.groups,
-        after=[terms[-1][0] for terms in arriving] + up_rows + [out_rows],
+        after=[terms[-1][0] for terms in arriving],
     )
 
     def finish(vectors, values, arrived):
@@ -1029,12 +1094,17 @@
     result = own_rows(
         finish, [shift_down], [resid], arriving, [(bf16, True)], after=(parts[0],), name="finish"
     )[0]
+    sum_up, _ = lax.optimization_barrier((sum_up, parts))
+    up_rows = move.sent(move.picked(sum_up.reshape(ranks, d_rows, batches, strip), 0))
+    arriving = move.scatter(parts, (sum_first, sum_out, result, *up_rows))
     out_up = jnp.moveaxis(move.ordered(up_rows), 0, 2).reshape(d_rows, batches * ranks * strip).astype(f32)
-    first_rows = move.sent(move.picked(sum_first.reshape(ranks, d_rows, 3, cols // 2), 0))
-    arriving = move.scatter(parts, (sum_first, result, out_up))
     grad_second, _ = lax.optimization_barrier((grad_second, parts))
     g_second = tn(input_low, grad_second).astype(bf16)
     sum_second = lax.psum_scatter(g_second, "batch", scatter_dimension=0, tiled=True)
+    sums_qkv = jnp.stack([s.reshape(ranks, d_rows, 3, cols // 2) for s in (sum_first, sum_second)], axis=3)
+    qkv_rows = move.sent(move.picked(sums_qkv.reshape(ranks, d_rows, 3, cols), 0))
+    sum_out, _ = lax.optimization_barrier((sum_out, sums_qkv))
+    out_rows = lax.ppermute(sum_out, EVERY, [(b, a) for a, b in order])
 
     def end(vectors, values, arrived):
         normed, inverse = norm_parts(values[0].astype(f32))
@@ -1055,7 +1125,7 @@
             sums_mid[1:4],
         ]
     )
-    vector_f = sums_ff[:3].reshape(3, batches, 1, strip)
+    vector_f = jnp.concatenate([sums_ff[:1] / gain_ffn, shift_sums[:1], sums_ff[1:2]]).reshape(3, batches, 1, strip)
     vector_f = lax.dynamic_update_slice(jnp.zeros((3, batches, ranks, strip), f32), vector_f, (0, 0, me, 0))
     vector = jnp.concatenate(
         [
@@ -1064,17 +1134,13 @@
         ],
         axis=1,
     )
-    vector = sum_small(vector, batches, ranks, [terms[-1][0] for terms in arriving])
-    second_rows = move.picked(sum_second.reshape(ranks, d_rows, 3, cols // 2), 0)
-    grad_total = own_rows(
-        end, [gain_in], [x_own, grad_resid], arriving, [(f32, True)], after=second_rows, name="end"
-    )[0]
-
-    second_rows = move.sent(second_rows)
-    halves = [jnp.moveaxis(move.ordered(r), 0, 2) for r in (first_rows, second_rows)]
-    out_qkv = jnp.stack(halves, axis=3).reshape(d_rows, 3 * D).astype(f32)
+    vector = sum_small(vector, batches, ranks, [terms[-1][0] for terms in arriving] + qkv_rows)
+    out_qkv = jnp.moveaxis(move.ordered(qkv_rows), 0, 2).reshape(d_rows, 3 * D).astype(f32)
     out_out = out_rows.astype(f32)
     out_down = sum_down.astype(f32)
+    grad_total = own_rows(
+        end, [gain_in], [x_own, grad_resid], arriving, [(f32, True)], after=(out_qkv, out_up), name="end"
+    )[0]
     own_d = vector[:cut].reshape(11, d_rows)
     own_f = vector[cut:].reshape(3, strip)
     return (

time: 944 us -> 885 us (0.938)
  waiting for transfers between devices: 236 us -> 184 us
  Pallas kernels: 363 us -> 383 us
  starting transfers between devices: 132 us -> 121 us
    ppermute x64 -> x61, waiting for transfers between devices: 186 us -> 154 us  [swap(): return lax.ppermute(value, 'seq', [(r, r ^ bit) for r in range(self.ranks)])]
    ppermute x64 -> x61, starting transfers between devices: 71.2 us -> 50.5 us  [swap(): return lax.ppermute(value, 'seq', [(r, r ^ bit) for r in range(self.ranks)])]
    pallas_call x20 -> x21, Pallas kernels: 363 us -> 383 us  [launch(): pl.pallas_call(kernel, out_shape=tuple((jax.ShapeDtypeStruct(s, d) for s,...]
    reduce_scatter x1, waiting for transfers between devices: 28.5 us -> 12.3 us  [local(): sum_up = lax.psum_scatter(g_up, 'batch', scatter_dimension=0, tiled=True)]
    reduce_scatter x1, waiting for transfers between devices: 12.5 us -> 0.02 us  [local(): sum_out = lax.psum_scatter(g_out, 'batch', scatter_dimension=0, tiled=True)]
    ppermute x7, starting transfers between devices: 38.4 us -> 49 us  [sum_small(): lax.ppermute(value[at:at + left], axis, [(r, r ^ s) for r in range(count)])]
    unnamed x154 -> x127, local copies, waits for them, and re-layouts: 25.8 us -> 23.7 us
  transfers between devices with their start and end apart: 89 -> 86, of which waited for: 34 -> 30; matrix products, arithmetic and copies ran while one was open for 17% -> 18% of each run, Pallas kernels for 28% -> 34%
where the time goes in v3:
time: 885 us; the launch traced here: 876 us
  Pallas kernels  383 us (43%)
  waiting for transfers between devices  184 us (21%)
  starting transfers between devices  121 us (14%)
  matrix products  79.7 us (9%)
  local copies, waits for them, and re-layouts  73.1 us (8%)
  other arithmetic  19.4 us (2%)
  between operations  16.3 us (2%)
    pallas_call x21, Pallas kernels, launch(): pl.pallas_call(kernel, out_shape=tuple((jax.ShapeDtypeStruct(s, d) for s,...  383 us
    ppermute x61, waiting for transfers between devices, swap(): return lax.ppermute(value, 'seq', [(r, r ^ bit) for r in range(self.ranks)])  154 us
    dot_general x5, matrix products, tn(): lax.dot_general(a, b, (((0,), (0,)), ((), ())), preferred_element_type=jn...  79.7 us
    ppermute x61, starting transfers between devices, swap(): return lax.ppermute(value, 'seq', [(r, r ^ bit) for r in range(self.ranks)])  50.5 us
    ppermute x7, starting transfers between devices, sum_small(): lax.ppermute(value[at:at + left], axis, [(r, r ^ s) for r in range(count)])  49 us
    unnamed x127, local copies, waits for them, and re-layouts  23.7 us
  transfers between devices with their start and end apart: 86, of which 30 were waited for; matrix products, arithmetic and copies ran while one was open for 18% of the time, Pallas kernels for 34%

profile of v3, /device:TPU:1, one launch (start us, length us, event | category | flops | bytes accessed | tf_op | source)
XLA Modules:
  0.0 876.1 jit_solution(6474136713334024564)
XLA Ops:
  81.4 11.6 %collective-permute-done.13.refs_4_ = bf16[256,2048]{1,0:T(8,128)(2,1)} collective-permute-done((bf16[256,2048]{1,0:T(8,128)(2,1)}, bf16[256,2048]{1,0:T(8,128)(2,1)}, u32[]{:S(2)}, u32[]{:S(2)}) %collective-permute-start.13) | collective-permute-done | bytes 1048608 | tf_op jit(solution)/shard_map/ppermute | solution.py:829
  93.0 22.5 %collective-permute-done.14.refs_5_ = bf16[256,2048]{1,0:T(8,128)(2,1)} collective-permute-done((bf16[256,2048]{1,0:T(8,128)(2,1)}, bf16[256,2048]{1,0:T(8,128)(2,1)}, u32[]{:S(2)}, u32[]{:S(2)}) %collective-permute-start.14) | collective-permute-done | bytes 1048608 | tf_op jit(solution)/shard_map/ppermute | solution.py:829
  120.0 11.8 %enter_attention.1 = (bf16[2048,2048]{1,0:T(8,128)(2,1)}, bf16[2048,2048]{1,0:T(8,128)(2,1)}, f32[2048,128]{1,0:T(8,128)}) custom-call(f32[1,2048]{1,0:T(1,128)} %slice.220.refs_0_, f32[1,2048]{1,0:T(1,128)} %slice.222.refs_1_, bf16[256,2048]{1,0:T(8,128)(2,1)} %get-tuple-element.117.refs_2_.refs_3_.refs_1_, ...), custom_call_target="tpu_custom_call" | custom-call | flops 12000000000 | bytes 24000000 | tf_op jit(solution)/shard_map/enter_attention/pallas_call | solution.py:58
  132.0 19.0 %qkv_project.1 = (bf16[2048,512]{1,0:T(8,128)(2,1)}, bf16[2048,512]{1,0:T(8,128)(2,1)}, bf16[2048,512]{1,0:T(8,128)(2,1)}) custom-call(bf16[2048,2048]{1,0:T(8,128)(2,1)} %get-tuple-element.121.refs_0_, bf16[2048,1536]{1,0:T(8,128)(2,1)} %all-gather.5.cloned.1.call-done.refs_1_.refs_0_, f32[1,1536]{1,0:T(1,128)} %bitcast.199, ...), custom_call_target="tpu_custom_call" | custom-call | flops 19000000512 | bytes 38000000 | tf_op jit(solution)/shard_map/qkv_project/pallas_call | solution.py:58
  157.4 35.4 %attention_forward.1 = (f32[2048,512]{1,0:T(8,128)}, f32[8,2048]{1,0:T(8,128)}, f32[8,2048]{1,0:T(8,128)}) custom-call(s32[8]{0:T(128)} %fusion.18.refs_0_, s32[8]{0:T(128)} %get-tuple-element.287.refs_1_, s32[8]{0:T(128)} %get-tuple-element.288.refs_2_, bf16[2048,512]{1,0:T(8,128)(2,1)} %get-tuple-element.129.refs_3_, ...), custom_call_target="tpu_custom_call" | custom-call | flops 41000001536 | bytes 82000000 | tf_op jit(solution)/shard_map/attention_forward/pallas_call | solution.py:58
  203.1 14.7 %out_project.1 = (bf16[2048,512]{1,0:T(8,128)(2,1)}, bf16[512,2048]{1,0:T(8,128)(2,1)}, bf16[512,2048]{1,0:T(8,128)(2,1)}, bf16[512,2048]{1,0:T(8,128)(2,1)}, bf16[512,2048]{1,0:T(8,128)(2,1)}) custom-call(f32[2048,512]{1,0:T(8,128)} %get-tuple-element.138.refs_0_.refs_1_, f32[1,512]{1,0:T(1,128)} %get-tuple-element.263.refs_1_.refs_2_, ...), custom_call_target="tpu_custom_call" | custom-call | flops 14000000000 | bytes 28000000 | tf_op jit(solution)/shard_map/out_project/pallas_call | solution.py:58
  223.3 32.1 %collective-permute-done.26.refs_1_.refs_6_ = bf16[512,2048]{1,0:T(8,128)(2,1)S(1)} collective-permute-done((bf16[512,2048]{1,0:T(8,128)(2,1)}, bf16[512,2048]{1,0:T(8,128)(2,1)S(1)}, u32[]{:S(2)}, u32[]{:S(2)}) %collective-permute-start.26) | collective-permute-done | bytes 2097184 | tf_op jit(solution)/shard_map/ppermute | solution.py:829
  290.3 10.6 %collective-permute-done.33.refs_5_ = bf16[256,2048]{1,0:T(8,128)(2,1)S(1)} collective-permute-done((bf16[256,2048]{1,0:T(8,128)(2,1)}, bf16[256,2048]{1,0:T(8,128)(2,1)S(1)}, u32[]{:S(2)}, u32[]{:S(2)}) %collective-permute-start.33) | collective-permute-done | bytes 1048608 | tf_op jit(solution)/shard_map/ppermute | solution.py:829
  302.3 25.1 %ffn_grad.1 = (f32[2048,2048]{1,0:T(8,128)}, f32[8,2048]{1,0:T(8,128)}, f32[8,2048]{1,0:T(8,128)}) custom-call(bf16[2048,2048]{1,0:T(8,128)(2,1)} %constant_dynamic-update-slice_fusion.refs_11_.refs_0_, bf16[2048,2048]{1,0:T(8,128)(2,1)} %all-gather.9.cloned.1.call-done.refs_1_, f32[1,2048]{1,0:T(1,128)} %bitcast.194), custom_call_target="tpu_custom_call" | custom-call | flops 24000000000 | bytes 48000000 | tf_op jit(solution)/shard_map/ffn_grad/pallas_call | solution.py:58
  327.5 18.3 %collective-permute-done.35.refs_7_ = bf16[256,2048]{1,0:T(8,128)(2,1)} collective-permute-done((bf16[256,2048]{1,0:T(8,128)(2,1)S(1)}, bf16[256,2048]{1,0:T(8,128)(2,1)}, u32[]{:S(2)}, u32[]{:S(2)}) %collective-permute-start.35) | collective-permute-done | bytes 1048608 | tf_op jit(solution)/shard_map/ppermute | solution.py:829
  345.7 35.0 %ffn_up.1 = (bf16[2048,2048]{1,0:T(8,128)(2,1)}, f32[2048,2048]{1,0:T(8,128)}, f32[8,2048]{1,0:T(8,128)}) custom-call(f32[2048,2048]{1,0:T(8,128)} %get-tuple-element.156.refs_0_.refs_1_, f32[8,2048]{1,0:T(8,128)} %get-tuple-element.157.refs_1_, bf16[2048,2048]{1,0:T(8,128)(2,1)} %all-gather.11.cloned.1.call-done.refs_2_.refs_4_, f32[1,2048]{1,0:T(1,128)} %bitcast.198, ...), custom_call_target="tpu_custom_call" | custom-call | flops 32999999488 | bytes 66000000 | tf_op jit(solution)/shard_map/ffn_up/pallas_call | solution.py:58
  387.1 45.9 %ffn_mid.1 = (bf16[2048,2048]{1,0:T(8,128)(2,1)}, bf16[2048,2048]{1,0:T(8,128)(2,1)}, f32[8,2048]{1,0:T(8,128)}, bf16[512,2048]{1,0:T(8,128)(2,1)}, bf16[512,204...) custom-call(f32[2048,2048]{1,0:T(8,128)} %get-tuple-element.167.refs_0_, ...), custom_call_target="tpu_custom_call" | custom-call | flops 46999998464 | bytes 94000000 | tf_op jit(solution)/shard_map/ffn_mid/pallas_call | solution.py:58
  434.5 23.8 %convolution_convert_fusion.1.refs_4_ = bf16[2048,2048]{1,0:T(8,128)(2,1)} fusion(bf16[2048,2048]{1,0:T(8,128)(2,1)} %get-tuple-element.169.refs_0_, bf16[2048,2048]{1,0:T(8,128)(2,1)} %constant_dynamic-update-slice_fusion.refs_11_.refs_0_), kind=kOutput, calls=%fused_computation.1 | convolution fusion | flops 17184063488 | bytes 25165824 | tf_op jit(solution)/shard_map/dot_general | solution.py:24
  472.9 23.8 %convolution_convert_fusion.refs_11_ = bf16[2048,2048]{1,0:T(8,128)(2,1)} fusion(bf16[2048,2048]{1,0:T(8,128)(2,1)} %get-tuple-element.176, bf16[2048,2048]{1,0:T(8,128)(2,1)} %get-tuple-element.178), kind=kOutput, calls=%fused_computation | convolution fusion | flops 17184063488 | bytes 25165824 | tf_op jit(solution)/shard_map/dot_general | solution.py:24
  498.1 11.6 %leave_ffn.1 = (f32[256,2048]{1,0:T(8,128)}, f32[256,2048]{1,0:T(8,128)}, bf16[256,2048]{1,0:T(8,128)(2,1)}, bf16[256,2048]{1,0:T(8,128)(2,1)}, f32[8,2048]{1,0:T(8,128)}) custom-call(f32[1,2048]{1,0:T(1,128)} %slice.214.refs_1_.refs_0_, f32[256,2048]{1,0:T(8,128)} %get-tuple-element.152.refs_1_, f32[256,2048]{1,0:T(8,128)} %get-tuple-element.153.refs_2_, ...), custom_call_target="tpu_custom_call" | custom-call | flops 99999997952 | bytes 200000000 | tf_op jit(solution)/shard_map/leave_ffn/pallas_call | solution.py:58
  525.6 26.4 %down_project.1 = (bf16[512,2048]{1,0:T(8,128)(2,1)}, bf16[512,2048]{1,0:T(8,128)(2,1)}, bf16[512,2048]{1,0:T(8,128)(2,1)}, bf16[512,2048]{1,0:T(8,128)(2,1)}) custom-call(bf16[2048,2048]{1,0:T(8,128)(2,1)} %get-tuple-element.169.refs_0_, bf16[2048,2048]{1,0:T(8,128)(2,1)} %all-gather.9.cloned.1.call-done.refs_1_, ...), custom_call_target="tpu_custom_call" | custom-call | flops 199999995904 | bytes 400000000 | tf_op jit(solution)/shard_map/down_project/pallas_call | solution.py:58
  558.2 15.9 %branch_back.1 = (bf16[2048,2048]{1,0:T(8,128)(2,1)}, f32[2048,512]{1,0:T(8,128)}, f32[8,2048]{1,0:T(8,128)}, f32[8,512]{1,0:T(8,128)}) custom-call(bf16[512,2048]{1,0:T(8,128)(2,1)} %all-gather.7.cloned.1.call-done.refs_3_.refs_0_, f32[2048,512]{1,0:T(8,128)} %get-tuple-element.138.refs_0_.refs_1_, f32[1,512]{1,0:T(1,128)} %get-tuple-element.263.refs_1_.refs_2_, ...), custom_call_target="tpu_custom_call" | custom-call | flops 149999992832 | bytes 300000000 | tf_op jit(solution)/shard_map/branch_back/pallas_call | solution.py:58
  598.4 35.2 %attention_backward.2.refs_4_.refs_3_ = bf16[2048,768]{1,0:T(8,128)(2,1)} custom-call(s32[8]{0:T(128)} %fusion.18.refs_0_, s32[8]{0:T(128)} %get-tuple-element.285.refs_1_, s32[8]{0:T(128)} %get-tuple-element.286.refs_2_, bf16[2048,512]{1,0:T(8,128)(2,1)} %get-tuple-element.129.refs_3_, bf16[2048,512]{1,0:T(8,128)(2,1)} %get-tuple-element.130.refs_4_, ...), custom_call_target="tpu_custom_call" | custom-call | flops 199999995904 | bytes 400000000 | tf_op jit(solution)/shard_map/attention_backward/pallas_call | solution.py:58
  638.9 11.5 %convolution_convert_fusion.3.refs_17_ = bf16[2048,768]{1,0:T(8,128)(2,1)} fusion(bf16[2048,2048]{1,0:T(8,128)(2,1)} %get-tuple-element.121.refs_0_, bf16[2048,768]{1,0:T(8,128)(2,1)} %attention_backward.2.refs_4_.refs_3_), kind=kOutput, calls=%fused_computation.3 | convolution fusion | flops 6444023808 | bytes 14680064 | tf_op jit(solution)/shard_map/dot_general | solution.py:24
  652.1 12.3 %reduce-scatter.8.cloned.1.call-done.refs_18_ = bf16[256,2048]{1,0:T(8,128)(2,1)} async-done(((bf16[2048,2048]{1,0:T(8,128)(2,1)}), bf16[256,2048]{1,0:T(8,128)(2,1)}) %reduce-scatter.8.cloned.1.call-update) | async-done | bytes 1048592 | tf_op jit(solution)/shard_map/reduce_scatter | solution.py:1039
  664.3 35.2 %attention_backward.3.refs_4_ = bf16[2048,768]{1,0:T(8,128)(2,1)} custom-call(s32[8]{0:T(128)} %fusion.18.refs_0_, s32[8]{0:T(128)} %get-tuple-element.285.refs_1_, s32[8]{0:T(128)} %get-tuple-element.286.refs_2_, bf16[2048,512]{1,0:T(8,128)(2,1)} %get-tuple-element.129.refs_3_, bf16[2048,512]{1,0:T(8,128)(2,1)} %get-tuple-element.130.refs_4_, ...), custom_call_target="tpu_custom_call" | custom-call | flops 199999995904 | bytes 400000000 | tf_op jit(solution)/shard_map/attention_backward/pallas_call | solution.py:58
  699.6 27.6 %input_back.1 = (f32[8,1536]{1,0:T(8,128)}, f32[8,2048]{1,0:T(8,128)}, bf16[512,2048]{1,0:T(8,128)(2,1)}, bf16[512,2048]{1,0:T(8,128)(2,1)}, bf16[512,2048]{1,0:T(8,128)(2,1)}, /*index=5*/bf16[512,2048]{1,0:T(8,128)(2,1)}) custom-call(bf16[2048,1536]{1,0:T(8,128)(2,1)} %all-gather.5.cloned.1.call-done.refs_1_.refs_0_, ...), custom_call_target="tpu_custom_call" | custom-call | flops 112000000000 | bytes 224000000 | tf_op jit(solution)/shard_map/input_back/pallas_call | solution.py:58
  733.3 11.5 %convolution_convert_fusion.2 = bf16[2048,768]{1,0:T(8,128)(2,1)} fusion(bf16[2048,2048]{1,0:T(8,128)(2,1)} %get-tuple-element.121.refs_0_, bf16[2048,768]{1,0:T(8,128)(2,1)} %attention_backward.3.refs_4_), kind=kOutput, calls=%fused_computation.2 | convolution fusion | flops 6444023808 | bytes 14680064 | tf_op jit(solution)/shard_map/dot_general | solution.py:24
  746.4 42.7 %collective-permute-start.70 = (f32[8,1472]{1,0:T(8,128)S(1)}, f32[8,1472]{1,0:T(8,128)S(1)}, u32[]{:S(2)}, u32[]{:S(2)}) collective-permute-start(f32[8,1472]{1,0:T(8,128)S(1)} %get-tuple-element.257), channel_id=1, source_target_pairs={{0,16},{4,20},{8,24},{12,28},{16,0},{20,4},{24,8},{28,12},{1,17},{... | collective-permute-start | bytes 141320 | tf_op jit(solution)/shard_map/ppermute | solution.py:915
  (455 shorter events, 300.6 us)
Async XLA Ops:
  7.2 124.8 %all-gather.5.cloned.1.call-start = ((), (), s32[]{:S(2)}) async-start(), calls=%async_computation.5 | async-start | bytes 7077888 | tf_op jit(solution)/shard_map/all_gather | solution.py:981
  17.1 44.0 %collective-permute-start.11 = (bf16[256,2048]{1,0:T(8,128)(2,1)}, bf16[256,2048]{1,0:T(8,128)(2,1)}, u32[]{:S(2)}, u32[]{:S(2)}) collective-permute-start(bf16[256,2048]{1,0:T(8,128)(2,1)} %get-tuple-element.117.refs_2_.refs_3_.refs_1_), channel_id=1, source_target_pairs={{0,1},{1,0},{2,3},{3,2},{4,5},{5,4},{6,7},{7,6},{8,9},{9,8},{10,11... | collective-permute-start | bytes 3145736 | tf_op jit(solution)/shard_map/ppermute | solution.py:829
  18.5 42.6 %collective-permute-start.12 = (bf16[256,2048]{1,0:T(8,128)(2,1)S(1)}, bf16[256,2048]{1,0:T(8,128)(2,1)}, u32[]{:S(2)}, u32[]{:S(2)}) collective-permute-start(bf16[256,2048]{1,0:T(8,128)(2,1)S(1)} %get-tuple-element.119.refs_6_.refs_4_.refs_2_), channel_id=1, source_target_pairs={{0,2},{1,3},{2,0},{3,1},{4,6},{5,7},{6,4},{7,5},{8,10},{9,11},{10,... | collective-permute-start | bytes 3145736 | tf_op jit(solution)/shard_map/ppermute | solution.py:829
  62.2 135.9 %all-gather.7.cloned.1.call-start = ((), (), s32[]{:S(2)}) async-start(), calls=%async_computation.6 | async-start | bytes 2359296 | tf_op jit(solution)/shard_map/all_gather | solution.py:994
  62.9 239.3 %all-gather.9.cloned.1.call-start = ((), (), s32[]{:S(2)}) async-start(), calls=%async_computation.7 | async-start | bytes 9437184 | tf_op jit(solution)/shard_map/all_gather | solution.py:995
  63.7 282.0 %all-gather.11.cloned.1.call-start = ((), (), s32[]{:S(2)}) async-start(), calls=%async_computation.8 | async-start | bytes 9437184 | tf_op jit(solution)/shard_map/all_gather | solution.py:1002
  70.6 44.8 %collective-permute-start.14 = (bf16[256,2048]{1,0:T(8,128)(2,1)}, bf16[256,2048]{1,0:T(8,128)(2,1)}, u32[]{:S(2)}, u32[]{:S(2)}) collective-permute-start(bf16[256,2048]{1,0:T(8,128)(2,1)} %collective-permute-done.11.refs_3_), channel_id=1, source_target_pairs={{0,2},{1,3},{2,0},{3,1},{4,6},{5,7},{6,4},{7,5},{8,10},{9,11},{10,... | collective-permute-start | bytes 3145736 | tf_op jit(solution)/shard_map/ppermute | solution.py:829
  70.6 44.8 %collective-permute-start.15 = (bf16[256,2048]{1,0:T(8,128)(2,1)S(1)}, bf16[256,2048]{1,0:T(8,128)(2,1)}, u32[]{:S(2)}, u32[]{:S(2)}) collective-permute-start(bf16[256,2048]{1,0:T(8,128)(2,1)S(1)} %get-tuple-element.119.refs_6_.refs_4_.refs_2_), channel_id=1, source_target_pairs={{0,1},{1,0},{2,3},{3,2},{4,5},{5,4},{6,7},{7,6},{8,9},{9,8},{10,11... | collective-permute-start | bytes 3145736 | tf_op jit(solution)/shard_map/ppermute | solution.py:829
  72.7 42.9 %collective-permute-start.16 = (bf16[256,2048]{1,0:T(8,128)(2,1)}, bf16[256,2048]{1,0:T(8,128)(2,1)}, u32[]{:S(2)}, u32[]{:S(2)}) collective-permute-start(bf16[256,2048]{1,0:T(8,128)(2,1)} %collective-permute-done.12.refs_7_), channel_id=1, source_target_pairs={{0,1},{1,0},{2,3},{3,2},{4,5},{5,4},{6,7},{7,6},{8,9},{9,8},{10,11... | collective-permute-start | bytes 3145736 | tf_op jit(solution)/shard_map/ppermute | solution.py:829
  156.9 441.4 %reduce-scatter.6.cloned.1.call-start = ((), (), s32[]{:S(2)}) async-start(), calls=%async_computation.9 | async-start | bytes 9437184 | tf_op jit(solution)/shard_map/reduce_scatter | solution.py:1035
  300.8 44.9 %collective-permute-start.35 = (bf16[256,2048]{1,0:T(8,128)(2,1)S(1)}, bf16[256,2048]{1,0:T(8,128)(2,1)}, u32[]{:S(2)}, u32[]{:S(2)}) collective-permute-start(bf16[256,2048]{1,0:T(8,128)(2,1)S(1)} %collective-permute-done.33.refs_5_), channel_id=1, source_target_pairs={{0,2},{1,3},{2,0},{3,1},{4,6},{5,7},{6,4},{7,5},{8,10},{9,11},{10,... | collective-permute-start | bytes 3145736 | tf_op jit(solution)/shard_map/ppermute | solution.py:829
  301.7 44.0 %collective-permute-start.38 = (bf16[256,2048]{1,0:T(8,128)(2,1)S(1)}, bf16[256,2048]{1,0:T(8,128)(2,1)}, u32[]{:S(2)}, u32[]{:S(2)}) collective-permute-start(bf16[256,2048]{1,0:T(8,128)(2,1)S(1)} %collective-permute-done.36.refs_9_), channel_id=1, source_target_pairs={{0,1},{1,0},{2,3},{3,2},{4,5},{5,4},{6,7},{7,6},{8,9},{9,8},{10,11... | collective-permute-start | bytes 3145736 | tf_op jit(solution)/shard_map/ppermute | solution.py:829
  458.3 206.1 %reduce-scatter.8.cloned.1.call-start = ((), (), s32[]{:S(2)}) async-start(), calls=%async_computation.10 | async-start | bytes 9437184 | tf_op jit(solution)/shard_map/reduce_scatter | solution.py:1039
  515.1 295.4 %reduce-scatter.12.cloned.1.call-start = ((), (), s32[]{:S(2)}) async-start(), calls=%async_computation.12 | async-start | bytes 2359296 | tf_op jit(solution)/shard_map/reduce_scatter | solution.py:1080
  576.8 56.9 %collective-permute-start.52 = (bf16[512,2048]{1,0:T(8,128)(2,1)}, bf16[512,2048]{1,0:T(8,128)(2,1)}, u32[]{:S(2)}, u32[]{:S(2)}) collective-permute-start(bf16[512,2048]{1,0:T(8,128)(2,1)} %get-tuple-element.186.refs_16_), channel_id=1, source_target_pairs={{0,2},{1,3},{2,0},{3,1},{4,6},{5,7},{6,4},{7,5},{8,10},{9,11},{10,... | collective-permute-start | bytes 6291464 | tf_op jit(solution)/shard_map/ppermute | solution.py:829
  576.8 56.9 %collective-permute-start.53 = (bf16[512,2048]{1,0:T(8,128)(2,1)}, bf16[512,2048]{1,0:T(8,128)(2,1)}, u32[]{:S(2)}, u32[]{:S(2)}) collective-permute-start(bf16[512,2048]{1,0:T(8,128)(2,1)} %get-tuple-element.188.refs_18_), channel_id=1, source_target_pairs={{0,1},{1,0},{2,3},{3,2},{4,5},{5,4},{6,7},{7,6},{8,9},{9,8},{10,11... | collective-permute-start | bytes 6291464 | tf_op jit(solution)/shard_map/ppermute | solution.py:829
  598.4 212.1 %reduce-scatter.10.cloned.1.call-start = ((), (), s32[]{:S(2)}) async-start(), calls=%async_computation.11 | async-start | bytes 3538944 | tf_op jit(solution)/shard_map/reduce_scatter | solution.py:1078
  637.1 62.4 %collective-permute-start.57 = (bf16[256,2048]{1,0:T(8,128)(2,1)}, bf16[256,2048]{1,0:T(8,128)(2,1)}, u32[]{:S(2)}, u32[]{:S(2)}) collective-permute-start(bf16[256,2048]{1,0:T(8,128)(2,1)} %get-tuple-element.196.refs_19_), channel_id=1, source_target_pairs={{0,1},{1,0},{2,3},{3,2},{4,5},{5,4},{6,7},{7,6},{8,9},{9,8},{10,11... | collective-permute-start | bytes 3145736 | tf_op jit(solution)/shard_map/ppermute | solution.py:829
  637.5 62.0 %collective-permute-start.58 = (bf16[256,2048]{1,0:T(8,128)(2,1)}, bf16[256,2048]{1,0:T(8,128)(2,1)}, u32[]{:S(2)}, u32[]{:S(2)}) collective-permute-start(bf16[256,2048]{1,0:T(8,128)(2,1)} %get-tuple-element.197.refs_20_), channel_id=1, source_target_pairs={{0,2},{1,3},{2,0},{3,1},{4,6},{5,7},{6,4},{7,5},{8,10},{9,11},{10,... | collective-permute-start | bytes 3145736 | tf_op jit(solution)/shard_map/ppermute | solution.py:829
  650.5 172.6 %reduce-scatter.14.cloned.1.call-start = ((), (), s32[]{:S(2)}) async-start(), calls=%async_computation.13 | async-start | bytes 3538944 | tf_op jit(solution)/shard_map/reduce_scatter | solution.py:1103
  727.2 83.3 %collective-permute-start.59 = (bf16[512,2048]{1,0:T(8,128)(2,1)}, bf16[512,2048]{1,0:T(8,128)(2,1)}, u32[]{:S(2)}, u32[]{:S(2)}) collective-permute-start(bf16[512,2048]{1,0:T(8,128)(2,1)} %get-tuple-element.203), channel_id=1, source_target_pairs={{0,2},{1,3},{2,0},{3,1},{4,6},{5,7},{6,4},{7,5},{8,10},{9,11},{10,... | collective-permute-start | bytes 6291464 | tf_op jit(solution)/shard_map/ppermute | solution.py:829
  728.3 82.2 %collective-permute-start.60 = (bf16[512,2048]{1,0:T(8,128)(2,1)}, bf16[512,2048]{1,0:T(8,128)(2,1)}, u32[]{:S(2)}, u32[]{:S(2)}) collective-permute-start(bf16[512,2048]{1,0:T(8,128)(2,1)} %get-tuple-element.205), channel_id=1, source_target_pairs={{0,1},{1,0},{2,3},{3,2},{4,5},{5,4},{6,7},{7,6},{8,9},{9,8},{10,11... | collective-permute-start | bytes 6291464 | tf_op jit(solution)/shard_map/ppermute | solution.py:829
  746.4 42.9 %collective-permute-start.71 = (f32[8,1472]{1,0:T(8,128)S(1)}, f32[8,1472]{1,0:T(8,128)S(1)}, u32[]{:S(2)}, u32[]{:S(2)}) collective-permute-start(f32[8,1472]{1,0:T(8,128)S(1)} %get-tuple-element.256), channel_id=1, source_target_pairs={{0,24},{4,28},{8,16},{12,20},{16,8},{20,12},{24,0},{28,4},{1,25},{... | collective-permute-start | bytes 141320 | tf_op jit(solution)/shard_map/ppermute | solution.py:915
  746.4 46.1 %collective-permute-start.70 = (f32[8,1472]{1,0:T(8,128)S(1)}, f32[8,1472]{1,0:T(8,128)S(1)}, u32[]{:S(2)}, u32[]{:S(2)}) collective-permute-start(f32[8,1472]{1,0:T(8,128)S(1)} %get-tuple-element.257), channel_id=1, source_target_pairs={{0,16},{4,20},{8,24},{12,28},{16,0},{20,4},{24,8},{28,12},{1,17},{... | collective-permute-start | bytes 141320 | tf_op jit(solution)/shard_map/ppermute | solution.py:915
  (117 other events, 2120.9 us)
Sparse Core Ops, SparseCore 0:
  62.3 69.6 all-gather.4
  134.2 27.7 all-gather.6
  163.6 81.6 all-gather.8
  246.7 80.5 all-gather.10
  458.4 115.6 reduce-scatter.5
  576.2 88.0 reduce-scatter.7
  666.6 33.3 reduce-scatter.11
  702.4 39.2 reduce-scatter.9
  744.9 78.0 reduce-scatter.13

commit v4 on v3

--- a/solution.py
+++ b/solution.py
@@ -81,25 +81,32 @@
 
 
 def arrivals(pieces, width):
-    counts = [p.shape[0] // BLK for p in pieces]
-    starts = [sum(counts[:a]) for a in range(len(counts))]
-    inputs = []
-    for piece, start, count in zip(pieces, starts, counts):
-        if count == 1:
-            inputs.append(fixed(piece))
-        else:
-            spec = pl.BlockSpec((BLK, width), lambda i, *_, s=start, c=count: (jnp.clip(i - s, 0, c - 1), 0))
-            inputs.append((piece, spec))
-
-    def read(refs, buffer):
+    if len(pieces) == 1:
+
+        def read_block(refs, buffer):
+            buffer[...] = refs[0][...]
+
+        return [(pieces[0], tile(BLK, width))], [], read_block
+
+    def read(refs, buffer, landing, sems):
         step = pl.program_id(0)
-        for ref, start, count in zip(refs, starts, counts):
-
-            @pl.when((step >= start) & (step < start + count))
+        copies = [pltpu.make_async_copy(ref, landing.at[a % 2], sems.at[a % 2]) for a, ref in enumerate(refs)]
+
+        @pl.when(step == 0)
+        def _():
+            copies[0].start()
+
+        for a in range(len(copies)):
+
+            @pl.when(step == a)
             def _():
-                buffer[...] = ref[...]
-
-    return inputs, read
+                if a + 1 < len(copies):
+                    copies[a + 1].start()
+                copies[a].wait()
+                buffer[...] = landing[a % 2]
+
+    inputs = [(p, pl.BlockSpec(memory_space=pl.ANY)) for p in pieces]
+    return inputs, [pltpu.VMEM((2, BLK, width), jnp.bfloat16), pltpu.SemaphoreType.DMA((2,))], read
 
 
 def departures(rows, width, groups):
@@ -142,11 +149,11 @@
 
 def enter_attention(pieces, gain, shift):
     rows, wide = sum(p.shape[0] for p in pieces), pieces[0].shape[1]
-    inputs, read = arrivals(pieces, wide)
+    inputs, landing, read = arrivals(pieces, wide)
 
     def body(g_ref, s_ref, *rest):
-        piece_refs, (x_ref, low_ref, stat_ref) = rest[: len(pieces)], rest[len(pieces) :]
-        read(piece_refs, x_ref)
+        piece_refs, (x_ref, low_ref, stat_ref, *scratch) = rest[: len(pieces)], rest[len(pieces) :]
+        read(piece_refs, x_ref, *scratch)
         spread = x_ref[...].astype(jnp.float32)
         center = jnp.mean(spread, axis=-1, keepdims=True)
         spread = spread - center
@@ -160,6 +167,7 @@
         (rows // BLK,),
         [fixed(gain), fixed(shift)] + inputs,
         [((rows, wide), jnp.bfloat16, tile(BLK, wide))] * 2 + [((rows, 128), jnp.float32, tile(BLK, 128))],
+        scratch=landing,
         name="enter_attention",
     )
 
@@ -450,13 +458,13 @@
 def ffn_up(pieces, grad, grad_sums, w_up, bias):
     rows, units = grad.shape
     wide = w_up.shape[0]
-    inputs, read = arrivals(pieces, wide)
+    inputs, landing, read = arrivals(pieces, wide)
     chunk = min(512, units)
     share = 1.0 / chunk
 
     def body(f_ref, t_ref, u_w, b_ref, *rest):
-        m_ref, up_ref, stat_ref = rest[len(pieces) :]
-        read(rest[: len(pieces)], m_ref)
+        m_ref, up_ref, stat_ref, *scratch = rest[len(pieces) :]
+        read(rest[: len(pieces)], m_ref, *scratch)
         parts = []
 
         def figures(at, up):
@@ -508,6 +516,7 @@
             ((rows, units), jnp.float32, tile(BLK, units)),
             ((8, rows), jnp.float32, pl.BlockSpec((8, BLK), lambda i, *_: (0, i))),
         ],
+        scratch=landing,
         name="ffn_up",
     )
 
@@ -567,12 +576,12 @@
     rows, width = attn.shape
     wide = w_out.shape[1]
     ranks = len(stats)
-    inputs, read = arrivals(pieces, wide)
+    inputs, landing, read = arrivals(pieces, wide)
 
     def body(w_ref, a_ref, g_ref, *rest):
         stat_refs, rest = rest[:ranks], rest[ranks:]
-        r_ref, grad_ref, stat_ref, sum_ref = rest[len(pieces) :]
-        read(rest[: len(pieces)], r_ref)
+        r_ref, grad_ref, stat_ref, sum_ref, *scratch = rest[len(pieces) :]
+        read(rest[: len(pieces)], r_ref, *scratch)
         center, inverse = columns(joined([r[0:1] for r in stat_refs], [r[1:2] for r in stat_refs], width))
 
         @pl.when(pl.program_id(0) == 0)
@@ -601,6 +610,7 @@
             ((8, width), jnp.float32, pl.BlockSpec((8, width), lambda i, *_: (0, 0))),
         ],
         after=after,
+        scratch=landing,
         name="branch_back",
     )
 

time: 885 us -> 901 us (1.018)
  starting transfers between devices: 121 us -> 146 us
    ppermute x7, starting transfers between devices: 49 us -> 70.1 us  [sum_small(): lax.ppermute(value[at:at + left], axis, [(r, r ^ s) for r in range(count)])]
    pallas_call x21, Pallas kernels: 383 us -> 374 us  [launch(): pl.pallas_call(kernel, out_shape=tuple((jax.ShapeDtypeStruct(s, d) for s,...]
  transfers between devices with their start and end apart: 86 -> 86, of which waited for: 30 -> 31; matrix products, arithmetic and copies ran while one was open for 18% -> 18% of each run, Pallas kernels for 34% -> 33%
where the time goes in v4:
time: 901 us; the launch traced here: 895 us
  Pallas kernels  374 us (42%)
  waiting for transfers between devices  188 us (21%)
  starting transfers between devices  146 us (16%)
  matrix products  79.6 us (9%)
  local copies, waits for them, and re-layouts  72.5 us (8%)
  other arithmetic  19.4 us (2%)
  between operations  16.3 us (2%)
    pallas_call x21, Pallas kernels, launch(): pl.pallas_call(kernel, out_shape=tuple((jax.ShapeDtypeStruct(s, d) for s,...  374 us
    ppermute x61, waiting for transfers between devices, swap(): return lax.ppermute(value, 'seq', [(r, r ^ bit) for r in range(self.ranks)])  155 us
    dot_general x5, matrix products, tn(): lax.dot_general(a, b, (((0,), (0,)), ((), ())), preferred_element_type=jn...  79.6 us
    ppermute x7, starting transfers between devices, sum_small(): lax.ppermute(value[at:at + left], axis, [(r, r ^ s) for r in range(count)])  70.1 us
    ppermute x61, starting transfers between devices, swap(): return lax.ppermute(value, 'seq', [(r, r ^ bit) for r in range(self.ranks)])  55.5 us
    unnamed x127, local copies, waits for them, and re-layouts  23.1 us
    reduce_scatter x1, waiting for transfers between devices, local(): sum_up = lax.psum_scatter(g_up, 'batch', scatter_dimension=0, tiled=True)  20.4 us
  transfers between devices with their start and end apart: 86, of which 31 were waited for; matrix products, arithmetic and copies ran while one was open for 18% of the time, Pallas kernels for 33%

profile of v4, /device:TPU:1, one launch (start us, length us, event | category | flops | bytes accessed | tf_op | source)
XLA Modules:
  0.0 894.8 jit_solution(5715696647884551806)
XLA Ops:
  81.4 11.6 %collective-permute-done.13.refs_4_ = bf16[256,2048]{1,0:T(8,128)(2,1)} collective-permute-done((bf16[256,2048]{1,0:T(8,128)(2,1)}, bf16[256,2048]{1,0:T(8,128)(2,1)}, u32[]{:S(2)}, u32[]{:S(2)}) %collective-permute-start.13) | collective-permute-done | bytes 1048608 | tf_op jit(solution)/shard_map/ppermute | solution.py:839
  93.0 22.5 %collective-permute-done.14.refs_5_ = bf16[256,2048]{1,0:T(8,128)(2,1)} collective-permute-done((bf16[256,2048]{1,0:T(8,128)(2,1)}, bf16[256,2048]{1,0:T(8,128)(2,1)}, u32[]{:S(2)}, u32[]{:S(2)}) %collective-permute-start.14) | collective-permute-done | bytes 1048608 | tf_op jit(solution)/shard_map/ppermute | solution.py:839
  120.0 13.4 %enter_attention.1 = (bf16[2048,2048]{1,0:T(8,128)(2,1)}, bf16[2048,2048]{1,0:T(8,128)(2,1)}, f32[2048,128]{1,0:T(8,128)}) custom-call(f32[1,2048]{1,0:T(1,128)} %slice.220.refs_0_, f32[1,2048]{1,0:T(1,128)} %slice.222.refs_1_, bf16[256,2048]{1,0:T(8,128)(2,1)} %get-tuple-element.117.refs_2_.refs_3_.refs_1_, ...), custom_call_target="tpu_custom_call" | custom-call | flops 12000000000 | bytes 24000000 | tf_op jit(solution)/shard_map/enter_attention/pallas_call | solution.py:58
  133.4 19.0 %qkv_project.1 = (bf16[2048,512]{1,0:T(8,128)(2,1)}, bf16[2048,512]{1,0:T(8,128)(2,1)}, bf16[2048,512]{1,0:T(8,128)(2,1)}) custom-call(bf16[2048,2048]{1,0:T(8,128)(2,1)} %get-tuple-element.121.refs_0_, bf16[2048,1536]{1,0:T(8,128)(2,1)} %all-gather.5.cloned.1.call-done.refs_1_.refs_0_, f32[1,1536]{1,0:T(1,128)} %bitcast.199, ...), custom_call_target="tpu_custom_call" | custom-call | flops 19000000512 | bytes 38000000 | tf_op jit(solution)/shard_map/qkv_project/pallas_call | solution.py:58
  158.9 31.7 %attention_forward.1 = (f32[2048,512]{1,0:T(8,128)}, f32[8,2048]{1,0:T(8,128)}, f32[8,2048]{1,0:T(8,128)}) custom-call(s32[8]{0:T(128)} %fusion.18.refs_0_, s32[8]{0:T(128)} %get-tuple-element.287.refs_1_, s32[8]{0:T(128)} %get-tuple-element.288.refs_2_, bf16[2048,512]{1,0:T(8,128)(2,1)} %get-tuple-element.129.refs_3_, ...), custom_call_target="tpu_custom_call" | custom-call | flops 41000001536 | bytes 82000000 | tf_op jit(solution)/shard_map/attention_forward/pallas_call | solution.py:58
  203.7 14.7 %out_project.1 = (bf16[2048,512]{1,0:T(8,128)(2,1)}, bf16[512,2048]{1,0:T(8,128)(2,1)}, bf16[512,2048]{1,0:T(8,128)(2,1)}, bf16[512,2048]{1,0:T(8,128)(2,1)}, bf16[512,2048]{1,0:T(8,128)(2,1)}) custom-call(f32[2048,512]{1,0:T(8,128)} %get-tuple-element.138.refs_0_.refs_1_, f32[1,512]{1,0:T(1,128)} %get-tuple-element.263.refs_1_.refs_2_, ...), custom_call_target="tpu_custom_call" | custom-call | flops 14000000000 | bytes 28000000 | tf_op jit(solution)/shard_map/out_project/pallas_call | solution.py:58
  224.8 30.0 %collective-permute-done.26.refs_1_.refs_6_ = bf16[512,2048]{1,0:T(8,128)(2,1)S(1)} collective-permute-done((bf16[512,2048]{1,0:T(8,128)(2,1)}, bf16[512,2048]{1,0:T(8,128)(2,1)S(1)}, u32[]{:S(2)}, u32[]{:S(2)}) %collective-permute-start.26) | collective-permute-done | bytes 2097184 | tf_op jit(solution)/shard_map/ppermute | solution.py:839
  303.4 25.1 %ffn_grad.1 = (f32[2048,2048]{1,0:T(8,128)}, f32[8,2048]{1,0:T(8,128)}, f32[8,2048]{1,0:T(8,128)}) custom-call(bf16[2048,2048]{1,0:T(8,128)(2,1)} %constant_dynamic-update-slice_fusion.refs_11_.refs_0_, bf16[2048,2048]{1,0:T(8,128)(2,1)} %all-gather.9.cloned.1.call-done.refs_1_, f32[1,2048]{1,0:T(1,128)} %bitcast.194), custom_call_target="tpu_custom_call" | custom-call | flops 24000000000 | bytes 48000000 | tf_op jit(solution)/shard_map/ffn_grad/pallas_call | solution.py:58
  328.6 17.5 %collective-permute-done.35.refs_7_ = bf16[256,2048]{1,0:T(8,128)(2,1)} collective-permute-done((bf16[256,2048]{1,0:T(8,128)(2,1)S(1)}, bf16[256,2048]{1,0:T(8,128)(2,1)}, u32[]{:S(2)}, u32[]{:S(2)}) %collective-permute-start.35) | collective-permute-done | bytes 1048608 | tf_op jit(solution)/shard_map/ppermute | solution.py:839
  346.1 34.0 %ffn_up.1 = (bf16[2048,2048]{1,0:T(8,128)(2,1)}, f32[2048,2048]{1,0:T(8,128)}, f32[8,2048]{1,0:T(8,128)}) custom-call(f32[2048,2048]{1,0:T(8,128)} %get-tuple-element.156.refs_0_.refs_1_, f32[8,2048]{1,0:T(8,128)} %get-tuple-element.157.refs_1_, bf16[2048,2048]{1,0:T(8,128)(2,1)} %all-gather.11.cloned.1.call-done.refs_2_.refs_4_, f32[1,2048]{1,0:T(1,128)} %bitcast.198, ...), custom_call_target="tpu_custom_call" | custom-call | flops 32999999488 | bytes 66000000 | tf_op jit(solution)/shard_map/ffn_up/pallas_call | solution.py:58
  386.1 45.9 %ffn_mid.1 = (bf16[2048,2048]{1,0:T(8,128)(2,1)}, bf16[2048,2048]{1,0:T(8,128)(2,1)}, f32[8,2048]{1,0:T(8,128)}, bf16[512,2048]{1,0:T(8,128)(2,1)}, bf16[512,204...) custom-call(f32[2048,2048]{1,0:T(8,128)} %get-tuple-element.167.refs_0_, ...), custom_call_target="tpu_custom_call" | custom-call | flops 46999998464 | bytes 94000000 | tf_op jit(solution)/shard_map/ffn_mid/pallas_call | solution.py:58
  434.0 23.8 %convolution_convert_fusion.1.refs_4_ = bf16[2048,2048]{1,0:T(8,128)(2,1)} fusion(bf16[2048,2048]{1,0:T(8,128)(2,1)} %get-tuple-element.169.refs_0_, bf16[2048,2048]{1,0:T(8,128)(2,1)} %constant_dynamic-update-slice_fusion.refs_11_.refs_0_), kind=kOutput, calls=%fused_computation.1 | convolution fusion | flops 17184063488 | bytes 25165824 | tf_op jit(solution)/shard_map/dot_general | solution.py:24
  471.4 23.8 %convolution_convert_fusion.refs_11_ = bf16[2048,2048]{1,0:T(8,128)(2,1)} fusion(bf16[2048,2048]{1,0:T(8,128)(2,1)} %get-tuple-element.176, bf16[2048,2048]{1,0:T(8,128)(2,1)} %get-tuple-element.178), kind=kOutput, calls=%fused_computation | convolution fusion | flops 17184063488 | bytes 25165824 | tf_op jit(solution)/shard_map/dot_general | solution.py:24
  496.6 11.6 %leave_ffn.1 = (f32[256,2048]{1,0:T(8,128)}, f32[256,2048]{1,0:T(8,128)}, bf16[256,2048]{1,0:T(8,128)(2,1)}, bf16[256,2048]{1,0:T(8,128)(2,1)}, f32[8,2048]{1,0:T(8,128)}) custom-call(f32[1,2048]{1,0:T(1,128)} %slice.214.refs_1_.refs_0_, f32[256,2048]{1,0:T(8,128)} %get-tuple-element.152.refs_1_, f32[256,2048]{1,0:T(8,128)} %get-tuple-element.153.refs_2_, ...), custom_call_target="tpu_custom_call" | custom-call | flops 99999997952 | bytes 200000000 | tf_op jit(solution)/shard_map/leave_ffn/pallas_call | solution.py:58
  524.0 26.4 %down_project.1 = (bf16[512,2048]{1,0:T(8,128)(2,1)}, bf16[512,2048]{1,0:T(8,128)(2,1)}, bf16[512,2048]{1,0:T(8,128)(2,1)}, bf16[512,2048]{1,0:T(8,128)(2,1)}) custom-call(bf16[2048,2048]{1,0:T(8,128)(2,1)} %get-tuple-element.169.refs_0_, bf16[2048,2048]{1,0:T(8,128)(2,1)} %all-gather.9.cloned.1.call-done.refs_1_, ...), custom_call_target="tpu_custom_call" | custom-call | flops 199999995904 | bytes 400000000 | tf_op jit(solution)/shard_map/down_project/pallas_call | solution.py:58
  554.3 16.0 %branch_back.1 = (bf16[2048,2048]{1,0:T(8,128)(2,1)}, f32[2048,512]{1,0:T(8,128)}, f32[8,2048]{1,0:T(8,128)}, f32[8,512]{1,0:T(8,128)}) custom-call(bf16[512,2048]{1,0:T(8,128)(2,1)} %all-gather.7.cloned.1.call-done.refs_3_.refs_0_, f32[2048,512]{1,0:T(8,128)} %get-tuple-element.138.refs_0_.refs_1_, f32[1,512]{1,0:T(1,128)} %get-tuple-element.263.refs_1_.refs_2_, ...), custom_call_target="tpu_custom_call" | custom-call | flops 149999992832 | bytes 300000000 | tf_op jit(solution)/shard_map/branch_back/pallas_call | solution.py:58
  595.8 32.1 %attention_backward.2.refs_4_.refs_3_ = bf16[2048,768]{1,0:T(8,128)(2,1)} custom-call(s32[8]{0:T(128)} %fusion.18.refs_0_, s32[8]{0:T(128)} %get-tuple-element.285.refs_1_, s32[8]{0:T(128)} %get-tuple-element.286.refs_2_, bf16[2048,512]{1,0:T(8,128)(2,1)} %get-tuple-element.129.refs_3_, bf16[2048,512]{1,0:T(8,128)(2,1)} %get-tuple-element.130.refs_4_, ...), custom_call_target="tpu_custom_call" | custom-call | flops 199999995904 | bytes 400000000 | tf_op jit(solution)/shard_map/attention_backward/pallas_call | solution.py:58
  632.5 11.5 %convolution_convert_fusion.3.refs_17_ = bf16[2048,768]{1,0:T(8,128)(2,1)} fusion(bf16[2048,2048]{1,0:T(8,128)(2,1)} %get-tuple-element.121.refs_0_, bf16[2048,768]{1,0:T(8,128)(2,1)} %attention_backward.2.refs_4_.refs_3_), kind=kOutput, calls=%fused_computation.3 | convolution fusion | flops 6444023808 | bytes 14680064 | tf_op jit(solution)/shard_map/dot_general | solution.py:24
  645.6 20.4 %reduce-scatter.8.cloned.1.call-done.refs_18_ = bf16[256,2048]{1,0:T(8,128)(2,1)} async-done(((bf16[2048,2048]{1,0:T(8,128)(2,1)}), bf16[256,2048]{1,0:T(8,128)(2,1)}) %reduce-scatter.8.cloned.1.call-update) | async-done | bytes 1048592 | tf_op jit(solution)/shard_map/reduce_scatter | solution.py:1049
  666.0 32.1 %attention_backward.3.refs_4_ = bf16[2048,768]{1,0:T(8,128)(2,1)} custom-call(s32[8]{0:T(128)} %fusion.18.refs_0_, s32[8]{0:T(128)} %get-tuple-element.285.refs_1_, s32[8]{0:T(128)} %get-tuple-element.286.refs_2_, bf16[2048,512]{1,0:T(8,128)(2,1)} %get-tuple-element.129.refs_3_, bf16[2048,512]{1,0:T(8,128)(2,1)} %get-tuple-element.130.refs_4_, ...), custom_call_target="tpu_custom_call" | custom-call | flops 199999995904 | bytes 400000000 | tf_op jit(solution)/shard_map/attention_backward/pallas_call | solution.py:58
  698.2 27.7 %input_back.1 = (f32[8,1536]{1,0:T(8,128)}, f32[8,2048]{1,0:T(8,128)}, bf16[512,2048]{1,0:T(8,128)(2,1)}, bf16[512,2048]{1,0:T(8,128)(2,1)}, bf16[512,2048]{1,0:T(8,128)(2,1)}, /*index=5*/bf16[512,2048]{1,0:T(8,128)(2,1)}) custom-call(bf16[2048,1536]{1,0:T(8,128)(2,1)} %all-gather.5.cloned.1.call-done.refs_1_.refs_0_, ...), custom_call_target="tpu_custom_call" | custom-call | flops 112000000000 | bytes 224000000 | tf_op jit(solution)/shard_map/input_back/pallas_call | solution.py:58
  745.1 39.8 %collective-permute-start.71 = (f32[8,1472]{1,0:T(8,128)S(1)}, f32[8,1472]{1,0:T(8,128)S(1)}, u32[]{:S(2)}, u32[]{:S(2)}) collective-permute-start(f32[8,1472]{1,0:T(8,128)S(1)} %get-tuple-element.256), channel_id=1, source_target_pairs={{0,24},{4,28},{8,16},{12,20},{16,8},{20,12},{24,0},{28,4},{1,25},{... | collective-permute-start | bytes 141320 | tf_op jit(solution)/shard_map/ppermute | solution.py:925
  835.1 12.0 %collective-permute-done.68 = bf16[64,3,512]{2,0,1:T(8,128)(2,1)S(1)} collective-permute-done((bf16[64,3,512]{2,0,1:T(8,128)(2,1)S(1)}, bf16[64,3,512]{2,0,1:T(8,128)(2,1)S(1)}, u32[]{:S(2)}, u32[]{:S(2)}) %collective-permute-start.68) | collective-permute-done | bytes 196640 | tf_op jit(solution)/shard_map/ppermute | solution.py:839
  856.5 18.7 %collective-permute-start.74 = (f32[1,1472]{1,0:T(1,128)S(1)}, f32[1,1472]{1,0:T(1,128)S(1)}, u32[]{:S(2)}, u32[]{:S(2)}) collective-permute-start(f32[1,1472]{1,0:T(1,128)S(1)} %get-tuple-element.269), channel_id=1, source_target_pairs={{0,2},{1,3},{2,0},{3,1},{4,6},{5,7},{6,4},{7,5},{8,10},{9,11},{10,... | collective-permute-start | bytes 17672 | tf_op jit(solution)/shard_map/ppermute | solution.py:925
  (455 shorter events, 317.1 us)
Async XLA Ops:
  7.2 126.2 %all-gather.5.cloned.1.call-start = ((), (), s32[]{:S(2)}) async-start(), calls=%async_computation.5 | async-start | bytes 7077888 | tf_op jit(solution)/shard_map/all_gather | solution.py:991
  17.1 44.0 %collective-permute-start.11 = (bf16[256,2048]{1,0:T(8,128)(2,1)}, bf16[256,2048]{1,0:T(8,128)(2,1)}, u32[]{:S(2)}, u32[]{:S(2)}) collective-permute-start(bf16[256,2048]{1,0:T(8,128)(2,1)} %get-tuple-element.117.refs_2_.refs_3_.refs_1_), channel_id=1, source_target_pairs={{0,1},{1,0},{2,3},{3,2},{4,5},{5,4},{6,7},{7,6},{8,9},{9,8},{10,11... | collective-permute-start | bytes 3145736 | tf_op jit(solution)/shard_map/ppermute | solution.py:839
  18.5 42.6 %collective-permute-start.12 = (bf16[256,2048]{1,0:T(8,128)(2,1)S(1)}, bf16[256,2048]{1,0:T(8,128)(2,1)}, u32[]{:S(2)}, u32[]{:S(2)}) collective-permute-start(bf16[256,2048]{1,0:T(8,128)(2,1)S(1)} %get-tuple-element.119.refs_6_.refs_4_.refs_2_), channel_id=1, source_target_pairs={{0,2},{1,3},{2,0},{3,1},{4,6},{5,7},{6,4},{7,5},{8,10},{9,11},{10,... | collective-permute-start | bytes 3145736 | tf_op jit(solution)/shard_map/ppermute | solution.py:839
  62.2 137.3 %all-gather.7.cloned.1.call-start = ((), (), s32[]{:S(2)}) async-start(), calls=%async_computation.6 | async-start | bytes 2359296 | tf_op jit(solution)/shard_map/all_gather | solution.py:1004
  62.9 240.5 %all-gather.9.cloned.1.call-start = ((), (), s32[]{:S(2)}) async-start(), calls=%async_computation.7 | async-start | bytes 9437184 | tf_op jit(solution)/shard_map/all_gather | solution.py:1005
  63.7 282.4 %all-gather.11.cloned.1.call-start = ((), (), s32[]{:S(2)}) async-start(), calls=%async_computation.8 | async-start | bytes 9437184 | tf_op jit(solution)/shard_map/all_gather | solution.py:1012
  70.6 44.8 %collective-permute-start.14 = (bf16[256,2048]{1,0:T(8,128)(2,1)}, bf16[256,2048]{1,0:T(8,128)(2,1)}, u32[]{:S(2)}, u32[]{:S(2)}) collective-permute-start(bf16[256,2048]{1,0:T(8,128)(2,1)} %collective-permute-done.11.refs_3_), channel_id=1, source_target_pairs={{0,2},{1,3},{2,0},{3,1},{4,6},{5,7},{6,4},{7,5},{8,10},{9,11},{10,... | collective-permute-start | bytes 3145736 | tf_op jit(solution)/shard_map/ppermute | solution.py:839
  70.6 44.8 %collective-permute-start.15 = (bf16[256,2048]{1,0:T(8,128)(2,1)S(1)}, bf16[256,2048]{1,0:T(8,128)(2,1)}, u32[]{:S(2)}, u32[]{:S(2)}) collective-permute-start(bf16[256,2048]{1,0:T(8,128)(2,1)S(1)} %get-tuple-element.119.refs_6_.refs_4_.refs_2_), channel_id=1, source_target_pairs={{0,1},{1,0},{2,3},{3,2},{4,5},{5,4},{6,7},{7,6},{8,9},{9,8},{10,11... | collective-permute-start | bytes 3145736 | tf_op jit(solution)/shard_map/ppermute | solution.py:839
  72.7 42.9 %collective-permute-start.16 = (bf16[256,2048]{1,0:T(8,128)(2,1)}, bf16[256,2048]{1,0:T(8,128)(2,1)}, u32[]{:S(2)}, u32[]{:S(2)}) collective-permute-start(bf16[256,2048]{1,0:T(8,128)(2,1)} %collective-permute-done.12.refs_7_), channel_id=1, source_target_pairs={{0,1},{1,0},{2,3},{3,2},{4,5},{5,4},{6,7},{7,6},{8,9},{9,8},{10,11... | collective-permute-start | bytes 3145736 | tf_op jit(solution)/shard_map/ppermute | solution.py:839
  153.4 40.6 %collective-permute-start.20 = (bf16[256,2048]{1,0:T(8,128)(2,1)}, bf16[256,2048]{1,0:T(8,128)(2,1)}, u32[]{:S(2)}, u32[]{:S(2)}) collective-permute-start(bf16[256,2048]{1,0:T(8,128)(2,1)} %collective-permute-done.17.refs_8_.refs_9_), channel_id=1, source_target_pairs={{0,2},{1,3},{2,0},{3,1},{4,6},{5,7},{6,4},{7,5},{8,10},{9,11},{10,... | collective-permute-start | bytes 3145736 | tf_op jit(solution)/shard_map/ppermute | solution.py:839
  158.4 437.3 %reduce-scatter.6.cloned.1.call-start = ((), (), s32[]{:S(2)}) async-start(), calls=%async_computation.9 | async-start | bytes 9437184 | tf_op jit(solution)/shard_map/reduce_scatter | solution.py:1045
  301.8 44.3 %collective-permute-start.35 = (bf16[256,2048]{1,0:T(8,128)(2,1)S(1)}, bf16[256,2048]{1,0:T(8,128)(2,1)}, u32[]{:S(2)}, u32[]{:S(2)}) collective-permute-start(bf16[256,2048]{1,0:T(8,128)(2,1)S(1)} %collective-permute-done.33.refs_5_), channel_id=1, source_target_pairs={{0,2},{1,3},{2,0},{3,1},{4,6},{5,7},{6,4},{7,5},{8,10},{9,11},{10,... | collective-permute-start | bytes 3145736 | tf_op jit(solution)/shard_map/ppermute | solution.py:839
  302.7 43.4 %collective-permute-start.38 = (bf16[256,2048]{1,0:T(8,128)(2,1)S(1)}, bf16[256,2048]{1,0:T(8,128)(2,1)}, u32[]{:S(2)}, u32[]{:S(2)}) collective-permute-start(bf16[256,2048]{1,0:T(8,128)(2,1)S(1)} %collective-permute-done.36.refs_9_), channel_id=1, source_target_pairs={{0,1},{1,0},{2,3},{3,2},{4,5},{5,4},{6,7},{7,6},{8,9},{9,8},{10,11... | collective-permute-start | bytes 3145736 | tf_op jit(solution)/shard_map/ppermute | solution.py:839
  457.7 208.3 %reduce-scatter.8.cloned.1.call-start = ((), (), s32[]{:S(2)}) async-start(), calls=%async_computation.10 | async-start | bytes 9437184 | tf_op jit(solution)/shard_map/reduce_scatter | solution.py:1049
  513.6 300.7 %reduce-scatter.12.cloned.1.call-start = ((), (), s32[]{:S(2)}) async-start(), calls=%async_computation.12 | async-start | bytes 2359296 | tf_op jit(solution)/shard_map/reduce_scatter | solution.py:1090
  573.0 54.9 %collective-permute-start.52 = (bf16[512,2048]{1,0:T(8,128)(2,1)}, bf16[512,2048]{1,0:T(8,128)(2,1)}, u32[]{:S(2)}, u32[]{:S(2)}) collective-permute-start(bf16[512,2048]{1,0:T(8,128)(2,1)} %get-tuple-element.186.refs_16_), channel_id=1, source_target_pairs={{0,2},{1,3},{2,0},{3,1},{4,6},{5,7},{6,4},{7,5},{8,10},{9,11},{10,... | collective-permute-start | bytes 6291464 | tf_op jit(solution)/shard_map/ppermute | solution.py:839
  574.0 53.9 %collective-permute-start.53 = (bf16[512,2048]{1,0:T(8,128)(2,1)}, bf16[512,2048]{1,0:T(8,128)(2,1)}, u32[]{:S(2)}, u32[]{:S(2)}) collective-permute-start(bf16[512,2048]{1,0:T(8,128)(2,1)} %get-tuple-element.188.refs_18_), channel_id=1, source_target_pairs={{0,1},{1,0},{2,3},{3,2},{4,5},{5,4},{6,7},{7,6},{8,9},{9,8},{10,11... | collective-permute-start | bytes 6291464 | tf_op jit(solution)/shard_map/ppermute | solution.py:839
  595.8 218.6 %reduce-scatter.10.cloned.1.call-start = ((), (), s32[]{:S(2)}) async-start(), calls=%async_computation.11 | async-start | bytes 3538944 | tf_op jit(solution)/shard_map/reduce_scatter | solution.py:1088
  631.3 66.8 %collective-permute-start.57 = (bf16[256,2048]{1,0:T(8,128)(2,1)}, bf16[256,2048]{1,0:T(8,128)(2,1)}, u32[]{:S(2)}, u32[]{:S(2)}) collective-permute-start(bf16[256,2048]{1,0:T(8,128)(2,1)} %get-tuple-element.196.refs_19_), channel_id=1, source_target_pairs={{0,1},{1,0},{2,3},{3,2},{4,5},{5,4},{6,7},{7,6},{8,9},{9,8},{10,11... | collective-permute-start | bytes 3145736 | tf_op jit(solution)/shard_map/ppermute | solution.py:839
  631.7 66.4 %collective-permute-start.58 = (bf16[256,2048]{1,0:T(8,128)(2,1)}, bf16[256,2048]{1,0:T(8,128)(2,1)}, u32[]{:S(2)}, u32[]{:S(2)}) collective-permute-start(bf16[256,2048]{1,0:T(8,128)(2,1)} %get-tuple-element.197.refs_20_), channel_id=1, source_target_pairs={{0,2},{1,3},{2,0},{3,1},{4,6},{5,7},{6,4},{7,5},{8,10},{9,11},{10,... | collective-permute-start | bytes 3145736 | tf_op jit(solution)/shard_map/ppermute | solution.py:839
  644.0 181.1 %reduce-scatter.14.cloned.1.call-start = ((), (), s32[]{:S(2)}) async-start(), calls=%async_computation.13 | async-start | bytes 3538944 | tf_op jit(solution)/shard_map/reduce_scatter | solution.py:1113
  725.9 88.4 %collective-permute-start.59 = (bf16[512,2048]{1,0:T(8,128)(2,1)}, bf16[512,2048]{1,0:T(8,128)(2,1)}, u32[]{:S(2)}, u32[]{:S(2)}) collective-permute-start(bf16[512,2048]{1,0:T(8,128)(2,1)} %get-tuple-element.203), channel_id=1, source_target_pairs={{0,2},{1,3},{2,0},{3,1},{4,6},{5,7},{6,4},{7,5},{8,10},{9,11},{10,... | collective-permute-start | bytes 6291464 | tf_op jit(solution)/shard_map/ppermute | solution.py:839
  727.1 87.3 %collective-permute-start.60 = (bf16[512,2048]{1,0:T(8,128)(2,1)}, bf16[512,2048]{1,0:T(8,128)(2,1)}, u32[]{:S(2)}, u32[]{:S(2)}) collective-permute-start(bf16[512,2048]{1,0:T(8,128)(2,1)} %get-tuple-element.205), channel_id=1, source_target_pairs={{0,1},{1,0},{2,3},{3,2},{4,5},{5,4},{6,7},{7,6},{8,9},{9,8},{10,11... | collective-permute-start | bytes 6291464 | tf_op jit(solution)/shard_map/ppermute | solution.py:839
  745.1 46.4 %collective-permute-start.71 = (f32[8,1472]{1,0:T(8,128)S(1)}, f32[8,1472]{1,0:T(8,128)S(1)}, u32[]{:S(2)}, u32[]{:S(2)}) collective-permute-start(f32[8,1472]{1,0:T(8,128)S(1)} %get-tuple-element.256), channel_id=1, source_target_pairs={{0,24},{4,28},{8,16},{12,20},{16,8},{20,12},{24,0},{28,4},{1,25},{... | collective-permute-start | bytes 141320 | tf_op jit(solution)/shard_map/ppermute | solution.py:925
  (117 other events, 2153.7 us)
Sparse Core Ops, SparseCore 0:
  62.3 69.6 all-gather.4
  134.2 27.7 all-gather.6
  163.6 81.5 all-gather.8
  246.6 80.5 all-gather.10
  457.9 117.9 reduce-scatter.5
  578.0 87.9 reduce-scatter.7
  668.3 33.4 reduce-scatter.11
  704.1 39.2 reduce-scatter.9
  746.3 78.6 reduce-scatter.13
